TPU v7x, 32 devices: a whole 2x2x4 slice. The times are simulated.
32 devices in a mesh: grp: 4 (over y, x), gx: 2 (over core), gy: 4 (over z).
Axes of the slice: x: 2, y: 2, z: 4, core: 2. Of those that a mesh axis runs over, the one named last changes fastest.
Arguments:
- source_term: float32 [16, 64, 1024], P('gx', 'gy', 'grp'), may hold values from -6 to 6
- conductivity: float32 [16, 64, 1024], P('gx', 'gy', 'grp'), may hold values from 0.5 to 4
- initial_field: float32 [16, 64, 1024], P('gx', 'gy', 'grp'), may hold values from -6 to 6
Outputs:
- solution: float32 [16, 64, 1024], P('gx', 'gy', 'grp')
All inputs are finite; a program needn't handle non-finite values.
Results may differ from a plain program's by a relative error of at most 0.0001.
Values sent between devices are 32-bit elements; how exact they have to be, the bound alone decides.
No kernel may reach another device: no remote copies, remote signals or barrier semaphores. Data moves between devices by JAX's collectives and lax.ppermute only.
A program may use at most 64 MiB of HBM per device.

v0:
```python
import jax
import jax.numpy as jnp
from jax import lax
from jax.sharding import PartitionSpec as P

ITERS = 2


FIRST_RATE = 0.8
CARRY_RATE = 9.0 / 41.0
FRESH_RATE = 40.0 / 41.0


def extended(cells, sides, width):
    for axis, dim in sides:
        count = lax.axis_size(axis)
        ends = count - 1
        head = lax.slice_in_dim(cells, 0, width, axis=dim)
        tail = lax.slice_in_dim(cells, cells.shape[dim] - width, cells.shape[dim], axis=dim)
        cells = jnp.concatenate(
            [
                lax.ppermute(tail, axis, [(i, (i + 1) % count) for i in range(ends)]),
                cells,
                lax.ppermute(head, axis, [((i + 1) % count, i) for i in range(ends)]),
            ],
            axis=dim,
        )
    return cells


def neighbours(padded):
    return [
        padded[:-2, 1:-1, 1:-1],
        padded[2:, 1:-1, 1:-1],
        padded[1:-1, :-2, 1:-1],
        padded[1:-1, 2:, 1:-1],
        padded[1:-1, 1:-1, :-2],
        padded[1:-1, 1:-1, 2:],
    ]


def apply_operator(field_pad, cond_pad):
    center_field = field_pad[1:-1, 1:-1, 1:-1]
    center_cond = cond_pad[1:-1, 1:-1, 1:-1]
    result = jnp.zeros_like(center_field)
    for near_field, near_cond in zip(neighbours(field_pad), neighbours(cond_pad)):
        result = result + 0.5 * (center_cond + near_cond) * (center_field - near_field)
    return result


def diagonal_of(cond_pad):
    center_cond = cond_pad[1:-1, 1:-1, 1:-1]
    result = jnp.zeros_like(center_cond)
    for near_cond in neighbours(cond_pad):
        result = result + 0.5 * (center_cond + near_cond)
    return result


def block_mean(field):
    sizea, sizeb, sizec = field.shape
    return field.reshape(sizea // 2, 2, sizeb // 2, 2, sizec // 2, 2).mean(axis=(1, 3, 5))


def prolong(coarse):
    sizea, sizeb, sizec = coarse.shape
    spread = jnp.broadcast_to(coarse[:, None, :, None, :, None], (sizea, 2, sizeb, 2, sizec, 2))
    return spread.reshape(2 * sizea, 2 * sizeb, 2 * sizec)


def finish(residual, first, first_pad, cond_pad, diagonal):
    image = 0.25 * apply_operator(first_pad, cond_pad)
    second = CARRY_RATE * first + FRESH_RATE * (residual - image) / diagonal
    return first + second


def shards(source_term, conductivity, initial_field):
    coarse_cond = block_mean(conductivity)
    coarse_pad = extended(coarse_cond, (("grp", 2), ("gx", 0), ("gy", 1)), 1)
    coarse_diag = 0.25 * diagonal_of(coarse_pad)
    cond_pad = extended(conductivity, (("grp", 2), ("gx", 0), ("gy", 1)), 1)
    fine_diag = diagonal_of(cond_pad)
    field = initial_field
    for iteration in range(ITERS):
        field_pad = extended(field, (("grp", 2), ("gx", 0), ("gy", 1)), 1)
        residual = source_term - apply_operator(field_pad, cond_pad)
        first = FIRST_RATE * residual / fine_diag
        first_pad = extended(first, (("grp", 2), ("gx", 0), ("gy", 1)), 1)
        image = apply_operator(first_pad, cond_pad)
        fine_corr = first + (CARRY_RATE * first + FRESH_RATE * (residual - image) / fine_diag)
        coarse_res = block_mean(residual)
        coarse_first = FIRST_RATE * coarse_res / coarse_diag
        coarse_first_pad = extended(coarse_first, (("grp", 2), ("gx", 0), ("gy", 1)), 1)
        coarse_corr = finish(coarse_res, coarse_first, coarse_first_pad, coarse_pad, coarse_diag)
        field = field + fine_corr + prolong(coarse_corr)
    return field


def solution(mesh):
    return jax.shard_map(
        shards,
        mesh=mesh,
        in_specs=(P("gx", "gy", "grp"), P("gx", "gy", "grp"), P("gx", "gy", "grp")),
        out_specs=P("gx", "gy", "grp"),
        check_vma=False,
    )
```

profile of v0, /device:TPU:18, one launch (start us, length us, event | category | flops | bytes accessed | tf_op | source)
XLA Modules:
  0.0 208.0 jit_solution(5719068194416359653)
XLA Ops:
  1.0 2.4 %collective-permute-start.1 = (f32[8,16,1]{2,1,0:T(8,128)S(1)}, f32[8,16,1]{2,1,0:T(8,128)S(1)}, u32[]{:S(2)}, u32[]{:S(2)}) collective-permute-start(f32[8,16,1]{2,1,0:T(8,128)S(1)} %get-tuple-element.43), channel_id=1, source_target_pairs={{8,0},{16,8},{24,16},{9,1},{17,9},{25,17},{10,2},{18,10},{26,18},{... | collective-permute-start | bytes 1544 | tf_op jit(solution)/shard_map/ppermute | solution.py:24
  3.4 4.3 %collective-permute-start = (f32[8,16,1]{2,1,0:T(8,128)S(1)}, f32[8,16,1]{2,1,0:T(8,128)S(1)}, u32[]{:S(2)}, u32[]{:S(2)}) collective-permute-start(f32[8,16,1]{2,1,0:T(8,128)S(1)} %get-tuple-element.42), channel_id=1, source_target_pairs={{0,8},{8,16},{16,24},{1,9},{9,17},{17,25},{2,10},{10,18},{18,26},{... | collective-permute-start | bytes 1544 | tf_op jit(solution)/shard_map/ppermute | solution.py:22
  8.7 2.1 collective-permute-start.4
  10.8 10.5 %reshape.18 = f32[4,2,8,2,128,2]{5,4,3,2,1,0:T(8,128)} reshape(f32[8,16,256]{2,1,0:T(8,128)} %param.4) | data formatting | bytes 262144 | tf_op jit(solution)/shard_map/reshape | solution.py:61
  21.3 4.0 %reduce_sum.28 = f32[4,8,128]{2,1,0:T(8,128)S(1)} reduce(f32[4,2,8,2,128,2]{5,4,3,2,1,0:T(8,128)} %reshape.18, f32[]{:T(128)} %constant.6.clone.1), dimensions={1,3,5}, to_apply=%region_1.0 | reduce | flops 28672 | bytes 147460 | tf_op jit(solution)/shard_map/reduce_sum | solution.py:61
  27.3 4.8 %collective-permute-start.18 = (f32[4,8,1]{2,1,0:T(8,128)S(1)}, f32[4,8,1]{2,1,0:T(8,128)S(1)}, u32[]{:S(2)}, u32[]{:S(2)}) collective-permute-start(f32[4,8,1]{2,1,0:T(8,128)S(1)} %get-tuple-element.60), channel_id=1, source_target_pairs={{0,8},{8,16},{16,24},{1,9},{9,17},{17,25},{2,10},{10,18},{18,26},{... | collective-permute-start | bytes 392 | tf_op jit(solution)/shard_map/ppermute | solution.py:22
  32.1 3.9 %collective-permute-start.3 = (f32[8,16,1]{2,1,0:T(8,128)S(1)}, f32[8,16,1]{2,1,0:T(8,128)S(1)}, u32[]{:S(2)}, u32[]{:S(2)}) collective-permute-start(f32[8,16,1]{2,1,0:T(8,128)S(1)} %get-tuple-element.40), channel_id=1, source_target_pairs={{0,8},{8,16},{16,24},{1,9},{9,17},{17,25},{2,10},{10,18},{18,26},{... | collective-permute-start | bytes 1544 | tf_op jit(solution)/shard_map/ppermute | solution.py:22
  40.2 3.0 %collective-permute-start.5 = (f32[1,16,258]{2,1,0:T(8,128)S(1)}, f32[1,16,258]{2,1,0:T(8,128)S(1)}, u32[]{:S(2)}, u32[]{:S(2)}) collective-permute-start(f32[1,16,258]{2,1,0:T(8,128)S(1)} %get-tuple-element.32), channel_id=1, source_target_pairs={{0,4},{1,5},{2,6},{3,7},{8,12},{9,13},{10,14},{11,15},{16,20},{17,... | collective-permute-start | bytes 49544 | tf_op jit(solution)/shard_map/ppermute | solution.py:22
  46.1 2.4 %collective-permute-start.11 = (f32[10,1,258]{2,1,0:T(1,128)S(1)}, f32[10,1,258]{2,1,0:T(1,128)S(1)}, u32[]{:S(2)}, u32[]{:S(2)}) collective-permute-start(f32[10,1,258]{2,1,0:T(1,128)S(1)} %get-tuple-element.23), channel_id=1, source_target_pairs={{1,0},{2,1},{3,2},{5,4},{6,5},{7,6},{9,8},{10,9},{11,10},{13,12},{... | collective-permute-start | bytes 30968 | tf_op jit(solution)/shard_map/ppermute | solution.py:24
  48.5 3.5 %collective-permute-start.9 = (f32[10,1,258]{2,1,0:T(1,128)S(1)}, f32[10,1,258]{2,1,0:T(1,128)S(1)}, u32[]{:S(2)}, u32[]{:S(2)}) collective-permute-start(f32[10,1,258]{2,1,0:T(1,128)S(1)} %get-tuple-element.22), channel_id=1, source_target_pairs={{0,1},{1,2},{2,3},{4,5},{5,6},{6,7},{8,9},{9,10},{10,11},{12,13},{... | collective-permute-start | bytes 30968 | tf_op jit(solution)/shard_map/ppermute | solution.py:22
  52.1 1.9 collective-permute-start.8
  54.0 3.9 %collective-permute-start.10 = (f32[10,1,258]{2,1,0:T(1,128)S(1)}, f32[10,1,258]{2,1,0:T(1,128)S(1)}, u32[]{:S(2)}, u32[]{:S(2)}) collective-permute-start(f32[10,1,258]{2,1,0:T(1,128)S(1)} %get-tuple-element.20), channel_id=1, source_target_pairs={{1,0},{2,1},{3,2},{5,4},{6,5},{7,6},{9,8},{10,9},{11,10},{13,12},{... | collective-permute-start | bytes 30968 | tf_op jit(solution)/shard_map/ppermute | solution.py:24
  58.1 1.9 collective-permute-start.22
  60.0 3.9 %collective-permute-start.23 = (f32[6,1,130]{2,1,0:T(1,128)S(1)}, f32[6,1,130]{2,1,0:T(1,128)S(1)}, u32[]{:S(2)}, u32[]{:S(2)}) collective-permute-start(f32[6,1,130]{2,1,0:T(1,128)S(1)} %get-tuple-element.48), channel_id=1, source_target_pairs={{1,0},{2,1},{3,2},{5,4},{6,5},{7,6},{9,8},{10,9},{11,10},{13,12},{... | collective-permute-start | bytes 9368 | tf_op jit(solution)/shard_map/ppermute | solution.py:24
  64.5 9.8 %reshape.17 = f32[4,2,8,2,128,2]{5,4,3,2,1,0:T(8,128)} reshape(f32[8,16,256]{2,1,0:T(8,128)S(1)} %get-tuple-element.9) | data formatting | bytes 262144 | tf_op jit(solution)/shard_map/reshape | solution.py:61
  74.2 4.0 %reduce_sum.27 = f32[4,8,128]{2,1,0:T(8,128)S(1)} reduce(f32[4,2,8,2,128,2]{5,4,3,2,1,0:T(8,128)} %reshape.17, f32[]{:T(128)} %constant.6.clone.1), dimensions={1,3,5}, to_apply=%region_0.0 | reduce | flops 28672 | bytes 147460 | tf_op jit(solution)/shard_map/reduce_sum | solution.py:61
  78.5 1.9 collective-permute-start.25
  80.4 4.8 %collective-permute-start.24 = (f32[4,8,1]{2,1,0:T(8,128)S(1)}, f32[4,8,1]{2,1,0:T(8,128)S(1)}, u32[]{:S(2)}, u32[]{:S(2)}) collective-permute-start(f32[4,8,1]{2,1,0:T(8,128)S(1)} %get-tuple-element.58), channel_id=1, source_target_pairs={{0,8},{8,16},{16,24},{1,9},{9,17},{17,25},{2,10},{10,18},{18,26},{... | collective-permute-start | bytes 392 | tf_op jit(solution)/shard_map/ppermute | solution.py:22
  85.3 1.9 collective-permute-start.13
  87.2 4.8 %collective-permute-start.12 = (f32[8,16,1]{2,1,0:T(8,128)S(1)}, f32[8,16,1]{2,1,0:T(8,128)S(1)}, u32[]{:S(2)}, u32[]{:S(2)}) collective-permute-start(f32[8,16,1]{2,1,0:T(8,128)S(1)} %get-tuple-element.38), channel_id=1, source_target_pairs={{0,8},{8,16},{16,24},{1,9},{9,17},{17,25},{2,10},{10,18},{18,26},{... | collective-permute-start | bytes 1544 | tf_op jit(solution)/shard_map/ppermute | solution.py:22
  93.4 3.0 %collective-permute-start.26 = (f32[1,8,130]{2,1,0:T(8,128)S(1)}, f32[1,8,130]{2,1,0:T(8,128)S(1)}, u32[]{:S(2)}, u32[]{:S(2)}) collective-permute-start(f32[1,8,130]{2,1,0:T(8,128)S(1)} %get-tuple-element.52), channel_id=1, source_target_pairs={{0,4},{1,5},{2,6},{3,7},{8,12},{9,13},{10,14},{11,15},{16,20},{17,... | collective-permute-start | bytes 12488 | tf_op jit(solution)/shard_map/ppermute | solution.py:22
  97.9 3.0 %collective-permute-start.14 = (f32[1,16,258]{2,1,0:T(8,128)S(1)}, f32[1,16,258]{2,1,0:T(8,128)S(1)}, u32[]{:S(2)}, u32[]{:S(2)}) collective-permute-start(f32[1,16,258]{2,1,0:T(8,128)S(1)} %get-tuple-element.28), channel_id=1, source_target_pairs={{0,4},{1,5},{2,6},{3,7},{8,12},{9,13},{10,14},{11,15},{16,20},{17,... | collective-permute-start | bytes 49544 | tf_op jit(solution)/shard_map/ppermute | solution.py:22
  101.0 2.4 %collective-permute-start.29 = (f32[6,1,130]{2,1,0:T(1,128)S(1)}, f32[6,1,130]{2,1,0:T(1,128)S(1)}, u32[]{:S(2)}, u32[]{:S(2)}) collective-permute-start(f32[6,1,130]{2,1,0:T(1,128)S(1)} %get-tuple-element.47), channel_id=1, source_target_pairs={{1,0},{2,1},{3,2},{5,4},{6,5},{7,6},{9,8},{10,9},{11,10},{13,12},{... | collective-permute-start | bytes 9368 | tf_op jit(solution)/shard_map/ppermute | solution.py:24
  103.4 3.5 %collective-permute-start.28 = (f32[6,1,130]{2,1,0:T(1,128)S(1)}, f32[6,1,130]{2,1,0:T(1,128)S(1)}, u32[]{:S(2)}, u32[]{:S(2)}) collective-permute-start(f32[6,1,130]{2,1,0:T(1,128)S(1)} %get-tuple-element.46), channel_id=1, source_target_pairs={{0,1},{1,2},{2,3},{4,5},{5,6},{6,7},{8,9},{9,10},{10,11},{12,13},{... | collective-permute-start | bytes 9368 | tf_op jit(solution)/shard_map/ppermute | solution.py:22
  107.1 2.4 %collective-permute-start.17 = (f32[10,1,258]{2,1,0:T(1,128)S(1)}, f32[10,1,258]{2,1,0:T(1,128)S(1)}, u32[]{:S(2)}, u32[]{:S(2)}) collective-permute-start(f32[10,1,258]{2,1,0:T(1,128)S(1)} %get-tuple-element.19), channel_id=1, source_target_pairs={{1,0},{2,1},{3,2},{5,4},{6,5},{7,6},{9,8},{10,9},{11,10},{13,12},{... | collective-permute-start | bytes 30968 | tf_op jit(solution)/shard_map/ppermute | solution.py:24
  109.4 3.5 %collective-permute-start.16 = (f32[10,1,258]{2,1,0:T(1,128)S(1)}, f32[10,1,258]{2,1,0:T(1,128)S(1)}, u32[]{:S(2)}, u32[]{:S(2)}) collective-permute-start(f32[10,1,258]{2,1,0:T(1,128)S(1)} %get-tuple-element.18), channel_id=1, source_target_pairs={{0,1},{1,2},{2,3},{4,5},{5,6},{6,7},{8,9},{9,10},{10,11},{12,13},{... | collective-permute-start | bytes 30968 | tf_op jit(solution)/shard_map/ppermute | solution.py:22
  113.1 3.9 %broadcast_in_dim.4 = f32[4,2,8,2,128,2]{5,4,3,2,1,0:T(8,128)} broadcast(f32[4,8,128]{2,1,0:T(8,128)S(1)} %fusion.127), dimensions={0,2,4} | broadcast | bytes 147456 | tf_op jit(solution)/shard_map/broadcast_in_dim | solution.py:66
  117.0 6.9 %reshape.19 = f32[8,16,256]{2,1,0:T(8,128)S(1)} reshape(f32[4,2,8,2,128,2]{5,4,3,2,1,0:T(8,128)} %broadcast_in_dim.4) | data formatting | bytes 262144 | tf_op jit(solution)/shard_map/reshape | solution.py:67
  124.4 1.9 collective-permute-start.31
  126.3 4.8 %collective-permute-start.30 = (f32[8,16,1]{2,1,0:T(8,128)S(1)}, f32[8,16,1]{2,1,0:T(8,128)S(1)}, u32[]{:S(2)}, u32[]{:S(2)}) collective-permute-start(f32[8,16,1]{2,1,0:T(8,128)S(1)} %get-tuple-element.36), channel_id=1, source_target_pairs={{0,8},{8,16},{16,24},{1,9},{9,17},{17,25},{2,10},{10,18},{18,26},{... | collective-permute-start | bytes 1544 | tf_op jit(solution)/shard_map/ppermute | solution.py:22
  134.4 3.0 %collective-permute-start.32 = (f32[1,16,258]{2,1,0:T(8,128)S(1)}, f32[1,16,258]{2,1,0:T(8,128)S(1)}, u32[]{:S(2)}, u32[]{:S(2)}) collective-permute-start(f32[1,16,258]{2,1,0:T(8,128)S(1)} %get-tuple-element.26), channel_id=1, source_target_pairs={{0,4},{1,5},{2,6},{3,7},{8,12},{9,13},{10,14},{11,15},{16,20},{17,... | collective-permute-start | bytes 49544 | tf_op jit(solution)/shard_map/ppermute | solution.py:22
  138.4 2.4 %collective-permute-start.35 = (f32[10,1,258]{2,1,0:T(1,128)S(1)}, f32[10,1,258]{2,1,0:T(1,128)S(1)}, u32[]{:S(2)}, u32[]{:S(2)}) collective-permute-start(f32[10,1,258]{2,1,0:T(1,128)S(1)} %get-tuple-element.17), channel_id=1, source_target_pairs={{1,0},{2,1},{3,2},{5,4},{6,5},{7,6},{9,8},{10,9},{11,10},{13,12},{... | collective-permute-start | bytes 30968 | tf_op jit(solution)/shard_map/ppermute | solution.py:24
  140.8 3.5 %collective-permute-start.34 = (f32[10,1,258]{2,1,0:T(1,128)S(1)}, f32[10,1,258]{2,1,0:T(1,128)S(1)}, u32[]{:S(2)}, u32[]{:S(2)}) collective-permute-start(f32[10,1,258]{2,1,0:T(1,128)S(1)} %get-tuple-element.16), channel_id=1, source_target_pairs={{0,1},{1,2},{2,3},{4,5},{5,6},{6,7},{8,9},{9,10},{10,11},{12,13},{... | collective-permute-start | bytes 30968 | tf_op jit(solution)/shard_map/ppermute | solution.py:22
  144.3 2.1 %collective-permute-done.34 = f32[10,1,258]{2,1,0:T(1,128)S(1)} collective-permute-done((f32[10,1,258]{2,1,0:T(1,128)S(1)}, f32[10,1,258]{2,1,0:T(1,128)S(1)}, u32[]{:S(2)}, u32[]{:S(2)}) %collective-permute-start.34) | collective-permute-done | bytes 10352 | tf_op jit(solution)/shard_map/ppermute | solution.py:22
  146.8 9.8 %reshape.20 = f32[4,2,8,2,128,2]{5,4,3,2,1,0:T(8,128)} reshape(f32[8,16,256]{2,1,0:T(8,128)S(1)} %get-tuple-element.6) | data formatting | bytes 262144 | tf_op jit(solution)/shard_map/reshape | solution.py:61
  156.6 4.0 %reduce_sum.29 = f32[4,8,128]{2,1,0:T(8,128)S(1)} reduce(f32[4,2,8,2,128,2]{5,4,3,2,1,0:T(8,128)} %reshape.20, f32[]{:T(128)} %constant.6.clone.1), dimensions={1,3,5}, to_apply=%region_2.0 | reduce | flops 28672 | bytes 147460 | tf_op jit(solution)/shard_map/reduce_sum | solution.py:61
  160.8 1.9 collective-permute-start.43
  162.7 5.3 %collective-permute-start.42 = (f32[4,8,1]{2,1,0:T(8,128)S(1)}, f32[4,8,1]{2,1,0:T(8,128)S(1)}, u32[]{:S(2)}, u32[]{:S(2)}) collective-permute-start(f32[4,8,1]{2,1,0:T(8,128)S(1)} %get-tuple-element.56), channel_id=1, source_target_pairs={{0,8},{8,16},{16,24},{1,9},{9,17},{17,25},{2,10},{10,18},{18,26},{... | collective-permute-start | bytes 392 | tf_op jit(solution)/shard_map/ppermute | solution.py:22
  168.1 1.9 collective-permute-start.37
  170.1 4.8 %collective-permute-start.36 = (f32[8,16,1]{2,1,0:T(8,128)S(1)}, f32[8,16,1]{2,1,0:T(8,128)S(1)}, u32[]{:S(2)}, u32[]{:S(2)}) collective-permute-start(f32[8,16,1]{2,1,0:T(8,128)S(1)} %get-tuple-element.34), channel_id=1, source_target_pairs={{0,8},{8,16},{16,24},{1,9},{9,17},{17,25},{2,10},{10,18},{18,26},{... | collective-permute-start | bytes 1544 | tf_op jit(solution)/shard_map/ppermute | solution.py:22
  176.3 3.0 %collective-permute-start.44 = (f32[1,8,130]{2,1,0:T(8,128)S(1)}, f32[1,8,130]{2,1,0:T(8,128)S(1)}, u32[]{:S(2)}, u32[]{:S(2)}) collective-permute-start(f32[1,8,130]{2,1,0:T(8,128)S(1)} %get-tuple-element.50), channel_id=1, source_target_pairs={{0,4},{1,5},{2,6},{3,7},{8,12},{9,13},{10,14},{11,15},{16,20},{17,... | collective-permute-start | bytes 12488 | tf_op jit(solution)/shard_map/ppermute | solution.py:22
  180.7 3.0 %collective-permute-start.38 = (f32[1,16,258]{2,1,0:T(8,128)S(1)}, f32[1,16,258]{2,1,0:T(8,128)S(1)}, u32[]{:S(2)}, u32[]{:S(2)}) collective-permute-start(f32[1,16,258]{2,1,0:T(8,128)S(1)} %get-tuple-element.24), channel_id=1, source_target_pairs={{0,4},{1,5},{2,6},{3,7},{8,12},{9,13},{10,14},{11,15},{16,20},{17,... | collective-permute-start | bytes 49544 | tf_op jit(solution)/shard_map/ppermute | solution.py:22
  183.9 1.9 collective-permute-start.47
  185.8 3.9 %collective-permute-start.46 = (f32[6,1,130]{2,1,0:T(1,128)S(1)}, f32[6,1,130]{2,1,0:T(1,128)S(1)}, u32[]{:S(2)}, u32[]{:S(2)}) collective-permute-start(f32[6,1,130]{2,1,0:T(1,128)S(1)} %get-tuple-element.44), channel_id=1, source_target_pairs={{0,1},{1,2},{2,3},{4,5},{5,6},{6,7},{8,9},{9,10},{10,11},{12,13},{... | collective-permute-start | bytes 9368 | tf_op jit(solution)/shard_map/ppermute | solution.py:22
  189.9 1.9 collective-permute-start.41
  191.8 3.9 %collective-permute-start.40 = (f32[10,1,258]{2,1,0:T(1,128)S(1)}, f32[10,1,258]{2,1,0:T(1,128)S(1)}, u32[]{:S(2)}, u32[]{:S(2)}) collective-permute-start(f32[10,1,258]{2,1,0:T(1,128)S(1)} %get-tuple-element.14), channel_id=1, source_target_pairs={{0,1},{1,2},{2,3},{4,5},{5,6},{6,7},{8,9},{9,10},{10,11},{12,13},{... | collective-permute-start | bytes 30968 | tf_op jit(solution)/shard_map/ppermute | solution.py:22
  195.9 3.9 %broadcast_in_dim.5 = f32[4,2,8,2,128,2]{5,4,3,2,1,0:T(8,128)} broadcast(f32[4,8,128]{2,1,0:T(8,128)S(1)} %fusion.104), dimensions={0,2,4} | broadcast | bytes 147456 | tf_op jit(solution)/shard_map/broadcast_in_dim | solution.py:66
  199.8 6.9 %reshape.21 = f32[8,16,256]{2,1,0:T(8,128)S(1)} reshape(f32[4,2,8,2,128,2]{5,4,3,2,1,0:T(8,128)} %broadcast_in_dim.5) | data formatting | bytes 262144 | tf_op jit(solution)/shard_map/reshape | solution.py:67
  (97 shorter events, 24.5 us)
Async XLA Ops:
  1.0 39.2 %collective-permute-start.1 = (f32[8,16,1]{2,1,0:T(8,128)S(1)}, f32[8,16,1]{2,1,0:T(8,128)S(1)}, u32[]{:S(2)}, u32[]{:S(2)}) collective-permute-start(f32[8,16,1]{2,1,0:T(8,128)S(1)} %get-tuple-element.43), channel_id=1, source_target_pairs={{8,0},{16,8},{24,16},{9,1},{17,9},{25,17},{10,2},{18,10},{26,18},{... | collective-permute-start | bytes 1544 | tf_op jit(solution)/shard_map/ppermute | solution.py:24
  3.4 39.8 %collective-permute-start = (f32[8,16,1]{2,1,0:T(8,128)S(1)}, f32[8,16,1]{2,1,0:T(8,128)S(1)}, u32[]{:S(2)}, u32[]{:S(2)}) collective-permute-start(f32[8,16,1]{2,1,0:T(8,128)S(1)} %get-tuple-element.42), channel_id=1, source_target_pairs={{0,8},{8,16},{16,24},{1,9},{9,17},{17,25},{2,10},{10,18},{18,26},{... | collective-permute-start | bytes 1544 | tf_op jit(solution)/shard_map/ppermute | solution.py:22
  8.7 28.7 %collective-permute-start.4 = (f32[8,16,1]{2,1,0:T(8,128)S(1)}, f32[8,16,1]{2,1,0:T(8,128)S(1)}, u32[]{:S(2)}, u32[]{:S(2)}) collective-permute-start(f32[8,16,1]{2,1,0:T(8,128)S(1)} %get-tuple-element.41), channel_id=1, source_target_pairs={{8,0},{16,8},{24,16},{9,1},{17,9},{25,17},{10,2},{18,10},{26,18},{... | collective-permute-start | bytes 1544 | tf_op jit(solution)/shard_map/ppermute | solution.py:24
  25.4 6.8 %collective-permute-start.19 = (f32[4,8,1]{2,1,0:T(8,128)S(1)}, f32[4,8,1]{2,1,0:T(8,128)S(1)}, u32[]{:S(2)}, u32[]{:S(2)}) collective-permute-start(f32[4,8,1]{2,1,0:T(8,128)S(1)} %get-tuple-element.61), channel_id=1, source_target_pairs={{8,0},{16,8},{24,16},{9,1},{17,9},{25,17},{10,2},{18,10},{26,18},{... | collective-permute-start | bytes 392 | tf_op jit(solution)/shard_map/ppermute | solution.py:24
  27.3 8.8 %collective-permute-start.18 = (f32[4,8,1]{2,1,0:T(8,128)S(1)}, f32[4,8,1]{2,1,0:T(8,128)S(1)}, u32[]{:S(2)}, u32[]{:S(2)}) collective-permute-start(f32[4,8,1]{2,1,0:T(8,128)S(1)} %get-tuple-element.60), channel_id=1, source_target_pairs={{0,8},{8,16},{16,24},{1,9},{9,17},{17,25},{2,10},{10,18},{18,26},{... | collective-permute-start | bytes 392 | tf_op jit(solution)/shard_map/ppermute | solution.py:22
  32.1 6.6 %collective-permute-start.3 = (f32[8,16,1]{2,1,0:T(8,128)S(1)}, f32[8,16,1]{2,1,0:T(8,128)S(1)}, u32[]{:S(2)}, u32[]{:S(2)}) collective-permute-start(f32[8,16,1]{2,1,0:T(8,128)S(1)} %get-tuple-element.40), channel_id=1, source_target_pairs={{0,8},{8,16},{16,24},{1,9},{9,17},{17,25},{2,10},{10,18},{18,26},{... | collective-permute-start | bytes 1544 | tf_op jit(solution)/shard_map/ppermute | solution.py:22
  36.1 17.9 %collective-permute-start.20 = (f32[1,8,130]{2,1,0:T(8,128)S(1)}, f32[1,8,130]{2,1,0:T(8,128)S(1)}, u32[]{:S(2)}, u32[]{:S(2)}) collective-permute-start(f32[1,8,130]{2,1,0:T(8,128)S(1)} %get-tuple-element.55), channel_id=1, source_target_pairs={{0,4},{1,5},{2,6},{3,7},{8,12},{9,13},{10,14},{11,15},{16,20},{17,... | collective-permute-start | bytes 12488 | tf_op jit(solution)/shard_map/ppermute | solution.py:22
  37.4 20.5 %collective-permute-start.21 = (f32[1,8,130]{2,1,0:T(8,128)S(1)}, f32[1,8,130]{2,1,0:T(8,128)S(1)}, u32[]{:S(2)}, u32[]{:S(2)}) collective-permute-start(f32[1,8,130]{2,1,0:T(8,128)S(1)} %get-tuple-element.54), channel_id=1, source_target_pairs={{4,0},{5,1},{6,2},{7,3},{12,8},{13,9},{14,10},{15,11},{20,16},{21,... | collective-permute-start | bytes 12488 | tf_op jit(solution)/shard_map/ppermute | solution.py:24
  38.9 5.8 %collective-permute-start.7 = (f32[1,16,258]{2,1,0:T(8,128)S(1)}, f32[1,16,258]{2,1,0:T(8,128)S(1)}, u32[]{:S(2)}, u32[]{:S(2)}) collective-permute-start(f32[1,16,258]{2,1,0:T(8,128)S(1)} %get-tuple-element.33), channel_id=1, source_target_pairs={{4,0},{5,1},{6,2},{7,3},{12,8},{13,9},{14,10},{15,11},{20,16},{21,... | collective-permute-start | bytes 49544 | tf_op jit(solution)/shard_map/ppermute | solution.py:24
  40.2 5.8 %collective-permute-start.5 = (f32[1,16,258]{2,1,0:T(8,128)S(1)}, f32[1,16,258]{2,1,0:T(8,128)S(1)}, u32[]{:S(2)}, u32[]{:S(2)}) collective-permute-start(f32[1,16,258]{2,1,0:T(8,128)S(1)} %get-tuple-element.32), channel_id=1, source_target_pairs={{0,4},{1,5},{2,6},{3,7},{8,12},{9,13},{10,14},{11,15},{16,20},{17,... | collective-permute-start | bytes 49544 | tf_op jit(solution)/shard_map/ppermute | solution.py:22
  43.3 5.1 %collective-permute-start.2 = (f32[1,16,258]{2,1,0:T(8,128)S(1)}, f32[1,16,258]{2,1,0:T(8,128)S(1)}, u32[]{:S(2)}, u32[]{:S(2)}) collective-permute-start(f32[1,16,258]{2,1,0:T(8,128)S(1)} %get-tuple-element.31), channel_id=1, source_target_pairs={{0,4},{1,5},{2,6},{3,7},{8,12},{9,13},{10,14},{11,15},{16,20},{17,... | collective-permute-start | bytes 49544 | tf_op jit(solution)/shard_map/ppermute | solution.py:22
  44.6 7.3 %collective-permute-start.6 = (f32[1,16,258]{2,1,0:T(8,128)S(1)}, f32[1,16,258]{2,1,0:T(8,128)S(1)}, u32[]{:S(2)}, u32[]{:S(2)}) collective-permute-start(f32[1,16,258]{2,1,0:T(8,128)S(1)} %get-tuple-element.30), channel_id=1, source_target_pairs={{4,0},{5,1},{6,2},{7,3},{12,8},{13,9},{14,10},{15,11},{20,16},{21,... | collective-permute-start | bytes 49544 | tf_op jit(solution)/shard_map/ppermute | solution.py:24
  46.1 13.9 %collective-permute-start.11 = (f32[10,1,258]{2,1,0:T(1,128)S(1)}, f32[10,1,258]{2,1,0:T(1,128)S(1)}, u32[]{:S(2)}, u32[]{:S(2)}) collective-permute-start(f32[10,1,258]{2,1,0:T(1,128)S(1)} %get-tuple-element.23), channel_id=1, source_target_pairs={{1,0},{2,1},{3,2},{5,4},{6,5},{7,6},{9,8},{10,9},{11,10},{13,12},{... | collective-permute-start | bytes 30968 | tf_op jit(solution)/shard_map/ppermute | solution.py:24
  48.5 15.5 %collective-permute-start.9 = (f32[10,1,258]{2,1,0:T(1,128)S(1)}, f32[10,1,258]{2,1,0:T(1,128)S(1)}, u32[]{:S(2)}, u32[]{:S(2)}) collective-permute-start(f32[10,1,258]{2,1,0:T(1,128)S(1)} %get-tuple-element.22), channel_id=1, source_target_pairs={{0,1},{1,2},{2,3},{4,5},{5,6},{6,7},{8,9},{9,10},{10,11},{12,13},{... | collective-permute-start | bytes 30968 | tf_op jit(solution)/shard_map/ppermute | solution.py:22
  52.1 11.9 %collective-permute-start.8 = (f32[10,1,258]{2,1,0:T(1,128)S(1)}, f32[10,1,258]{2,1,0:T(1,128)S(1)}, u32[]{:S(2)}, u32[]{:S(2)}) collective-permute-start(f32[10,1,258]{2,1,0:T(1,128)S(1)} %get-tuple-element.21), channel_id=1, source_target_pairs={{0,1},{1,2},{2,3},{4,5},{5,6},{6,7},{8,9},{9,10},{10,11},{12,13},{... | collective-permute-start | bytes 30968 | tf_op jit(solution)/shard_map/ppermute | solution.py:22
  54.0 9.9 %collective-permute-start.10 = (f32[10,1,258]{2,1,0:T(1,128)S(1)}, f32[10,1,258]{2,1,0:T(1,128)S(1)}, u32[]{:S(2)}, u32[]{:S(2)}) collective-permute-start(f32[10,1,258]{2,1,0:T(1,128)S(1)} %get-tuple-element.20), channel_id=1, source_target_pairs={{1,0},{2,1},{3,2},{5,4},{6,5},{7,6},{9,8},{10,9},{11,10},{13,12},{... | collective-permute-start | bytes 30968 | tf_op jit(solution)/shard_map/ppermute | solution.py:24
  58.1 20.2 %collective-permute-start.22 = (f32[6,1,130]{2,1,0:T(1,128)S(1)}, f32[6,1,130]{2,1,0:T(1,128)S(1)}, u32[]{:S(2)}, u32[]{:S(2)}) collective-permute-start(f32[6,1,130]{2,1,0:T(1,128)S(1)} %get-tuple-element.49), channel_id=1, source_target_pairs={{0,1},{1,2},{2,3},{4,5},{5,6},{6,7},{8,9},{9,10},{10,11},{12,13},{... | collective-permute-start | bytes 9368 | tf_op jit(solution)/shard_map/ppermute | solution.py:22
  60.0 18.3 %collective-permute-start.23 = (f32[6,1,130]{2,1,0:T(1,128)S(1)}, f32[6,1,130]{2,1,0:T(1,128)S(1)}, u32[]{:S(2)}, u32[]{:S(2)}) collective-permute-start(f32[6,1,130]{2,1,0:T(1,128)S(1)} %get-tuple-element.48), channel_id=1, source_target_pairs={{1,0},{2,1},{3,2},{5,4},{6,5},{7,6},{9,8},{10,9},{11,10},{13,12},{... | collective-permute-start | bytes 9368 | tf_op jit(solution)/shard_map/ppermute | solution.py:24
  78.5 13.6 %collective-permute-start.25 = (f32[4,8,1]{2,1,0:T(8,128)S(1)}, f32[4,8,1]{2,1,0:T(8,128)S(1)}, u32[]{:S(2)}, u32[]{:S(2)}) collective-permute-start(f32[4,8,1]{2,1,0:T(8,128)S(1)} %get-tuple-element.59), channel_id=1, source_target_pairs={{8,0},{16,8},{24,16},{9,1},{17,9},{25,17},{10,2},{18,10},{26,18},{... | collective-permute-start | bytes 392 | tf_op jit(solution)/shard_map/ppermute | solution.py:24
  80.4 11.7 %collective-permute-start.24 = (f32[4,8,1]{2,1,0:T(8,128)S(1)}, f32[4,8,1]{2,1,0:T(8,128)S(1)}, u32[]{:S(2)}, u32[]{:S(2)}) collective-permute-start(f32[4,8,1]{2,1,0:T(8,128)S(1)} %get-tuple-element.58), channel_id=1, source_target_pairs={{0,8},{8,16},{16,24},{1,9},{9,17},{17,25},{2,10},{10,18},{18,26},{... | collective-permute-start | bytes 392 | tf_op jit(solution)/shard_map/ppermute | solution.py:22
  85.3 11.2 %collective-permute-start.13 = (f32[8,16,1]{2,1,0:T(8,128)S(1)}, f32[8,16,1]{2,1,0:T(8,128)S(1)}, u32[]{:S(2)}, u32[]{:S(2)}) collective-permute-start(f32[8,16,1]{2,1,0:T(8,128)S(1)} %get-tuple-element.39), channel_id=1, source_target_pairs={{8,0},{16,8},{24,16},{9,1},{17,9},{25,17},{10,2},{18,10},{26,18},{... | collective-permute-start | bytes 1544 | tf_op jit(solution)/shard_map/ppermute | solution.py:24
  87.2 9.3 %collective-permute-start.12 = (f32[8,16,1]{2,1,0:T(8,128)S(1)}, f32[8,16,1]{2,1,0:T(8,128)S(1)}, u32[]{:S(2)}, u32[]{:S(2)}) collective-permute-start(f32[8,16,1]{2,1,0:T(8,128)S(1)} %get-tuple-element.38), channel_id=1, source_target_pairs={{0,8},{8,16},{16,24},{1,9},{9,17},{17,25},{2,10},{10,18},{18,26},{... | collective-permute-start | bytes 1544 | tf_op jit(solution)/shard_map/ppermute | solution.py:22
  92.1 8.8 %collective-permute-start.27 = (f32[1,8,130]{2,1,0:T(8,128)S(1)}, f32[1,8,130]{2,1,0:T(8,128)S(1)}, u32[]{:S(2)}, u32[]{:S(2)}) collective-permute-start(f32[1,8,130]{2,1,0:T(8,128)S(1)} %get-tuple-element.53), channel_id=1, source_target_pairs={{4,0},{5,1},{6,2},{7,3},{12,8},{13,9},{14,10},{15,11},{20,16},{21,... | collective-permute-start | bytes 12488 | tf_op jit(solution)/shard_map/ppermute | solution.py:24
  93.4 7.5 %collective-permute-start.26 = (f32[1,8,130]{2,1,0:T(8,128)S(1)}, f32[1,8,130]{2,1,0:T(8,128)S(1)}, u32[]{:S(2)}, u32[]{:S(2)}) collective-permute-start(f32[1,8,130]{2,1,0:T(8,128)S(1)} %get-tuple-element.52), channel_id=1, source_target_pairs={{0,4},{1,5},{2,6},{3,7},{8,12},{9,13},{10,14},{11,15},{16,20},{17,... | collective-permute-start | bytes 12488 | tf_op jit(solution)/shard_map/ppermute | solution.py:22
  96.6 10.3 %collective-permute-start.15 = (f32[1,16,258]{2,1,0:T(8,128)S(1)}, f32[1,16,258]{2,1,0:T(8,128)S(1)}, u32[]{:S(2)}, u32[]{:S(2)}) collective-permute-start(f32[1,16,258]{2,1,0:T(8,128)S(1)} %get-tuple-element.29), channel_id=1, source_target_pairs={{4,0},{5,1},{6,2},{7,3},{12,8},{13,9},{14,10},{15,11},{20,16},{21,... | collective-permute-start | bytes 49544 | tf_op jit(solution)/shard_map/ppermute | solution.py:24
  97.9 9.0 %collective-permute-start.14 = (f32[1,16,258]{2,1,0:T(8,128)S(1)}, f32[1,16,258]{2,1,0:T(8,128)S(1)}, u32[]{:S(2)}, u32[]{:S(2)}) collective-permute-start(f32[1,16,258]{2,1,0:T(8,128)S(1)} %get-tuple-element.28), channel_id=1, source_target_pairs={{0,4},{1,5},{2,6},{3,7},{8,12},{9,13},{10,14},{11,15},{16,20},{17,... | collective-permute-start | bytes 49544 | tf_op jit(solution)/shard_map/ppermute | solution.py:22
  101.0 11.9 %collective-permute-start.29 = (f32[6,1,130]{2,1,0:T(1,128)S(1)}, f32[6,1,130]{2,1,0:T(1,128)S(1)}, u32[]{:S(2)}, u32[]{:S(2)}) collective-permute-start(f32[6,1,130]{2,1,0:T(1,128)S(1)} %get-tuple-element.47), channel_id=1, source_target_pairs={{1,0},{2,1},{3,2},{5,4},{6,5},{7,6},{9,8},{10,9},{11,10},{13,12},{... | collective-permute-start | bytes 9368 | tf_op jit(solution)/shard_map/ppermute | solution.py:24
  103.4 9.5 %collective-permute-start.28 = (f32[6,1,130]{2,1,0:T(1,128)S(1)}, f32[6,1,130]{2,1,0:T(1,128)S(1)}, u32[]{:S(2)}, u32[]{:S(2)}) collective-permute-start(f32[6,1,130]{2,1,0:T(1,128)S(1)} %get-tuple-element.46), channel_id=1, source_target_pairs={{0,1},{1,2},{2,3},{4,5},{5,6},{6,7},{8,9},{9,10},{10,11},{12,13},{... | collective-permute-start | bytes 9368 | tf_op jit(solution)/shard_map/ppermute | solution.py:22
  107.1 16.9 %collective-permute-start.17 = (f32[10,1,258]{2,1,0:T(1,128)S(1)}, f32[10,1,258]{2,1,0:T(1,128)S(1)}, u32[]{:S(2)}, u32[]{:S(2)}) collective-permute-start(f32[10,1,258]{2,1,0:T(1,128)S(1)} %get-tuple-element.19), channel_id=1, source_target_pairs={{1,0},{2,1},{3,2},{5,4},{6,5},{7,6},{9,8},{10,9},{11,10},{13,12},{... | collective-permute-start | bytes 30968 | tf_op jit(solution)/shard_map/ppermute | solution.py:24
  109.4 14.5 %collective-permute-start.16 = (f32[10,1,258]{2,1,0:T(1,128)S(1)}, f32[10,1,258]{2,1,0:T(1,128)S(1)}, u32[]{:S(2)}, u32[]{:S(2)}) collective-permute-start(f32[10,1,258]{2,1,0:T(1,128)S(1)} %get-tuple-element.18), channel_id=1, source_target_pairs={{0,1},{1,2},{2,3},{4,5},{5,6},{6,7},{8,9},{9,10},{10,11},{12,13},{... | collective-permute-start | bytes 30968 | tf_op jit(solution)/shard_map/ppermute | solution.py:22
  124.4 7.1 %collective-permute-start.31 = (f32[8,16,1]{2,1,0:T(8,128)S(1)}, f32[8,16,1]{2,1,0:T(8,128)S(1)}, u32[]{:S(2)}, u32[]{:S(2)}) collective-permute-start(f32[8,16,1]{2,1,0:T(8,128)S(1)} %get-tuple-element.37), channel_id=1, source_target_pairs={{8,0},{16,8},{24,16},{9,1},{17,9},{25,17},{10,2},{18,10},{26,18},{... | collective-permute-start | bytes 1544 | tf_op jit(solution)/shard_map/ppermute | solution.py:24
  126.3 6.7 %collective-permute-start.30 = (f32[8,16,1]{2,1,0:T(8,128)S(1)}, f32[8,16,1]{2,1,0:T(8,128)S(1)}, u32[]{:S(2)}, u32[]{:S(2)}) collective-permute-start(f32[8,16,1]{2,1,0:T(8,128)S(1)} %get-tuple-element.36), channel_id=1, source_target_pairs={{0,8},{8,16},{16,24},{1,9},{9,17},{17,25},{2,10},{10,18},{18,26},{... | collective-permute-start | bytes 1544 | tf_op jit(solution)/shard_map/ppermute | solution.py:22
  133.1 4.3 %collective-permute-start.33 = (f32[1,16,258]{2,1,0:T(8,128)S(1)}, f32[1,16,258]{2,1,0:T(8,128)S(1)}, u32[]{:S(2)}, u32[]{:S(2)}) collective-permute-start(f32[1,16,258]{2,1,0:T(8,128)S(1)} %get-tuple-element.27), channel_id=1, source_target_pairs={{4,0},{5,1},{6,2},{7,3},{12,8},{13,9},{14,10},{15,11},{20,16},{21,... | collective-permute-start | bytes 49544 | tf_op jit(solution)/shard_map/ppermute | solution.py:24
  134.4 3.9 %collective-permute-start.32 = (f32[1,16,258]{2,1,0:T(8,128)S(1)}, f32[1,16,258]{2,1,0:T(8,128)S(1)}, u32[]{:S(2)}, u32[]{:S(2)}) collective-permute-start(f32[1,16,258]{2,1,0:T(8,128)S(1)} %get-tuple-element.26), channel_id=1, source_target_pairs={{0,4},{1,5},{2,6},{3,7},{8,12},{9,13},{10,14},{11,15},{16,20},{17,... | collective-permute-start | bytes 49544 | tf_op jit(solution)/shard_map/ppermute | solution.py:22
  138.4 5.9 %collective-permute-start.35 = (f32[10,1,258]{2,1,0:T(1,128)S(1)}, f32[10,1,258]{2,1,0:T(1,128)S(1)}, u32[]{:S(2)}, u32[]{:S(2)}) collective-permute-start(f32[10,1,258]{2,1,0:T(1,128)S(1)} %get-tuple-element.17), channel_id=1, source_target_pairs={{1,0},{2,1},{3,2},{5,4},{6,5},{7,6},{9,8},{10,9},{11,10},{13,12},{... | collective-permute-start | bytes 30968 | tf_op jit(solution)/shard_map/ppermute | solution.py:24
  140.8 5.6 %collective-permute-start.34 = (f32[10,1,258]{2,1,0:T(1,128)S(1)}, f32[10,1,258]{2,1,0:T(1,128)S(1)}, u32[]{:S(2)}, u32[]{:S(2)}) collective-permute-start(f32[10,1,258]{2,1,0:T(1,128)S(1)} %get-tuple-element.16), channel_id=1, source_target_pairs={{0,1},{1,2},{2,3},{4,5},{5,6},{6,7},{8,9},{9,10},{10,11},{12,13},{... | collective-permute-start | bytes 30968 | tf_op jit(solution)/shard_map/ppermute | solution.py:22
  160.8 14.1 %collective-permute-start.43 = (f32[4,8,1]{2,1,0:T(8,128)S(1)}, f32[4,8,1]{2,1,0:T(8,128)S(1)}, u32[]{:S(2)}, u32[]{:S(2)}) collective-permute-start(f32[4,8,1]{2,1,0:T(8,128)S(1)} %get-tuple-element.57), channel_id=1, source_target_pairs={{8,0},{16,8},{24,16},{9,1},{17,9},{25,17},{10,2},{18,10},{26,18},{... | collective-permute-start | bytes 392 | tf_op jit(solution)/shard_map/ppermute | solution.py:24
  162.7 12.2 %collective-permute-start.42 = (f32[4,8,1]{2,1,0:T(8,128)S(1)}, f32[4,8,1]{2,1,0:T(8,128)S(1)}, u32[]{:S(2)}, u32[]{:S(2)}) collective-permute-start(f32[4,8,1]{2,1,0:T(8,128)S(1)} %get-tuple-element.56), channel_id=1, source_target_pairs={{0,8},{8,16},{16,24},{1,9},{9,17},{17,25},{2,10},{10,18},{18,26},{... | collective-permute-start | bytes 392 | tf_op jit(solution)/shard_map/ppermute | solution.py:22
  168.1 11.2 %collective-permute-start.37 = (f32[8,16,1]{2,1,0:T(8,128)S(1)}, f32[8,16,1]{2,1,0:T(8,128)S(1)}, u32[]{:S(2)}, u32[]{:S(2)}) collective-permute-start(f32[8,16,1]{2,1,0:T(8,128)S(1)} %get-tuple-element.35), channel_id=1, source_target_pairs={{8,0},{16,8},{24,16},{9,1},{17,9},{25,17},{10,2},{18,10},{26,18},{... | collective-permute-start | bytes 1544 | tf_op jit(solution)/shard_map/ppermute | solution.py:24
  170.1 9.3 %collective-permute-start.36 = (f32[8,16,1]{2,1,0:T(8,128)S(1)}, f32[8,16,1]{2,1,0:T(8,128)S(1)}, u32[]{:S(2)}, u32[]{:S(2)}) collective-permute-start(f32[8,16,1]{2,1,0:T(8,128)S(1)} %get-tuple-element.34), channel_id=1, source_target_pairs={{0,8},{8,16},{16,24},{1,9},{9,17},{17,25},{2,10},{10,18},{18,26},{... | collective-permute-start | bytes 1544 | tf_op jit(solution)/shard_map/ppermute | solution.py:22
  175.0 8.8 %collective-permute-start.45 = (f32[1,8,130]{2,1,0:T(8,128)S(1)}, f32[1,8,130]{2,1,0:T(8,128)S(1)}, u32[]{:S(2)}, u32[]{:S(2)}) collective-permute-start(f32[1,8,130]{2,1,0:T(8,128)S(1)} %get-tuple-element.51), channel_id=1, source_target_pairs={{4,0},{5,1},{6,2},{7,3},{12,8},{13,9},{14,10},{15,11},{20,16},{21,... | collective-permute-start | bytes 12488 | tf_op jit(solution)/shard_map/ppermute | solution.py:24
  176.3 7.5 %collective-permute-start.44 = (f32[1,8,130]{2,1,0:T(8,128)S(1)}, f32[1,8,130]{2,1,0:T(8,128)S(1)}, u32[]{:S(2)}, u32[]{:S(2)}) collective-permute-start(f32[1,8,130]{2,1,0:T(8,128)S(1)} %get-tuple-element.50), channel_id=1, source_target_pairs={{0,4},{1,5},{2,6},{3,7},{8,12},{9,13},{10,14},{11,15},{16,20},{17,... | collective-permute-start | bytes 12488 | tf_op jit(solution)/shard_map/ppermute | solution.py:22
  179.4 10.3 %collective-permute-start.39 = (f32[1,16,258]{2,1,0:T(8,128)S(1)}, f32[1,16,258]{2,1,0:T(8,128)S(1)}, u32[]{:S(2)}, u32[]{:S(2)}) collective-permute-start(f32[1,16,258]{2,1,0:T(8,128)S(1)} %get-tuple-element.25), channel_id=1, source_target_pairs={{4,0},{5,1},{6,2},{7,3},{12,8},{13,9},{14,10},{15,11},{20,16},{21,... | collective-permute-start | bytes 49544 | tf_op jit(solution)/shard_map/ppermute | solution.py:24
  180.7 9.0 %collective-permute-start.38 = (f32[1,16,258]{2,1,0:T(8,128)S(1)}, f32[1,16,258]{2,1,0:T(8,128)S(1)}, u32[]{:S(2)}, u32[]{:S(2)}) collective-permute-start(f32[1,16,258]{2,1,0:T(8,128)S(1)} %get-tuple-element.24), channel_id=1, source_target_pairs={{0,4},{1,5},{2,6},{3,7},{8,12},{9,13},{10,14},{11,15},{16,20},{17,... | collective-permute-start | bytes 49544 | tf_op jit(solution)/shard_map/ppermute | solution.py:22
  183.9 11.9 %collective-permute-start.47 = (f32[6,1,130]{2,1,0:T(1,128)S(1)}, f32[6,1,130]{2,1,0:T(1,128)S(1)}, u32[]{:S(2)}, u32[]{:S(2)}) collective-permute-start(f32[6,1,130]{2,1,0:T(1,128)S(1)} %get-tuple-element.45), channel_id=1, source_target_pairs={{1,0},{2,1},{3,2},{5,4},{6,5},{7,6},{9,8},{10,9},{11,10},{13,12},{... | collective-permute-start | bytes 9368 | tf_op jit(solution)/shard_map/ppermute | solution.py:24
  185.8 10.0 %collective-permute-start.46 = (f32[6,1,130]{2,1,0:T(1,128)S(1)}, f32[6,1,130]{2,1,0:T(1,128)S(1)}, u32[]{:S(2)}, u32[]{:S(2)}) collective-permute-start(f32[6,1,130]{2,1,0:T(1,128)S(1)} %get-tuple-element.44), channel_id=1, source_target_pairs={{0,1},{1,2},{2,3},{4,5},{5,6},{6,7},{8,9},{9,10},{10,11},{12,13},{... | collective-permute-start | bytes 9368 | tf_op jit(solution)/shard_map/ppermute | solution.py:22
  189.9 16.9 %collective-permute-start.41 = (f32[10,1,258]{2,1,0:T(1,128)S(1)}, f32[10,1,258]{2,1,0:T(1,128)S(1)}, u32[]{:S(2)}, u32[]{:S(2)}) collective-permute-start(f32[10,1,258]{2,1,0:T(1,128)S(1)} %get-tuple-element.15), channel_id=1, source_target_pairs={{1,0},{2,1},{3,2},{5,4},{6,5},{7,6},{9,8},{10,9},{11,10},{13,12},{... | collective-permute-start | bytes 30968 | tf_op jit(solution)/shard_map/ppermute | solution.py:24
  191.8 15.0 %collective-permute-start.40 = (f32[10,1,258]{2,1,0:T(1,128)S(1)}, f32[10,1,258]{2,1,0:T(1,128)S(1)}, u32[]{:S(2)}, u32[]{:S(2)}) collective-permute-start(f32[10,1,258]{2,1,0:T(1,128)S(1)} %get-tuple-element.14), channel_id=1, source_target_pairs={{0,1},{1,2},{2,3},{4,5},{5,6},{6,7},{8,9},{9,10},{10,11},{12,13},{... | collective-permute-start | bytes 30968 | tf_op jit(solution)/shard_map/ppermute | solution.py:22
  (3 other events, 119.9 us)
where the time goes:
time: 210 us; the launch traced here: 208 us
  starting transfers between devices  131 us (62%)
  local copies, waits for them, and re-layouts  54.1 us (26%)
  other arithmetic  16.6 us (8%)
  waiting for transfers between devices  4.94 us (2%)
    ppermute x24, starting transfers between devices, extended(): lax.ppermute(tail, axis, [(i, (i + 1) % count) for i in range(ends)])  84 us
    ppermute x24, starting transfers between devices, extended(): lax.ppermute(head, axis, [((i + 1) % count, i) for i in range(ends)])  47.4 us
    reshape x3, local copies, waits for them, and re-layouts, block_mean(): field.reshape(sizea // 2, 2, sizeb // 2, 2, sizec // 2, 2)  30.1 us
    reshape x2, local copies, waits for them, and re-layouts, prolong(): return spread.reshape(2 * sizea, 2 * sizeb, 2 * sizec)  13.9 us
    reduce_sum x3, other arithmetic, block_mean(): field.reshape(sizea // 2, 2, sizeb // 2, 2, sizec // 2, 2)  12.1 us
    broadcast_in_dim x2, local copies, waits for them, and re-layouts, prolong(): jnp.broadcast_to(coarse[:, None, :, None, :, None], (sizea, 2, sizeb, 2,...  7.8 us
    ppermute x24, waiting for transfers between devices, extended(): lax.ppermute(tail, axis, [(i, (i + 1) % count) for i in range(ends)])  4.58 us
  transfers between devices with their start and end apart: 48, of which 4 were waited for; matrix products, arithmetic and copies ran while one was open for 26% of the time, Pallas kernels for 0%

commit v1 on v0

v1 whole, which is shorter than its diff:
```python
import functools

import jax
import jax.numpy as jnp
from jax import lax
from jax.experimental import pallas as pl
from jax.experimental.pallas import tpu as pltpu
from jax.sharding import PartitionSpec as P

ITERS = 2
HALO = 4 * ITERS
LANES = 128
KEEP = 48.0 / 41.0
SPREAD = 32.0 / 41.0
VMEM = pl.BlockSpec(memory_space=pltpu.VMEM)


def ahead(v, axis, n=1):
    return pltpu.roll(v, v.shape[axis] - n, axis)


def behind(v, axis, n=1):
    return pltpu.roll(v, n, axis)


def swaps(axis, count):
    rounds = []
    for start in (0, 1):
        pairs = [(i, i + 1) for i in range(start, count - 1, 2)]
        if pairs:
            rounds.append(pairs + [(j, i) for i, j in pairs])
    return rounds


def is_odd(axis):
    return lax.rem(lax.axis_index(axis), 2)


def pack_rows(s, c, f, first, second):
    odd = is_odd("gy")
    last = s.shape[1] - HALO
    row_a = pl.multiple_of((1 - odd) * last, 8)
    row_b = pl.multiple_of(odd * last, 8)
    for a, ref in enumerate((s, c, f)):
        first[a] = ref[:, pl.ds(row_a, HALO), :]
        second[a] = ref[:, pl.ds(row_b, HALO), :]


def slots(rows):
    return [(a, g, a * (rows // 8) + g) for a in range(3) for g in range(rows // 8)]


def pack_columns(s, c, f, got_a, got_b, block, first, second):
    odd_y = is_odd("gy")
    odd_z = is_odd("grp")
    depth, own, width = s.shape
    rows = own + 2 * HALO
    for a, ref in enumerate((s, c, f)):
        block[a, :, HALO : HALO + own, :] = ref[...]
        from_a, from_b = got_a[a], got_b[a]
        block[a, :, 0:HALO, :] = jnp.where(odd_y == 1, from_a, from_b)
        block[a, :, HALO + own : rows, :] = jnp.where(odd_y == 1, from_b, from_a)
    lane = lax.broadcasted_iota(jnp.int32, (8, LANES), 1)

    def plane(p, carry):
        heads = [jnp.zeros((8, LANES), jnp.float32) for _ in range(first.shape[0])]
        tails = list(heads)
        for a, g, slot in slots(rows):
            at = 8 * (slot % 16)
            mine = (lane >= at) & (lane < at + HALO)
            head = pltpu.roll(block[a, p, 8 * g : 8 * g + 8, 0:LANES], at, 1)
            tail = pltpu.roll(
                block[a, p, 8 * g : 8 * g + 8, width - LANES : width], (at + HALO) % LANES, 1
            )
            heads[slot // 16] = jnp.where(mine, head, heads[slot // 16])
            tails[slot // 16] = jnp.where(mine, tail, tails[slot // 16])
        for t, (head, tail) in enumerate(zip(heads, tails)):
            first[t, p] = jnp.where(odd_z == 1, head, tail)
            second[t, p] = jnp.where(odd_z == 1, tail, head)
        return carry

    lax.fori_loop(0, depth, plane, 0)


def solve(cells, own_at, own, out):
    (src, cond, field, wx, wy, wz, inv, sum8, cwx, cwy, cwz, cinv, res, q, cq, err) = cells
    total = cond.shape[0]
    rows, lanes = cond.shape[1:]

    def reach(halo):
        low = max(1, own_at - halo)
        high = min(total, own_at + own + halo)
        return (low + 1) // 2, (high + 1) // 2

    zero = jnp.zeros((rows, lanes), jnp.float32)
    for ref in (q, cq, err, sum8):
        ref[0] = zero

    def gather8(k, carry):
        t = cond[2 * k - 1] + cond[2 * k]
        t = t + ahead(t, 0)
        sum8[k] = t + ahead(t, 1)
        return carry

    lax.fori_loop(*reach(HALO), gather8, 0)

    def weights(c, below, above, step):
        x = c + above
        y = c + ahead(c, 0, step)
        z = c + ahead(c, 1, step)
        k = (c + below + x) + (y + behind(y, 0, step)) + (z + behind(z, 1, step))
        return x, y, z, jnp.where(c > 0.0, 1.0 / k, 0.0)

    def setup(k, carry):
        for p in (2 * k - 1, 2 * k):
            wx[p], wy[p], wz[p], inv[p] = weights(cond[p], cond[p - 1], cond[p + 1], 1)
        cwx[k], cwy[k], cwz[k], cinv[k] = weights(sum8[k], sum8[k - 1], sum8[k + 1], 2)
        return carry

    low, high = reach(HALO - 2)
    wx[2 * low - 2] = cond[2 * low - 2] + cond[2 * low - 1]
    cwx[low - 1] = sum8[low - 1] + sum8[low]
    lax.fori_loop(low, high, setup, 0)

    row = lax.broadcasted_iota(jnp.int32, (rows, lanes), 0)
    lane = lax.broadcasted_iota(jnp.int32, (rows, lanes), 1)
    even_row = lax.rem(row, 2) == 0
    even_lane = lax.rem(lane, 2) == 0

    def image(v, p):
        here = v[p]
        across = wx[p - 1] * (here - v[p - 1]) - wx[p] * (v[p + 1] - here)
        fy = wy[p] * (ahead(here, 0) - here)
        fz = wz[p] * (ahead(here, 1) - here)
        return across + (behind(fy, 0) - fy) + (behind(fz, 1) - fz)

    def spread(v, p, x, y, z, step):
        here = v[p]
        n = x[p - 1] * v[p - 1] + x[p] * v[p + 1]
        n = n + (y[p] * ahead(here, 0, step) + behind(y[p] * here, 0, step))
        return n + (z[p] * ahead(here, 1, step) + behind(z[p] * here, 1, step))

    def smooth(v, p, x, y, z, diag, step):
        return KEEP * v[p] + SPREAD * (diag[p] * spread(v, p, x, y, z, step))

    for it in range(ITERS):
        halo = 4 * (ITERS - 1 - it)

        def residuals(k, carry, it=it):
            both = None
            for p in (2 * k - 1, 2 * k):
                if it == 0:
                    r = 2.0 * src[p] - image(field, p)
                else:
                    r = res[p] - image(err, p)
                res[p] = r
                q[p] = r * inv[p]
                both = r if both is None else both + r
            both = both + ahead(both, 0)
            both = both + ahead(both, 1)
            cq[k] = (4.0 * both) * cinv[k]
            return carry

        lax.fori_loop(*reach(halo + 2), residuals, 0)

        def corrections(k, carry, it=it):
            coarse = smooth(cq, k, cwx, cwy, cwz, cinv, 2)
            coarse = jnp.where(even_lane, coarse, behind(coarse, 1))
            coarse = jnp.where(even_row, coarse, behind(coarse, 0))
            for p in (2 * k - 1, 2 * k):
                e = smooth(q, p, wx, wy, wz, inv, 1) + coarse
                if it < ITERS - 1:
                    err[p] = err[p] + e if it else e
                else:
                    out(p, field[p] + (err[p] + e if it else e))
            return carry

        lax.fori_loop(*reach(halo), corrections, 0)


def finish(reflect, n_x, *refs):
    block = refs[0]
    near = refs[1 : 1 + n_x]
    got = refs[1 + n_x : 3 + n_x]
    near_got = refs[3 + n_x : 3 + 2 * n_x]
    result = refs[3 + 2 * n_x]
    cells = refs[4 + 2 * n_x :]
    _, depth, rows, width = block.shape
    odd_x = is_odd("gx")
    odd_z = is_odd("grp")
    own_at = 1 if reflect else 1 + HALO
    tiles = [cells[0], cells[1], cells[2]]
    lane = lax.broadcasted_iota(jnp.int32, (8, LANES), 1)

    def place(src, src_a, src_b, p_from, p_to):
        for a in range(3):
            tiles[a][p_to, :, 0:width] = src[a, p_from]
        for t in range(src_a.shape[0]):
            va, vb = src_a[t, p_from], src_b[t, p_from]
            upper = jnp.where(odd_z == 1, vb, va)
            lower = jnp.where(odd_z == 1, va, vb)
            for a, g, slot in slots(rows):
                if slot // 16 == t:
                    at = 8 * (slot % 16)
                    right = pltpu.roll(upper, (LANES - at) % LANES, 1)
                    left = pltpu.roll(lower, (2 * LANES - HALO - at) % LANES, 1)
                    tile = jnp.where(lane >= LANES - HALO, left, 0.0)
                    tile = jnp.where(lane < HALO, right, tile)
                    tiles[a][p_to, 8 * g : 8 * g + 8, width : width + LANES] = tile

    zero = jnp.zeros(tiles[0].shape[1:], jnp.float32)
    for tile in tiles:
        tile[0] = zero

    def own_plane(p, carry):
        to = jnp.where(odd_x == 1, depth - 1 - p, p) if reflect else p
        place(block, got[0], got[1], p, own_at + to)
        return carry

    lax.fori_loop(0, depth, own_plane, 0)

    def near_plane(p, carry):
        if reflect:
            at = jnp.where(odd_x == 1, depth - 1 - p, p)
            place(near[0], near_got[0].at[0], near_got[0].at[1], at, 1 + depth + p)
        else:
            for i in range(2):
                above = odd_x == i
                at = jnp.where(above, p, depth - HALO + p)
                to = jnp.where(above, own_at + depth + p, 1 + p)
                place(near[i], near_got[i].at[0], near_got[i].at[1], at, to)
        return carry

    lax.fori_loop(0, HALO, near_plane, 0)

    def out(p, v):
        at = p - own_at
        if reflect:
            at = jnp.where(odd_x == 1, depth - 1 - at, at)
        result[at] = v[HALO : rows - HALO, 0:width]

    solve(cells, own_at, depth, out)


def shards(sizes, source_term, conductivity, initial_field):
    depth, own, width = source_term.shape
    rows = own + 2 * HALO
    f32 = jnp.float32
    params = pltpu.CompilerParams(vmem_limit_bytes=48 * 1024 * 1024)
    args = (source_term, conductivity, initial_field)

    face = jax.ShapeDtypeStruct((3, depth, HALO, width), f32)
    msgs = pl.pallas_call(
        pack_rows, out_shape=(face, face), in_specs=[VMEM] * 3, out_specs=(VMEM, VMEM),
        compiler_params=params, name="pack_rows",
    )(*args)

    def exchange(values, axis):
        found = [lax.ppermute(v, axis, pairs) for v, pairs in zip(values, swaps(axis, sizes[axis]))]
        return found + [jnp.zeros_like(v) for v in values[len(found) :]]

    got = exchange(msgs, "gy")
    n_tiles = -(-3 * (rows // 8) // 16)
    strip = jax.ShapeDtypeStruct((n_tiles, depth, 8, LANES), f32)
    block, *cols = pl.pallas_call(
        pack_columns,
        out_shape=(jax.ShapeDtypeStruct((3, depth, rows, width), f32), strip, strip),
        in_specs=[VMEM] * 5, out_specs=(VMEM,) * 3,
        compiler_params=params, name="pack_columns",
    )(*args, *got)

    reflect = sizes["gx"] == 2
    n_x = 1 if reflect else 2
    got = exchange(cols, "grp")
    near = exchange([block] * n_x, "gx")
    near_got = exchange([jnp.stack(got)] * n_x, "gx")

    total = 1 + depth + HALO * n_x + 1
    lanes = width + LANES
    fine = pltpu.VMEM((total, rows, lanes), f32)
    coarse = pltpu.VMEM((total // 2 + 1, rows, lanes), f32)
    return pl.pallas_call(
        functools.partial(finish, reflect, n_x),
        out_shape=jax.ShapeDtypeStruct(source_term.shape, f32),
        in_specs=[VMEM] * (3 + 2 * n_x), out_specs=VMEM,
        scratch_shapes=[fine] * 7 + [coarse] * 5 + [fine] * 2 + [coarse] + [fine],
        compiler_params=params, name="finish",
    )(block, *near, *got, *near_got)


def solution(mesh):
    spec = P("gx", "gy", "grp")
    return jax.shard_map(
        functools.partial(shards, dict(mesh.shape)),
        mesh=mesh,
        in_specs=(spec,) * 3,
        out_specs=spec,
        check_vma=False,
    )
```

time: 210 us -> 33.1 us (0.16)
  the two profiles are of different devices: /device:TPU:18 before, /device:TPU:21 now
where the time goes in v1:
time: 33.1 us; the launch traced here: 32.9 us
  Pallas kernels  10.4 us (31%)
  starting transfers between devices  10 us (30%)
  waiting for transfers between devices  9.76 us (29%)
  local copies, waits for them, and re-layouts  2.71 us (8%)
    ppermute x6, starting transfers between devices, exchange(): lax.ppermute(v, axis, pairs)  10 us
    ppermute x6, waiting for transfers between devices, exchange(): lax.ppermute(v, axis, pairs)  9.76 us
    pallas_call x1, Pallas kernels, shards(): pl.pallas_call(functools.partial(finish, reflect, n_x), out_shape=jax.Sha...  9.57 us
    unnamed x6, local copies, waits for them, and re-layouts  2.71 us
    pallas_call x1, Pallas kernels, shards(): pl.pallas_call(pack_columns, out_shape=(jax.ShapeDtypeStruct((3, depth, r...  0.81 us
  transfers between devices with their start and end apart: 6, of which 4 were waited for; matrix products, arithmetic and copies ran while one was open for 0% of the time, Pallas kernels for 0%

profile of v1, /device:TPU:21, one launch (start us, length us, event | category | flops | bytes accessed | tf_op | source)
XLA Modules:
  0.0 32.9 jit_solution(1339435434926202157)
XLA Ops:
  0.0 0.0 copy-start
  0.0 0.9 %copy-done = f32[8,16,256]{2,1,0:T(8,128)S(1)} copy-done((f32[8,16,256]{2,1,0:T(8,128)S(1)}, f32[8,16,256]{2,1,0:T(8,128)}, u32[]{:S(2)}) %copy-start) | copy-done | bytes 131096
  0.9 0.0 copy-start.1
  0.9 0.9 %copy-done.1 = f32[8,16,256]{2,1,0:T(8,128)S(1)} copy-done((f32[8,16,256]{2,1,0:T(8,128)S(1)}, f32[8,16,256]{2,1,0:T(8,128)}, u32[]{:S(2)}) %copy-start.1) | copy-done | bytes 131096
  1.8 0.0 copy-start.2
  1.8 0.9 %copy-done.2 = f32[8,16,256]{2,1,0:T(8,128)S(1)} copy-done((f32[8,16,256]{2,1,0:T(8,128)S(1)}, f32[8,16,256]{2,1,0:T(8,128)}, u32[]{:S(2)}) %copy-start.2) | copy-done | bytes 131096
  2.7 1.4 %collective-permute-start = (f32[3,8,8,256]{3,2,1,0:T(8,128)S(1)}, f32[3,8,8,256]{3,2,1,0:T(8,128)S(1)}, u32[]{:S(2)}, u32[]{:S(2)}) collective-permute-start(f32[3,8,8,256]{3,2,1,0:T(8,128)S(1)} %get-tuple-element.10), channel_id=1, source_target_pairs={{0,1},{2,3},{1,0},{3,2},{4,5},{6,7},{5,4},{7,6},{8,9},{10,11},{9,8... | collective-permute-start | bytes 589832 | tf_op jit(solution)/shard_map/ppermute | solution.py:259
  4.1 1.9 %collective-permute-start.1 = (f32[3,8,8,256]{3,2,1,0:T(8,128)S(1)}, f32[3,8,8,256]{3,2,1,0:T(8,128)S(1)}, u32[]{:S(2)}, u32[]{:S(2)}) collective-permute-start(f32[3,8,8,256]{3,2,1,0:T(8,128)S(1)} %get-tuple-element.11), channel_id=1, source_target_pairs={{1,2},{2,1},{5,6},{6,5},{9,10},{10,9},{13,14},{14,13},{17,18},{18,... | collective-permute-start | bytes 589832 | tf_op jit(solution)/shard_map/ppermute | solution.py:259
  6.0 2.6 %collective-permute-done.got_a = f32[3,8,8,256]{3,2,1,0:T(8,128)S(1)} collective-permute-done((f32[3,8,8,256]{3,2,1,0:T(8,128)S(1)}, f32[3,8,8,256]{3,2,1,0:T(8,128)S(1)}, u32[]{:S(2)}, u32[]{:S(2)}) %collective-permute-start) | collective-permute-done | bytes 196640 | tf_op jit(solution)/shard_map/ppermute | solution.py:259
  8.6 2.9 %collective-permute-done.1.got_b = f32[3,8,8,256]{3,2,1,0:T(8,128)S(1)} collective-permute-done((f32[3,8,8,256]{3,2,1,0:T(8,128)S(1)}, f32[3,8,8,256]{3,2,1,0:T(8,128)S(1)}, u32[]{:S(2)}, u32[]{:S(2)}) %collective-permute-start.1) | collective-permute-done | bytes 196640 | tf_op jit(solution)/shard_map/ppermute | solution.py:259
  11.4 0.8 %pack_columns.1 = (f32[3,8,32,256]{3,2,1,0:T(8,128)S(1)}, f32[1,8,8,128]{3,2,1,0:T(8,128)S(1)}, f32[1,8,8,128]{3,2,1,0:T(8,128)S(1)}) custom-call(f32[8,16,256]{2,1,0:T(8,128)S(1)} %copy-done, f32[8,16,256]{2,1,0:T(8,128)S(1)} %copy-done.1, f32[8,16,256]{2,1,0:T(8,128)S(1)} %copy-done.2, f32[3,8,8,256]{3,2,1,0:T(8,128)S(1)} %collective-permute-done.got_a, ...), custom_call_target="tpu_custom_call" | custom-call | tf_op jit(solution)/shard_map/pack_columns/pallas_call | solution.py:265
  12.3 1.9 %collective-permute-start.2 = (f32[3,8,32,256]{3,2,1,0:T(8,128)S(1)}, f32[3,8,32,256]{3,2,1,0:T(8,128)S(1)}, u32[]{:S(2)}, u32[]{:S(2)}) collective-permute-start(f32[3,8,32,256]{3,2,1,0:T(8,128)S(1)} %get-tuple-element.12.refs_0_), channel_id=1, source_target_pairs={{0,4},{4,0},{1,5},{5,1},{2,6},{6,2},{3,7},{7,3},{8,12},{12,8},{9,1... | collective-permute-start | bytes 2359304 | tf_op jit(solution)/shard_map/ppermute | solution.py:259
  14.2 1.2 %collective-permute-start.3 = (f32[1,8,8,128]{3,2,1,0:T(8,128)S(1)}, f32[1,8,8,128]{3,2,1,0:T(8,128)S(1)}, u32[]{:S(2)}, u32[]{:S(2)}) collective-permute-start(f32[1,8,8,128]{3,2,1,0:T(8,128)S(1)} %get-tuple-element.13), channel_id=1, source_target_pairs={{0,8},{16,24},{8,0},{24,16},{1,9},{17,25},{9,1},{25,17},{2,10},{18... | collective-permute-start | bytes 98312 | tf_op jit(solution)/shard_map/ppermute | solution.py:259
  15.4 2.1 %collective-permute-start.4 = (f32[1,8,8,128]{3,2,1,0:T(8,128)S(1)}, f32[1,8,8,128]{3,2,1,0:T(8,128)S(1)}, u32[]{:S(2)}, u32[]{:S(2)}) collective-permute-start(f32[1,8,8,128]{3,2,1,0:T(8,128)S(1)} %get-tuple-element.14), channel_id=1, source_target_pairs={{8,16},{16,8},{9,17},{17,9},{10,18},{18,10},{11,19},{19,11},{12,20... | collective-permute-start | bytes 98312 | tf_op jit(solution)/shard_map/ppermute | solution.py:259
  17.5 0.0 collective-permute-done.3.refs_2_
  17.5 3.4 %collective-permute-done.4.refs_3_ = f32[1,8,8,128]{3,2,1,0:T(8,128)S(1)} collective-permute-done((f32[1,8,8,128]{3,2,1,0:T(8,128)S(1)}, f32[1,8,8,128]{3,2,1,0:T(8,128)S(1)}, u32[]{:S(2)}, u32[]{:S(2)}) %collective-permute-start.4) | collective-permute-done | bytes 32800 | tf_op jit(solution)/shard_map/ppermute | solution.py:259
  21.0 1.5 %collective-permute-start.5 = (f32[2,1,8,8,128]{4,3,2,1,0:T(8,128)S(1)}, f32[2,1,8,8,128]{4,3,2,1,0:T(8,128)S(1)}, u32[]{:S(2)}, u32[]{:S(2)}) collective-permute-start(f32[2,1,8,8,128]{4,3,2,1,0:T(8,128)S(1)} %pad_maximum_fusion), channel_id=1, source_target_pairs={{0,4},{4,0},{1,5},{5,1},{2,6},{6,2},{3,7},{7,3},{8,12},{12,8},{9,1... | collective-permute-start | bytes 196616 | tf_op jit(solution)/shard_map/ppermute | solution.py:259
  22.5 0.9 %collective-permute-done.5.refs_4_ = f32[2,1,8,8,128]{4,3,2,1,0:T(8,128)S(1)} collective-permute-done((f32[2,1,8,8,128]{4,3,2,1,0:T(8,128)S(1)}, f32[2,1,8,8,128]{4,3,2,1,0:T(8,128)S(1)}, u32[]{:S(2)}, u32[]{:S(2)}) %collective-permute-start.5) | collective-permute-done | bytes 65568 | tf_op jit(solution)/shard_map/ppermute | solution.py:259
  23.4 0.0 collective-permute-done.2.refs_1_
  23.4 9.6 %finish.1 = f32[8,16,256]{2,1,0:T(8,128)} custom-call(f32[3,8,32,256]{3,2,1,0:T(8,128)S(1)} %get-tuple-element.12.refs_0_, f32[3,8,32,256]{3,2,1,0:T(8,128)S(1)} %collective-permute-done.2.refs_1_, f32[1,8,8,128]{3,2,1,0:T(8,128)S(1)} %collective-permute-done.3.refs_2_, f32[1,8,8,128]{3,2,1,0:T(8,128)S(1)} %collective-permute-done.4.refs_3_, ...), custom_call_target="tpu_custom_call" | custom-call | tf_op jit(solution)/shard_map/finish/pallas_call | solution.py:282
  (2 shorter events, 0.0 us)
Async XLA Ops:
  0.0 0.9 %copy-start = (f32[8,16,256]{2,1,0:T(8,128)S(1)}, f32[8,16,256]{2,1,0:T(8,128)}, u32[]{:S(2)}) copy-start(f32[8,16,256]{2,1,0:T(8,128)} %s.3) | copy-start | bytes 393220
  0.9 0.9 %copy-start.1 = (f32[8,16,256]{2,1,0:T(8,128)S(1)}, f32[8,16,256]{2,1,0:T(8,128)}, u32[]{:S(2)}) copy-start(f32[8,16,256]{2,1,0:T(8,128)} %c.3) | copy-start | bytes 393220
  1.8 0.9 %copy-start.2 = (f32[8,16,256]{2,1,0:T(8,128)S(1)}, f32[8,16,256]{2,1,0:T(8,128)}, u32[]{:S(2)}) copy-start(f32[8,16,256]{2,1,0:T(8,128)} %f.3) | copy-start | bytes 393220
  2.7 5.8 %collective-permute-start = (f32[3,8,8,256]{3,2,1,0:T(8,128)S(1)}, f32[3,8,8,256]{3,2,1,0:T(8,128)S(1)}, u32[]{:S(2)}, u32[]{:S(2)}) collective-permute-start(f32[3,8,8,256]{3,2,1,0:T(8,128)S(1)} %get-tuple-element.10), channel_id=1, source_target_pairs={{0,1},{2,3},{1,0},{3,2},{4,5},{6,7},{5,4},{7,6},{8,9},{10,11},{9,8... | collective-permute-start | bytes 589832 | tf_op jit(solution)/shard_map/ppermute | solution.py:259
  4.1 7.3 %collective-permute-start.1 = (f32[3,8,8,256]{3,2,1,0:T(8,128)S(1)}, f32[3,8,8,256]{3,2,1,0:T(8,128)S(1)}, u32[]{:S(2)}, u32[]{:S(2)}) collective-permute-start(f32[3,8,8,256]{3,2,1,0:T(8,128)S(1)} %get-tuple-element.11), channel_id=1, source_target_pairs={{1,2},{2,1},{5,6},{6,5},{9,10},{10,9},{13,14},{14,13},{17,18},{18,... | collective-permute-start | bytes 589832 | tf_op jit(solution)/shard_map/ppermute | solution.py:259
  12.3 11.1 %collective-permute-start.2 = (f32[3,8,32,256]{3,2,1,0:T(8,128)S(1)}, f32[3,8,32,256]{3,2,1,0:T(8,128)S(1)}, u32[]{:S(2)}, u32[]{:S(2)}) collective-permute-start(f32[3,8,32,256]{3,2,1,0:T(8,128)S(1)} %get-tuple-element.12.refs_0_), channel_id=1, source_target_pairs={{0,4},{4,0},{1,5},{5,1},{2,6},{6,2},{3,7},{7,3},{8,12},{12,8},{9,1... | collective-permute-start | bytes 2359304 | tf_op jit(solution)/shard_map/ppermute | solution.py:259
  14.2 3.3 %collective-permute-start.3 = (f32[1,8,8,128]{3,2,1,0:T(8,128)S(1)}, f32[1,8,8,128]{3,2,1,0:T(8,128)S(1)}, u32[]{:S(2)}, u32[]{:S(2)}) collective-permute-start(f32[1,8,8,128]{3,2,1,0:T(8,128)S(1)} %get-tuple-element.13), channel_id=1, source_target_pairs={{0,8},{16,24},{8,0},{24,16},{1,9},{17,25},{9,1},{25,17},{2,10},{18... | collective-permute-start | bytes 98312 | tf_op jit(solution)/shard_map/ppermute | solution.py:259
  15.4 5.5 %collective-permute-start.4 = (f32[1,8,8,128]{3,2,1,0:T(8,128)S(1)}, f32[1,8,8,128]{3,2,1,0:T(8,128)S(1)}, u32[]{:S(2)}, u32[]{:S(2)}) collective-permute-start(f32[1,8,8,128]{3,2,1,0:T(8,128)S(1)} %get-tuple-element.14), channel_id=1, source_target_pairs={{8,16},{16,8},{9,17},{17,9},{10,18},{18,10},{11,19},{19,11},{12,20... | collective-permute-start | bytes 98312 | tf_op jit(solution)/shard_map/ppermute | solution.py:259
  21.0 2.4 %collective-permute-start.5 = (f32[2,1,8,8,128]{4,3,2,1,0:T(8,128)S(1)}, f32[2,1,8,8,128]{4,3,2,1,0:T(8,128)S(1)}, u32[]{:S(2)}, u32[]{:S(2)}) collective-permute-start(f32[2,1,8,8,128]{4,3,2,1,0:T(8,128)S(1)} %pad_maximum_fusion), channel_id=1, source_target_pairs={{0,4},{4,0},{1,5},{5,1},{2,6},{6,2},{3,7},{7,3},{8,12},{12,8},{9,1... | collective-permute-start | bytes 196616 | tf_op jit(solution)/shard_map/ppermute | solution.py:259

commit v2 on v1

--- a/solution.py
+++ b/solution.py
@@ -36,42 +36,41 @@
     return lax.rem(lax.axis_index(axis), 2)
 
 
-def pack_rows(s, c, f, first, second):
+def pack_rows(own, first, second):
     odd = is_odd("gy")
-    last = s.shape[1] - HALO
-    row_a = pl.multiple_of((1 - odd) * last, 8)
-    row_b = pl.multiple_of(odd * last, 8)
-    for a, ref in enumerate((s, c, f)):
-        first[a] = ref[:, pl.ds(row_a, HALO), :]
-        second[a] = ref[:, pl.ds(row_b, HALO), :]
+    last = own.shape[2] - HALO
+    first[...] = own[:, :, pl.ds(pl.multiple_of((1 - odd) * last, 8), HALO), :]
+    second[...] = own[:, :, pl.ds(pl.multiple_of(odd * last, 8), HALO), :]
 
 
 def slots(rows):
     return [(a, g, a * (rows // 8) + g) for a in range(3) for g in range(rows // 8)]
 
 
-def pack_columns(s, c, f, got_a, got_b, block, first, second):
+def pack_columns(own, got_a, got_b, rim, first, second):
     odd_y = is_odd("gy")
     odd_z = is_odd("grp")
-    depth, own, width = s.shape
-    rows = own + 2 * HALO
-    for a, ref in enumerate((s, c, f)):
-        block[a, :, HALO : HALO + own, :] = ref[...]
-        from_a, from_b = got_a[a], got_b[a]
-        block[a, :, 0:HALO, :] = jnp.where(odd_y == 1, from_a, from_b)
-        block[a, :, HALO + own : rows, :] = jnp.where(odd_y == 1, from_b, from_a)
+    _, depth, inner, width = own.shape
+    groups = inner // 8 + 2
     lane = lax.broadcasted_iota(jnp.int32, (8, LANES), 1)
 
     def plane(p, carry):
         heads = [jnp.zeros((8, LANES), jnp.float32) for _ in range(first.shape[0])]
         tails = list(heads)
-        for a, g, slot in slots(rows):
+        for a, g, slot in slots(8 * groups):
+            if g == 0 or g == groups - 1:
+                from_a, from_b = got_a[a, p], got_b[a, p]
+                above = odd_y == (1 if g == 0 else 0)
+                strip = jnp.where(above, from_a, from_b)
+                rim[0 if g == 0 else 1, a, p] = strip
+                head, tail = strip[:, 0:LANES], strip[:, width - LANES : width]
+            else:
+                head = own[a, p, 8 * g - 8 : 8 * g, 0:LANES]
+                tail = own[a, p, 8 * g - 8 : 8 * g, width - LANES : width]
             at = 8 * (slot % 16)
             mine = (lane >= at) & (lane < at + HALO)
-            head = pltpu.roll(block[a, p, 8 * g : 8 * g + 8, 0:LANES], at, 1)
-            tail = pltpu.roll(
-                block[a, p, 8 * g : 8 * g + 8, width - LANES : width], (at + HALO) % LANES, 1
-            )
+            head = pltpu.roll(head, at, 1)
+            tail = pltpu.roll(tail, (at + HALO) % LANES, 1)
             heads[slot // 16] = jnp.where(mine, head, heads[slot // 16])
             tails[slot // 16] = jnp.where(mine, tail, tails[slot // 16])
         for t, (head, tail) in enumerate(zip(heads, tails)):
@@ -178,114 +177,178 @@
         lax.fori_loop(*reach(halo), corrections, 0)
 
 
-def finish(reflect, n_x, *refs):
-    block = refs[0]
-    near = refs[1 : 1 + n_x]
-    got = refs[1 + n_x : 3 + n_x]
-    near_got = refs[3 + n_x : 3 + 2 * n_x]
-    result = refs[3 + 2 * n_x]
+def layout(reflect, depth):
+    return (1, depth + HALO + 2) if reflect else (1 + HALO, depth + 2 * HALO + 2)
+
+
+def each_plane(reflect, depth, place):
+    odd_x = is_odd("gx")
+    own_at, _ = layout(reflect, depth)
+
+    def own_plane(p, carry):
+        to = jnp.where(odd_x == 1, depth - 1 - p, p) if reflect else p
+        place(None, p, own_at + to)
+        return carry
+
+    lax.fori_loop(0, depth, own_plane, 0)
+
+    def near_plane(p, carry):
+        if reflect:
+            place(0, jnp.where(odd_x == 1, depth - 1 - p, p), own_at + depth + p)
+            return carry
+        for i in range(2):
+            above = odd_x == i
+            at = jnp.where(above, p, depth - HALO + p)
+            place(i, at, jnp.where(above, own_at + depth + p, 1 + p))
+        return carry
+
+    lax.fori_loop(0, HALO, near_plane, 0)
+
+
+def out_plane(reflect, depth, p):
+    own_at, _ = layout(reflect, depth)
+    at = p - own_at
+    return jnp.where(is_odd("gx") == 1, depth - 1 - at, at) if reflect else at
+
+
+def interior(reflect, n_x, *refs):
+    own, rim = refs[0], refs[1]
+    near, near_rim = refs[2 : 2 + n_x], refs[2 + n_x : 2 + 2 * n_x]
+    result, ends = refs[2 + 2 * n_x : 4 + 2 * n_x]
     cells = refs[4 + 2 * n_x :]
-    _, depth, rows, width = block.shape
-    odd_x = is_odd("gx")
+    _, depth, inner, width = own.shape
+    rows = inner + 2 * HALO
+    lane = lax.broadcasted_iota(jnp.int32, (rows, LANES), 1)
+
+    def place(i, p_from, p_to):
+        block, halo = (own, rim) if i is None else (near[i], near_rim[i])
+        for a in range(3):
+            tile = cells[a]
+            tile[p_to, 0:HALO, :] = halo[0, a, p_from]
+            tile[p_to, HALO : HALO + inner, :] = block[a, p_from]
+            tile[p_to, HALO + inner : rows, :] = halo[1, a, p_from]
+            head = pltpu.roll(tile[p_to, :, 0:LANES], LANES // 2, 1)
+            tail = tile[p_to, :, width - LANES : width]
+            end = jnp.where((lane >= LANES // 2) & (lane < LANES // 2 + 2 * HALO), head, 0.0)
+            ends[a, p_to] = jnp.where(lane >= LANES - 2 * HALO, tail, end)
+
+    own_at, total = layout(reflect, depth)
+    for a in range(3):
+        for p in (0, total - 1):
+            cells[a][p] = jnp.zeros((rows, width), jnp.float32)
+            ends[a, p] = jnp.zeros((rows, LANES), jnp.float32)
+    each_plane(reflect, depth, place)
+
+    def out(p, v):
+        result[out_plane(reflect, depth, p)] = v[HALO : rows - HALO, :]
+
+    solve(cells, own_at, depth, out)
+
+
+def edges(reflect, n_x, *refs):
+    ends, inside, got_a, got_b = refs[:4]
+    near_got = refs[4 : 4 + n_x]
+    result = refs[4 + n_x]
+    cells = refs[5 + n_x :]
+    depth, inner, width = inside.shape
+    rows = inner + 2 * HALO
     odd_z = is_odd("grp")
-    own_at = 1 if reflect else 1 + HALO
-    tiles = [cells[0], cells[1], cells[2]]
     lane = lax.broadcasted_iota(jnp.int32, (8, LANES), 1)
-
-    def place(src, src_a, src_b, p_from, p_to):
-        for a in range(3):
-            tiles[a][p_to, :, 0:width] = src[a, p_from]
-        for t in range(src_a.shape[0]):
-            va, vb = src_a[t, p_from], src_b[t, p_from]
+    in_right = lane < HALO
+    in_left = (lane >= LANES // 2 - HALO) & (lane < LANES // 2)
+
+    def place(i, p_from, p_to):
+        for t in range(got_a.shape[0]):
+            if i is None:
+                va, vb = got_a[t, p_from], got_b[t, p_from]
+            else:
+                va, vb = near_got[i][0, t, p_from], near_got[i][1, t, p_from]
             upper = jnp.where(odd_z == 1, vb, va)
             lower = jnp.where(odd_z == 1, va, vb)
             for a, g, slot in slots(rows):
                 if slot // 16 == t:
                     at = 8 * (slot % 16)
                     right = pltpu.roll(upper, (LANES - at) % LANES, 1)
-                    left = pltpu.roll(lower, (2 * LANES - HALO - at) % LANES, 1)
-                    tile = jnp.where(lane >= LANES - HALO, left, 0.0)
-                    tile = jnp.where(lane < HALO, right, tile)
-                    tiles[a][p_to, 8 * g : 8 * g + 8, width : width + LANES] = tile
-
-    zero = jnp.zeros(tiles[0].shape[1:], jnp.float32)
-    for tile in tiles:
-        tile[0] = zero
-
-    def own_plane(p, carry):
-        to = jnp.where(odd_x == 1, depth - 1 - p, p) if reflect else p
-        place(block, got[0], got[1], p, own_at + to)
-        return carry
-
-    lax.fori_loop(0, depth, own_plane, 0)
-
-    def near_plane(p, carry):
-        if reflect:
-            at = jnp.where(odd_x == 1, depth - 1 - p, p)
-            place(near[0], near_got[0].at[0], near_got[0].at[1], at, 1 + depth + p)
-        else:
-            for i in range(2):
-                above = odd_x == i
-                at = jnp.where(above, p, depth - HALO + p)
-                to = jnp.where(above, own_at + depth + p, 1 + p)
-                place(near[i], near_got[i].at[0], near_got[i].at[1], at, to)
-        return carry
-
-    lax.fori_loop(0, HALO, near_plane, 0)
+                    left = pltpu.roll(lower, (LANES + LANES // 2 - HALO - at) % LANES, 1)
+                    tile = ends[a, p_to, 8 * g : 8 * g + 8, :]
+                    tile = jnp.where(in_left, left, tile)
+                    cells[a][p_to, 8 * g : 8 * g + 8, :] = jnp.where(in_right, right, tile)
+
+    own_at, total = layout(reflect, depth)
+    for a in range(3):
+        for p in (0, total - 1):
+            cells[a][p] = ends[a, p]
+    each_plane(reflect, depth, place)
+    result[...] = inside[...]
+    wide = lax.broadcasted_iota(jnp.int32, (inner, LANES), 1)
 
     def out(p, v):
-        at = p - own_at
-        if reflect:
-            at = jnp.where(odd_x == 1, depth - 1 - at, at)
-        result[at] = v[HALO : rows - HALO, 0:width]
+        at = out_plane(reflect, depth, p)
+        v = v[HALO : rows - HALO, :]
+        head = pltpu.roll(v, LANES // 2, 1)
+        result[at, :, 0:LANES] = jnp.where(wide < HALO, head, result[at, :, 0:LANES])
+        tail = result[at, :, width - LANES : width]
+        result[at, :, width - LANES : width] = jnp.where(wide >= LANES - HALO, v, tail)
 
     solve(cells, own_at, depth, out)
 
 
 def shards(sizes, source_term, conductivity, initial_field):
-    depth, own, width = source_term.shape
-    rows = own + 2 * HALO
+    depth, inner, width = source_term.shape
+    rows = inner + 2 * HALO
     f32 = jnp.float32
     params = pltpu.CompilerParams(vmem_limit_bytes=48 * 1024 * 1024)
     args = (source_term, conductivity, initial_field)
 
-    face = jax.ShapeDtypeStruct((3, depth, HALO, width), f32)
-    msgs = pl.pallas_call(
-        pack_rows, out_shape=(face, face), in_specs=[VMEM] * 3, out_specs=(VMEM, VMEM),
-        compiler_params=params, name="pack_rows",
-    )(*args)
-
     def exchange(values, axis):
         found = [lax.ppermute(v, axis, pairs) for v, pairs in zip(values, swaps(axis, sizes[axis]))]
         return found + [jnp.zeros_like(v) for v in values[len(found) :]]
 
+    def work(lanes):
+        total = layout(reflect, depth)[1]
+        fine = pltpu.VMEM((total, rows, lanes), f32)
+        coarse = pltpu.VMEM((total // 2 + 1, rows, lanes), f32)
+        return [fine] * 7 + [coarse] * 5 + [fine] * 2 + [coarse] + [fine]
+
+    reflect = sizes["gx"] == 2
+    n_x = 1 if reflect else 2
+    face = jax.ShapeDtypeStruct((3, depth, HALO, width), f32)
+    own = jnp.stack(args)
+    msgs = pl.pallas_call(
+        pack_rows, out_shape=(face, face), in_specs=[VMEM], out_specs=(VMEM, VMEM),
+        compiler_params=params, name="pack_rows",
+    )(own)
     got = exchange(msgs, "gy")
+    near = exchange([own] * n_x, "gx")
+
     n_tiles = -(-3 * (rows // 8) // 16)
     strip = jax.ShapeDtypeStruct((n_tiles, depth, 8, LANES), f32)
-    block, *cols = pl.pallas_call(
+    rim, *cols = pl.pallas_call(
         pack_columns,
-        out_shape=(jax.ShapeDtypeStruct((3, depth, rows, width), f32), strip, strip),
-        in_specs=[VMEM] * 5, out_specs=(VMEM,) * 3,
+        out_shape=(jax.ShapeDtypeStruct((2, 3, depth, HALO, width), f32), strip, strip),
+        in_specs=[VMEM] * 3, out_specs=(VMEM,) * 3,
         compiler_params=params, name="pack_columns",
-    )(*args, *got)
-
-    reflect = sizes["gx"] == 2
-    n_x = 1 if reflect else 2
+    )(own, *got)
     got = exchange(cols, "grp")
-    near = exchange([block] * n_x, "gx")
+    near_rim = exchange([rim] * n_x, "gx")
+
+    block = jax.ShapeDtypeStruct(source_term.shape, f32)
+    total = layout(reflect, depth)[1]
+    inside, ends = pl.pallas_call(
+        functools.partial(interior, reflect, n_x),
+        out_shape=(block, jax.ShapeDtypeStruct((3, total, rows, LANES), f32)),
+        in_specs=[VMEM] * (2 + 2 * n_x), out_specs=(VMEM, VMEM), scratch_shapes=work(width),
+        compiler_params=params, name="interior",
+        cost_estimate=pl.CostEstimate(flops=20_000_000, bytes_accessed=20_000_000, transcendentals=0),
+    )(own, rim, *near, *near_rim)
+    inside, ends, got = lax.optimization_barrier((inside, ends, got))
     near_got = exchange([jnp.stack(got)] * n_x, "gx")
-
-    total = 1 + depth + HALO * n_x + 1
-    lanes = width + LANES
-    fine = pltpu.VMEM((total, rows, lanes), f32)
-    coarse = pltpu.VMEM((total // 2 + 1, rows, lanes), f32)
     return pl.pallas_call(
-        functools.partial(finish, reflect, n_x),
-        out_shape=jax.ShapeDtypeStruct(source_term.shape, f32),
-        in_specs=[VMEM] * (3 + 2 * n_x), out_specs=VMEM,
-        scratch_shapes=[fine] * 7 + [coarse] * 5 + [fine] * 2 + [coarse] + [fine],
-        compiler_params=params, name="finish",
-    )(block, *near, *got, *near_got)
+        functools.partial(edges, reflect, n_x),
+        out_shape=block,
+        in_specs=[VMEM] * (4 + n_x), out_specs=VMEM, scratch_shapes=work(LANES),
+        compiler_params=params, name="edges",
+    )(ends, inside, *got, *near_got)
 
 
 def solution(mesh):

time: 33.1 us -> 35.2 us (1.063)
  the two profiles are of different devices: /device:TPU:21 before, /device:TPU:18 now
where the time goes in v2:
time: 35.2 us; the launch traced here: 34.7 us
  Pallas kernels  17.3 us (49%)
  starting transfers between devices  8.71 us (25%)
  waiting for transfers between devices  7.5 us (21%)
  other arithmetic  1.06 us (3%)
    ppermute x7, starting transfers between devices, exchange(): lax.ppermute(v, axis, pairs)  8.71 us
    pallas_call x1, Pallas kernels, shards(): pl.pallas_call(functools.partial(edges, reflect, n_x), out_shape=block, i...  8.44 us
    pallas_call x1, Pallas kernels, shards(): pl.pallas_call(functools.partial(interior, reflect, n_x), out_shape=(bloc...  8.1 us
    ppermute x7, waiting for transfers between devices, exchange(): lax.ppermute(v, axis, pairs)  7.5 us
    another operation x1, other arithmetic, shards(): own = jnp.stack(args)  1.06 us
    pallas_call x1, Pallas kernels, shards(): pl.pallas_call(pack_columns, out_shape=(jax.ShapeDtypeStruct((2, 3, depth...  0.77 us
  transfers between devices with their start and end apart: 7, of which 3 were waited for; matrix products, arithmetic and copies ran while one was open for 0% of the time, Pallas kernels for 26%

profile of v2, /device:TPU:18, one launch (start us, length us, event | category | flops | bytes accessed | tf_op | source)
XLA Modules:
  0.0 34.7 jit_solution(8141907782852554678)
XLA Ops:
  0.0 1.1 %pad_maximum_fusion.own.refs_0_ = f32[3,8,16,256]{3,2,1,0:T(8,128)S(1)} fusion(f32[1,8,16,256]{3,2,1,0:T(8,128)} %bitcast.7, f32[1,8,16,256]{3,2,1,0:T(8,128)} %bitcast.8, f32[1,8,16,256]{3,2,1,0:T(8,128)} %bitcast.9), kind=kLoop, calls=%fused_computation | loop fusion | flops 196608 | bytes 786432 | tf_op jit(solution)/shard_map/stack | solution.py:316
  1.1 1.6 %collective-permute-start = (f32[3,8,8,256]{3,2,1,0:T(8,128)S(1)}, f32[3,8,8,256]{3,2,1,0:T(8,128)S(1)}, u32[]{:S(2)}, u32[]{:S(2)}) collective-permute-start(f32[3,8,8,256]{3,2,1,0:T(8,128)S(1)} %get-tuple-element.16), channel_id=1, source_target_pairs={{0,1},{2,3},{1,0},{3,2},{4,5},{6,7},{5,4},{7,6},{8,9},{10,11},{9,8... | collective-permute-start | bytes 589832 | tf_op jit(solution)/shard_map/ppermute | solution.py:304
  2.7 1.9 %collective-permute-start.1 = (f32[3,8,8,256]{3,2,1,0:T(8,128)S(1)}, f32[3,8,8,256]{3,2,1,0:T(8,128)S(1)}, u32[]{:S(2)}, u32[]{:S(2)}) collective-permute-start(f32[3,8,8,256]{3,2,1,0:T(8,128)S(1)} %get-tuple-element.17), channel_id=1, source_target_pairs={{1,2},{2,1},{5,6},{6,5},{9,10},{10,9},{13,14},{14,13},{17,18},{18,... | collective-permute-start | bytes 589832 | tf_op jit(solution)/shard_map/ppermute | solution.py:304
  4.7 0.1 collective-permute-start.2
  4.7 3.1 %collective-permute-done.got_a = f32[3,8,8,256]{3,2,1,0:T(8,128)S(1)} collective-permute-done((f32[3,8,8,256]{3,2,1,0:T(8,128)S(1)}, f32[3,8,8,256]{3,2,1,0:T(8,128)S(1)}, u32[]{:S(2)}, u32[]{:S(2)}) %collective-permute-start) | collective-permute-done | bytes 196640 | tf_op jit(solution)/shard_map/ppermute | solution.py:304
  7.8 3.2 %collective-permute-done.1.got_b = f32[3,8,8,256]{3,2,1,0:T(8,128)S(1)} collective-permute-done((f32[3,8,8,256]{3,2,1,0:T(8,128)S(1)}, f32[3,8,8,256]{3,2,1,0:T(8,128)S(1)}, u32[]{:S(2)}, u32[]{:S(2)}) %collective-permute-start.1) | collective-permute-done | bytes 196640 | tf_op jit(solution)/shard_map/ppermute | solution.py:304
  11.0 0.8 %pack_columns.1 = (f32[2,3,8,8,256]{4,3,2,1,0:T(8,128)S(1)}, f32[1,8,8,128]{3,2,1,0:T(8,128)S(1)}, f32[1,8,8,128]{3,2,1,0:T(8,128)S(1)}) custom-call(f32[3,8,16,256]{3,2,1,0:T(8,128)S(1)} %pad_maximum_fusion.own.refs_0_, f32[3,8,8,256]{3,2,1,0:T(8,128)S(1)} %collective-permute-done.got_a, f32[3,8,8,256]{3,2,1,0:T(8,128)S(1)} %collective-permute-done.1.got_b), custom_call_target="tpu_custom_call" | custom-call | tf_op jit(solution)/shard_map/pack_columns/pallas_call | solution.py:326
  11.8 0.1 collective-permute-start.3
  11.8 0.6 %collective-permute-start.4 = (f32[1,8,8,128]{3,2,1,0:T(8,128)S(1)}, f32[1,8,8,128]{3,2,1,0:T(8,128)S(1)}, u32[]{:S(2)}, u32[]{:S(2)}) collective-permute-start(f32[1,8,8,128]{3,2,1,0:T(8,128)S(1)} %get-tuple-element.21), channel_id=1, source_target_pairs={{0,8},{16,24},{8,0},{24,16},{1,9},{17,25},{9,1},{25,17},{2,10},{18... | collective-permute-start | bytes 98312 | tf_op jit(solution)/shard_map/ppermute | solution.py:304
  12.4 4.3 %collective-permute-start.5 = (f32[1,8,8,128]{3,2,1,0:T(8,128)S(1)}, f32[1,8,8,128]{3,2,1,0:T(8,128)S(1)}, u32[]{:S(2)}, u32[]{:S(2)}) collective-permute-start(f32[1,8,8,128]{3,2,1,0:T(8,128)S(1)} %get-tuple-element.22), channel_id=1, source_target_pairs={{8,16},{16,8},{9,17},{17,9},{10,18},{18,10},{11,19},{19,11},{12,20... | collective-permute-start | bytes 98312 | tf_op jit(solution)/shard_map/ppermute | solution.py:304
  16.8 0.0 collective-permute-done.2.refs_2_
  16.8 0.0 collective-permute-done.3.refs_3_
  16.8 8.1 %interior.1 = (f32[8,16,256]{2,1,0:T(8,128)S(1)}, f32[3,18,32,128]{3,2,1,0:T(8,128)S(1)}) custom-call(f32[3,8,16,256]{3,2,1,0:T(8,128)S(1)} %pad_maximum_fusion.own.refs_0_, f32[2,3,8,8,256]{4,3,2,1,0:T(8,128)S(1)} %get-tuple-element.18.refs_1_, f32[3,8,16,256]{3,2,1,0:T(8,128)S(1)} %collective-permute-done.2.refs_2_, ...), custom_call_target="tpu_custom_call" | custom-call | flops 20000000 | bytes 20000000 | tf_op jit(solution)/shard_map/interior/pallas_call | solution.py:337
  24.9 0.0 collective-permute-done.4.refs_2_
  24.9 0.0 collective-permute-done.5.refs_3_
  25.0 0.1 collective-permute-start.6
  25.0 1.2 %collective-permute-done.6.refs_4_ = f32[2,1,8,8,128]{4,3,2,1,0:T(8,128)S(1)} collective-permute-done((f32[2,1,8,8,128]{4,3,2,1,0:T(8,128)S(1)}, f32[2,1,8,8,128]{4,3,2,1,0:T(8,128)S(1)}, u32[]{:S(2)}, u32[]{:S(2)}) %collective-permute-start.6) | collective-permute-done | bytes 65568 | tf_op jit(solution)/shard_map/ppermute | solution.py:304
  26.3 8.4 %edges.1 = f32[8,16,256]{2,1,0:T(8,128)} custom-call(f32[3,18,32,128]{3,2,1,0:T(8,128)S(1)} %get-tuple-element.23.refs_0_, f32[8,16,256]{2,1,0:T(8,128)S(1)} %get-tuple-element.24.refs_1_, f32[1,8,8,128]{3,2,1,0:T(8,128)S(1)} %collective-permute-done.4.refs_2_, f32[1,8,8,128]{3,2,1,0:T(8,128)S(1)} %collective-permute-done.5.refs_3_, ...), custom_call_target="tpu_custom_call" | custom-call | tf_op jit(solution)/shard_map/edges/pallas_call | solution.py:346
  (2 shorter events, 0.0 us)
Async XLA Ops:
  1.1 6.7 %collective-permute-start = (f32[3,8,8,256]{3,2,1,0:T(8,128)S(1)}, f32[3,8,8,256]{3,2,1,0:T(8,128)S(1)}, u32[]{:S(2)}, u32[]{:S(2)}) collective-permute-start(f32[3,8,8,256]{3,2,1,0:T(8,128)S(1)} %get-tuple-element.16), channel_id=1, source_target_pairs={{0,1},{2,3},{1,0},{3,2},{4,5},{6,7},{5,4},{7,6},{8,9},{10,11},{9,8... | collective-permute-start | bytes 589832 | tf_op jit(solution)/shard_map/ppermute | solution.py:304
  2.7 8.2 %collective-permute-start.1 = (f32[3,8,8,256]{3,2,1,0:T(8,128)S(1)}, f32[3,8,8,256]{3,2,1,0:T(8,128)S(1)}, u32[]{:S(2)}, u32[]{:S(2)}) collective-permute-start(f32[3,8,8,256]{3,2,1,0:T(8,128)S(1)} %get-tuple-element.17), channel_id=1, source_target_pairs={{1,2},{2,1},{5,6},{6,5},{9,10},{10,9},{13,14},{14,13},{17,18},{18,... | collective-permute-start | bytes 589832 | tf_op jit(solution)/shard_map/ppermute | solution.py:304
  4.7 12.1 %collective-permute-start.2 = (f32[3,8,16,256]{3,2,1,0:T(8,128)S(1)}, f32[3,8,16,256]{3,2,1,0:T(8,128)S(1)}, u32[]{:S(2)}, u32[]{:S(2)}) collective-permute-start(f32[3,8,16,256]{3,2,1,0:T(8,128)S(1)} %pad_maximum_fusion.own.refs_0_), channel_id=1, source_target_pairs={{0,4},{4,0},{1,5},{5,1},{2,6},{6,2},{3,7},{7,3},{8,12},{12,8},{9,1... | collective-permute-start | bytes 1179656 | tf_op jit(solution)/shard_map/ppermute | solution.py:304
  11.8 5.0 %collective-permute-start.3 = (f32[2,3,8,8,256]{4,3,2,1,0:T(8,128)S(1)}, f32[2,3,8,8,256]{4,3,2,1,0:T(8,128)S(1)}, u32[]{:S(2)}, u32[]{:S(2)}) collective-permute-start(f32[2,3,8,8,256]{4,3,2,1,0:T(8,128)S(1)} %get-tuple-element.18.refs_1_), channel_id=1, source_target_pairs={{0,4},{4,0},{1,5},{5,1},{2,6},{6,2},{3,7},{7,3},{8,12},{12,8},{9,1... | collective-permute-start | bytes 1179656 | tf_op jit(solution)/shard_map/ppermute | solution.py:304
  11.8 13.1 %collective-permute-start.4 = (f32[1,8,8,128]{3,2,1,0:T(8,128)S(1)}, f32[1,8,8,128]{3,2,1,0:T(8,128)S(1)}, u32[]{:S(2)}, u32[]{:S(2)}) collective-permute-start(f32[1,8,8,128]{3,2,1,0:T(8,128)S(1)} %get-tuple-element.21), channel_id=1, source_target_pairs={{0,8},{16,24},{8,0},{24,16},{1,9},{17,25},{9,1},{25,17},{2,10},{18... | collective-permute-start | bytes 98312 | tf_op jit(solution)/shard_map/ppermute | solution.py:304
  12.4 12.5 %collective-permute-start.5 = (f32[1,8,8,128]{3,2,1,0:T(8,128)S(1)}, f32[1,8,8,128]{3,2,1,0:T(8,128)S(1)}, u32[]{:S(2)}, u32[]{:S(2)}) collective-permute-start(f32[1,8,8,128]{3,2,1,0:T(8,128)S(1)} %get-tuple-element.22), channel_id=1, source_target_pairs={{8,16},{16,8},{9,17},{17,9},{10,18},{18,10},{11,19},{19,11},{12,20... | collective-permute-start | bytes 98312 | tf_op jit(solution)/shard_map/ppermute | solution.py:304
  25.0 1.3 %collective-permute-start.6 = (f32[2,1,8,8,128]{4,3,2,1,0:T(8,128)S(1)}, f32[2,1,8,8,128]{4,3,2,1,0:T(8,128)S(1)}, u32[]{:S(2)}, u32[]{:S(2)}) collective-permute-start(f32[2,1,8,8,128]{4,3,2,1,0:T(8,128)S(1)} %pad_maximum_fusion.1), channel_id=1, source_target_pairs={{0,4},{4,0},{1,5},{5,1},{2,6},{6,2},{3,7},{7,3},{8,12},{12,8},{9,1... | collective-permute-start | bytes 196616 | tf_op jit(solution)/shard_map/ppermute | solution.py:304

commit v3 on v2

--- a/solution.py
+++ b/solution.py
@@ -101,7 +101,7 @@
         sum8[k] = t + ahead(t, 1)
         return carry
 
-    lax.fori_loop(*reach(HALO), gather8, 0)
+    lax.fori_loop(*reach(HALO), gather8, 0, unroll=True)
 
     def weights(c, below, above, step):
         x = c + above
@@ -119,7 +119,7 @@
     low, high = reach(HALO - 2)
     wx[2 * low - 2] = cond[2 * low - 2] + cond[2 * low - 1]
     cwx[low - 1] = sum8[low - 1] + sum8[low]
-    lax.fori_loop(low, high, setup, 0)
+    lax.fori_loop(low, high, setup, 0, unroll=True)
 
     row = lax.broadcasted_iota(jnp.int32, (rows, lanes), 0)
     lane = lax.broadcasted_iota(jnp.int32, (rows, lanes), 1)
@@ -160,7 +160,7 @@
             cq[k] = (4.0 * both) * cinv[k]
             return carry
 
-        lax.fori_loop(*reach(halo + 2), residuals, 0)
+        lax.fori_loop(*reach(halo + 2), residuals, 0, unroll=True)
 
         def corrections(k, carry, it=it):
             coarse = smooth(cq, k, cwx, cwy, cwz, cinv, 2)
@@ -174,7 +174,7 @@
                     out(p, field[p] + (err[p] + e if it else e))
             return carry
 
-        lax.fori_loop(*reach(halo), corrections, 0)
+        lax.fori_loop(*reach(halo), corrections, 0, unroll=True)
 
 
 def layout(reflect, depth):
@@ -190,7 +190,7 @@
         place(None, p, own_at + to)
         return carry
 
-    lax.fori_loop(0, depth, own_plane, 0)
+    lax.fori_loop(0, depth, own_plane, 0, unroll=True)
 
     def near_plane(p, carry):
         if reflect:
@@ -202,7 +202,7 @@
             place(i, at, jnp.where(above, own_at + depth + p, 1 + p))
         return carry
 
-    lax.fori_loop(0, HALO, near_plane, 0)
+    lax.fori_loop(0, HALO, near_plane, 0, unroll=True)
 
 
 def out_plane(reflect, depth, p):

time: 35.2 us -> 29.6 us (0.84)
  Pallas kernels: 17.3 us -> 11.7 us
    pallas_call x1, Pallas kernels: 8.44 us -> 4.92 us  [shards(): pl.pallas_call(functools.partial(edges, reflect, n_x), out_shape=block, i...]
    pallas_call x1, Pallas kernels: 8.1 us -> 5.99 us  [shards(): pl.pallas_call(functools.partial(interior, reflect, n_x), out_shape=(bloc...]
  transfers between devices with their start and end apart: 7 -> 7, of which waited for: 3 -> 3; matrix products, arithmetic and copies ran while one was open for 0% -> 0% of each run, Pallas kernels for 26% -> 23%
where the time goes in v3:
time: 29.6 us; the launch traced here: 29.1 us
  Pallas kernels  11.7 us (40%)
  starting transfers between devices  8.71 us (29%)
  waiting for transfers between devices  7.5 us (25%)
  other arithmetic  1.06 us (4%)
    ppermute x7, starting transfers between devices, exchange(): lax.ppermute(v, axis, pairs)  8.71 us
    ppermute x7, waiting for transfers between devices, exchange(): lax.ppermute(v, axis, pairs)  7.5 us
    pallas_call x1, Pallas kernels, shards(): pl.pallas_call(functools.partial(interior, reflect, n_x), out_shape=(bloc...  5.99 us
    pallas_call x1, Pallas kernels, shards(): pl.pallas_call(functools.partial(edges, reflect, n_x), out_shape=block, i...  4.92 us
    another operation x1, other arithmetic, shards(): own = jnp.stack(args)  1.06 us
    pallas_call x1, Pallas kernels, shards(): pl.pallas_call(pack_columns, out_shape=(jax.ShapeDtypeStruct((2, 3, depth...  0.77 us
  transfers between devices with their start and end apart: 7, of which 3 were waited for; matrix products, arithmetic and copies ran while one was open for 0% of the time, Pallas kernels for 23%

profile of v3, /device:TPU:18, one launch (start us, length us, event | category | flops | bytes accessed | tf_op | source)
XLA Modules:
  0.0 29.1 jit_solution(15376155392823066904)
XLA Ops:
  0.0 1.1 %pad_maximum_fusion.own.refs_0_ = f32[3,8,16,256]{3,2,1,0:T(8,128)S(1)} fusion(f32[1,8,16,256]{3,2,1,0:T(8,128)} %bitcast.7, f32[1,8,16,256]{3,2,1,0:T(8,128)} %bitcast.8, f32[1,8,16,256]{3,2,1,0:T(8,128)} %bitcast.9), kind=kLoop, calls=%fused_computation | loop fusion | flops 196608 | bytes 786432 | tf_op jit(solution)/shard_map/stack | solution.py:316
  1.1 1.6 %collective-permute-start = (f32[3,8,8,256]{3,2,1,0:T(8,128)S(1)}, f32[3,8,8,256]{3,2,1,0:T(8,128)S(1)}, u32[]{:S(2)}, u32[]{:S(2)}) collective-permute-start(f32[3,8,8,256]{3,2,1,0:T(8,128)S(1)} %get-tuple-element.16), channel_id=1, source_target_pairs={{0,1},{2,3},{1,0},{3,2},{4,5},{6,7},{5,4},{7,6},{8,9},{10,11},{9,8... | collective-permute-start | bytes 589832 | tf_op jit(solution)/shard_map/ppermute | solution.py:304
  2.7 1.9 %collective-permute-start.1 = (f32[3,8,8,256]{3,2,1,0:T(8,128)S(1)}, f32[3,8,8,256]{3,2,1,0:T(8,128)S(1)}, u32[]{:S(2)}, u32[]{:S(2)}) collective-permute-start(f32[3,8,8,256]{3,2,1,0:T(8,128)S(1)} %get-tuple-element.17), channel_id=1, source_target_pairs={{1,2},{2,1},{5,6},{6,5},{9,10},{10,9},{13,14},{14,13},{17,18},{18,... | collective-permute-start | bytes 589832 | tf_op jit(solution)/shard_map/ppermute | solution.py:304
  4.7 0.1 collective-permute-start.2
  4.7 3.1 %collective-permute-done.got_a = f32[3,8,8,256]{3,2,1,0:T(8,128)S(1)} collective-permute-done((f32[3,8,8,256]{3,2,1,0:T(8,128)S(1)}, f32[3,8,8,256]{3,2,1,0:T(8,128)S(1)}, u32[]{:S(2)}, u32[]{:S(2)}) %collective-permute-start) | collective-permute-done | bytes 196640 | tf_op jit(solution)/shard_map/ppermute | solution.py:304
  7.8 3.2 %collective-permute-done.1.got_b = f32[3,8,8,256]{3,2,1,0:T(8,128)S(1)} collective-permute-done((f32[3,8,8,256]{3,2,1,0:T(8,128)S(1)}, f32[3,8,8,256]{3,2,1,0:T(8,128)S(1)}, u32[]{:S(2)}, u32[]{:S(2)}) %collective-permute-start.1) | collective-permute-done | bytes 196640 | tf_op jit(solution)/shard_map/ppermute | solution.py:304
  11.0 0.8 %pack_columns.1 = (f32[2,3,8,8,256]{4,3,2,1,0:T(8,128)S(1)}, f32[1,8,8,128]{3,2,1,0:T(8,128)S(1)}, f32[1,8,8,128]{3,2,1,0:T(8,128)S(1)}) custom-call(f32[3,8,16,256]{3,2,1,0:T(8,128)S(1)} %pad_maximum_fusion.own.refs_0_, f32[3,8,8,256]{3,2,1,0:T(8,128)S(1)} %collective-permute-done.got_a, f32[3,8,8,256]{3,2,1,0:T(8,128)S(1)} %collective-permute-done.1.got_b), custom_call_target="tpu_custom_call" | custom-call | tf_op jit(solution)/shard_map/pack_columns/pallas_call | solution.py:326
  11.8 0.1 collective-permute-start.3
  11.8 0.6 %collective-permute-start.4 = (f32[1,8,8,128]{3,2,1,0:T(8,128)S(1)}, f32[1,8,8,128]{3,2,1,0:T(8,128)S(1)}, u32[]{:S(2)}, u32[]{:S(2)}) collective-permute-start(f32[1,8,8,128]{3,2,1,0:T(8,128)S(1)} %get-tuple-element.21), channel_id=1, source_target_pairs={{0,8},{16,24},{8,0},{24,16},{1,9},{17,25},{9,1},{25,17},{2,10},{18... | collective-permute-start | bytes 98312 | tf_op jit(solution)/shard_map/ppermute | solution.py:304
  12.4 4.3 %collective-permute-start.5 = (f32[1,8,8,128]{3,2,1,0:T(8,128)S(1)}, f32[1,8,8,128]{3,2,1,0:T(8,128)S(1)}, u32[]{:S(2)}, u32[]{:S(2)}) collective-permute-start(f32[1,8,8,128]{3,2,1,0:T(8,128)S(1)} %get-tuple-element.22), channel_id=1, source_target_pairs={{8,16},{16,8},{9,17},{17,9},{10,18},{18,10},{11,19},{19,11},{12,20... | collective-permute-start | bytes 98312 | tf_op jit(solution)/shard_map/ppermute | solution.py:304
  16.8 0.0 collective-permute-done.2.refs_2_
  16.8 0.0 collective-permute-done.3.refs_3_
  16.8 6.0 %interior.1 = (f32[8,16,256]{2,1,0:T(8,128)S(1)}, f32[3,18,32,128]{3,2,1,0:T(8,128)S(1)}) custom-call(f32[3,8,16,256]{3,2,1,0:T(8,128)S(1)} %pad_maximum_fusion.own.refs_0_, f32[2,3,8,8,256]{4,3,2,1,0:T(8,128)S(1)} %get-tuple-element.18.refs_1_, f32[3,8,16,256]{3,2,1,0:T(8,128)S(1)} %collective-permute-done.2.refs_2_, ...), custom_call_target="tpu_custom_call" | custom-call | flops 20000000 | bytes 20000000 | tf_op jit(solution)/shard_map/interior/pallas_call | solution.py:337
  22.8 0.0 collective-permute-done.4.refs_2_
  22.8 0.0 collective-permute-done.5.refs_3_
  22.9 0.1 collective-permute-start.6
  22.9 1.2 %collective-permute-done.6.refs_4_ = f32[2,1,8,8,128]{4,3,2,1,0:T(8,128)S(1)} collective-permute-done((f32[2,1,8,8,128]{4,3,2,1,0:T(8,128)S(1)}, f32[2,1,8,8,128]{4,3,2,1,0:T(8,128)S(1)}, u32[]{:S(2)}, u32[]{:S(2)}) %collective-permute-start.6) | collective-permute-done | bytes 65568 | tf_op jit(solution)/shard_map/ppermute | solution.py:304
  24.2 4.9 %edges.1 = f32[8,16,256]{2,1,0:T(8,128)} custom-call(f32[3,18,32,128]{3,2,1,0:T(8,128)S(1)} %get-tuple-element.23.refs_0_, f32[8,16,256]{2,1,0:T(8,128)S(1)} %get-tuple-element.24.refs_1_, f32[1,8,8,128]{3,2,1,0:T(8,128)S(1)} %collective-permute-done.4.refs_2_, f32[1,8,8,128]{3,2,1,0:T(8,128)S(1)} %collective-permute-done.5.refs_3_, ...), custom_call_target="tpu_custom_call" | custom-call | tf_op jit(solution)/shard_map/edges/pallas_call | solution.py:346
  (2 shorter events, 0.0 us)
Async XLA Ops:
  1.1 6.7 %collective-permute-start = (f32[3,8,8,256]{3,2,1,0:T(8,128)S(1)}, f32[3,8,8,256]{3,2,1,0:T(8,128)S(1)}, u32[]{:S(2)}, u32[]{:S(2)}) collective-permute-start(f32[3,8,8,256]{3,2,1,0:T(8,128)S(1)} %get-tuple-element.16), channel_id=1, source_target_pairs={{0,1},{2,3},{1,0},{3,2},{4,5},{6,7},{5,4},{7,6},{8,9},{10,11},{9,8... | collective-permute-start | bytes 589832 | tf_op jit(solution)/shard_map/ppermute | solution.py:304
  2.7 8.2 %collective-permute-start.1 = (f32[3,8,8,256]{3,2,1,0:T(8,128)S(1)}, f32[3,8,8,256]{3,2,1,0:T(8,128)S(1)}, u32[]{:S(2)}, u32[]{:S(2)}) collective-permute-start(f32[3,8,8,256]{3,2,1,0:T(8,128)S(1)} %get-tuple-element.17), channel_id=1, source_target_pairs={{1,2},{2,1},{5,6},{6,5},{9,10},{10,9},{13,14},{14,13},{17,18},{18,... | collective-permute-start | bytes 589832 | tf_op jit(solution)/shard_map/ppermute | solution.py:304
  4.7 12.1 %collective-permute-start.2 = (f32[3,8,16,256]{3,2,1,0:T(8,128)S(1)}, f32[3,8,16,256]{3,2,1,0:T(8,128)S(1)}, u32[]{:S(2)}, u32[]{:S(2)}) collective-permute-start(f32[3,8,16,256]{3,2,1,0:T(8,128)S(1)} %pad_maximum_fusion.own.refs_0_), channel_id=1, source_target_pairs={{0,4},{4,0},{1,5},{5,1},{2,6},{6,2},{3,7},{7,3},{8,12},{12,8},{9,1... | collective-permute-start | bytes 1179656 | tf_op jit(solution)/shard_map/ppermute | solution.py:304
  11.8 5.0 %collective-permute-start.3 = (f32[2,3,8,8,256]{4,3,2,1,0:T(8,128)S(1)}, f32[2,3,8,8,256]{4,3,2,1,0:T(8,128)S(1)}, u32[]{:S(2)}, u32[]{:S(2)}) collective-permute-start(f32[2,3,8,8,256]{4,3,2,1,0:T(8,128)S(1)} %get-tuple-element.18.refs_1_), channel_id=1, source_target_pairs={{0,4},{4,0},{1,5},{5,1},{2,6},{6,2},{3,7},{7,3},{8,12},{12,8},{9,1... | collective-permute-start | bytes 1179656 | tf_op jit(solution)/shard_map/ppermute | solution.py:304
  11.8 11.0 %collective-permute-start.4 = (f32[1,8,8,128]{3,2,1,0:T(8,128)S(1)}, f32[1,8,8,128]{3,2,1,0:T(8,128)S(1)}, u32[]{:S(2)}, u32[]{:S(2)}) collective-permute-start(f32[1,8,8,128]{3,2,1,0:T(8,128)S(1)} %get-tuple-element.21), channel_id=1, source_target_pairs={{0,8},{16,24},{8,0},{24,16},{1,9},{17,25},{9,1},{25,17},{2,10},{18... | collective-permute-start | bytes 98312 | tf_op jit(solution)/shard_map/ppermute | solution.py:304
  12.4 10.4 %collective-permute-start.5 = (f32[1,8,8,128]{3,2,1,0:T(8,128)S(1)}, f32[1,8,8,128]{3,2,1,0:T(8,128)S(1)}, u32[]{:S(2)}, u32[]{:S(2)}) collective-permute-start(f32[1,8,8,128]{3,2,1,0:T(8,128)S(1)} %get-tuple-element.22), channel_id=1, source_target_pairs={{8,16},{16,8},{9,17},{17,9},{10,18},{18,10},{11,19},{19,11},{12,20... | collective-permute-start | bytes 98312 | tf_op jit(solution)/shard_map/ppermute | solution.py:304
  22.9 1.3 %collective-permute-start.6 = (f32[2,1,8,8,128]{4,3,2,1,0:T(8,128)S(1)}, f32[2,1,8,8,128]{4,3,2,1,0:T(8,128)S(1)}, u32[]{:S(2)}, u32[]{:S(2)}) collective-permute-start(f32[2,1,8,8,128]{4,3,2,1,0:T(8,128)S(1)} %pad_maximum_fusion.1), channel_id=1, source_target_pairs={{0,4},{4,0},{1,5},{5,1},{2,6},{6,2},{3,7},{7,3},{8,12},{12,8},{9,1... | collective-permute-start | bytes 196616 | tf_op jit(solution)/shard_map/ppermute | solution.py:304

commit v4 on v3

--- a/solution.py
+++ b/solution.py
@@ -23,13 +23,34 @@
     return pltpu.roll(v, n, axis)
 
 
-def swaps(axis, count):
+def swaps(axis, sizes):
+    count, fill = sizes[axis], sizes["gx"]
+    over = [name for name in sizes if name in (axis, "gx")]
+    filled = axis != "gx" and fill % 2 == 0
+
+    def at(i, k):
+        return i * fill + k if over[0] == axis else k * count + i
+
     rounds = []
     for start in (0, 1):
         pairs = [(i, i + 1) for i in range(start, count - 1, 2)]
-        if pairs:
-            rounds.append(pairs + [(j, i) for i, j in pairs])
-    return rounds
+        left = set(range(count)) - {i for pair in pairs for i in pair}
+        if not pairs:
+            continue
+        if filled:
+            pairs = [(at(i, k), at(j, k)) for i, j in pairs for k in range(fill)]
+            pairs += [(at(i, k), at(i, k + 1)) for i in sorted(left) for k in range(0, fill, 2)]
+        rounds.append(pairs + [(j, i) for i, j in pairs])
+    return (tuple(over) if filled else axis), rounds
+
+
+def is_odd(axis):
+    return lax.rem(lax.axis_index(axis), 2)
+
+
+def beyond(axis):
+    at = lax.axis_index(axis)
+    return at == 0, at == lax.axis_size(axis) - 1
 
 
 def is_odd(axis):
@@ -52,6 +73,7 @@
     odd_z = is_odd("grp")
     _, depth, inner, width = own.shape
     groups = inner // 8 + 2
+    first_y, last_y = beyond("gy")
     lane = lax.broadcasted_iota(jnp.int32, (8, LANES), 1)
 
     def plane(p, carry):
@@ -60,8 +82,9 @@
         for a, g, slot in slots(8 * groups):
             if g == 0 or g == groups - 1:
                 from_a, from_b = got_a[a, p], got_b[a, p]
-                above = odd_y == (1 if g == 0 else 0)
-                strip = jnp.where(above, from_a, from_b)
+                low = g == 0
+                strip = jnp.where(odd_y == (1 if low else 0), from_a, from_b)
+                strip = jnp.where(first_y if low else last_y, 0.0, strip)
                 rim[0 if g == 0 else 1, a, p] = strip
                 head, tail = strip[:, 0:LANES], strip[:, width - LANES : width]
             else:
@@ -253,6 +276,7 @@
     depth, inner, width = inside.shape
     rows = inner + 2 * HALO
     odd_z = is_odd("grp")
+    first_z, last_z = beyond("grp")
     lane = lax.broadcasted_iota(jnp.int32, (8, LANES), 1)
     in_right = lane < HALO
     in_left = (lane >= LANES // 2 - HALO) & (lane < LANES // 2)
@@ -263,8 +287,8 @@
                 va, vb = got_a[t, p_from], got_b[t, p_from]
             else:
                 va, vb = near_got[i][0, t, p_from], near_got[i][1, t, p_from]
-            upper = jnp.where(odd_z == 1, vb, va)
-            lower = jnp.where(odd_z == 1, va, vb)
+            upper = jnp.where(last_z, 0.0, jnp.where(odd_z == 1, vb, va))
+            lower = jnp.where(first_z, 0.0, jnp.where(odd_z == 1, va, vb))
             for a, g, slot in slots(rows):
                 if slot // 16 == t:
                     at = 8 * (slot % 16)
@@ -301,8 +325,9 @@
     args = (source_term, conductivity, initial_field)
 
     def exchange(values, axis):
-        found = [lax.ppermute(v, axis, pairs) for v, pairs in zip(values, swaps(axis, sizes[axis]))]
-        return found + [jnp.zeros_like(v) for v in values[len(found) :]]
+        over, rounds = swaps(axis, sizes)
+        found = [lax.ppermute(v, over, pairs) for v, pairs in reversed(list(zip(values, rounds)))]
+        return found[::-1] + [jnp.zeros_like(v) for v in values[len(found) :]]
 
     def work(lanes):
         total = layout(reflect, depth)[1]

time: 29.6 us -> 25.8 us (0.87)
  starting transfers between devices: 8.71 us -> 4.84 us
    ppermute x7, starting transfers between devices: 8.71 us -> 4.84 us  [exchange(): lax.ppermute(v, over, pairs)]
  transfers between devices with their start and end apart: 7 -> 7, of which waited for: 3 -> 3; matrix products, arithmetic and copies ran while one was open for 0% -> 0% of each run, Pallas kernels for 23% -> 27%
where the time goes in v4:
time: 25.8 us; the launch traced here: 25.3 us
  Pallas kernels  11.7 us (45%)
  waiting for transfers between devices  7.61 us (29%)
  starting transfers between devices  4.84 us (19%)
  other arithmetic  1.06 us (4%)
    ppermute x7, waiting for transfers between devices, exchange(): lax.ppermute(v, over, pairs)  7.61 us
    pallas_call x1, Pallas kernels, shards(): pl.pallas_call(functools.partial(interior, reflect, n_x), out_shape=(bloc...  5.99 us
    pallas_call x1, Pallas kernels, shards(): pl.pallas_call(functools.partial(edges, reflect, n_x), out_shape=block, i...  4.92 us
    ppermute x7, starting transfers between devices, exchange(): lax.ppermute(v, over, pairs)  4.84 us
    another operation x1, other arithmetic, shards(): own = jnp.stack(args)  1.06 us
    pallas_call x1, Pallas kernels, shards(): pl.pallas_call(pack_columns, out_shape=(jax.ShapeDtypeStruct((2, 3, depth...  0.77 us
  transfers between devices with their start and end apart: 7, of which 3 were waited for; matrix products, arithmetic and copies ran while one was open for 0% of the time, Pallas kernels for 27%

profile of v4, /device:TPU:18, one launch (start us, length us, event | category | flops | bytes accessed | tf_op | source)
XLA Modules:
  0.0 25.3 jit_solution(14899472952604392120)
XLA Ops:
  0.0 1.1 %pad_maximum_fusion.own.refs_0_ = f32[3,8,16,256]{3,2,1,0:T(8,128)S(1)} fusion(f32[1,8,16,256]{3,2,1,0:T(8,128)} %bitcast.7, f32[1,8,16,256]{3,2,1,0:T(8,128)} %bitcast.8, f32[1,8,16,256]{3,2,1,0:T(8,128)} %bitcast.9), kind=kLoop, calls=%fused_computation | loop fusion | flops 196608 | bytes 786432 | tf_op jit(solution)/shard_map/stack | solution.py:341
  1.1 1.6 %collective-permute-start = (f32[3,8,8,256]{3,2,1,0:T(8,128)S(1)}, f32[3,8,8,256]{3,2,1,0:T(8,128)S(1)}, u32[]{:S(2)}, u32[]{:S(2)}) collective-permute-start(f32[3,8,8,256]{3,2,1,0:T(8,128)S(1)} %get-tuple-element.16), channel_id=1, source_target_pairs={{0,1},{4,5},{2,3},{6,7},{1,0},{5,4},{3,2},{7,6},{8,9},{12,13},{10,... | collective-permute-start | bytes 589832 | tf_op jit(solution)/shard_map/ppermute | solution.py:329
  2.7 0.0 collective-permute-start.1
  2.8 0.0 collective-permute-start.2
  2.8 5.1 %collective-permute-done.got_a = f32[3,8,8,256]{3,2,1,0:T(8,128)S(1)} collective-permute-done((f32[3,8,8,256]{3,2,1,0:T(8,128)S(1)}, f32[3,8,8,256]{3,2,1,0:T(8,128)S(1)}, u32[]{:S(2)}, u32[]{:S(2)}) %collective-permute-start) | collective-permute-done | bytes 196640 | tf_op jit(solution)/shard_map/ppermute | solution.py:329
  7.8 1.3 %collective-permute-done.1.got_b = f32[3,8,8,256]{3,2,1,0:T(8,128)S(1)} collective-permute-done((f32[3,8,8,256]{3,2,1,0:T(8,128)S(1)}, f32[3,8,8,256]{3,2,1,0:T(8,128)S(1)}, u32[]{:S(2)}, u32[]{:S(2)}) %collective-permute-start.1) | collective-permute-done | bytes 196640 | tf_op jit(solution)/shard_map/ppermute | solution.py:329
  9.1 0.8 %pack_columns.1 = (f32[2,3,8,8,256]{4,3,2,1,0:T(8,128)S(1)}, f32[1,8,8,128]{3,2,1,0:T(8,128)S(1)}, f32[1,8,8,128]{3,2,1,0:T(8,128)S(1)}) custom-call(f32[3,8,16,256]{3,2,1,0:T(8,128)S(1)} %pad_maximum_fusion.own.refs_0_, f32[3,8,8,256]{3,2,1,0:T(8,128)S(1)} %collective-permute-done.got_a, f32[3,8,8,256]{3,2,1,0:T(8,128)S(1)} %collective-permute-done.1.got_b), custom_call_target="tpu_custom_call" | custom-call | tf_op jit(solution)/shard_map/pack_columns/pallas_call | solution.py:351
  9.9 0.1 collective-permute-start.3
  10.0 0.6 %collective-permute-start.4 = (f32[1,8,8,128]{3,2,1,0:T(8,128)S(1)}, f32[1,8,8,128]{3,2,1,0:T(8,128)S(1)}, u32[]{:S(2)}, u32[]{:S(2)}) collective-permute-start(f32[1,8,8,128]{3,2,1,0:T(8,128)S(1)} %get-tuple-element.21), channel_id=1, source_target_pairs={{0,8},{4,12},{16,24},{20,28},{8,0},{12,4},{24,16},{28,20},{1,9},{5... | collective-permute-start | bytes 98312 | tf_op jit(solution)/shard_map/ppermute | solution.py:329
  10.6 2.4 %collective-permute-start.5 = (f32[1,8,8,128]{3,2,1,0:T(8,128)S(1)}, f32[1,8,8,128]{3,2,1,0:T(8,128)S(1)}, u32[]{:S(2)}, u32[]{:S(2)}) collective-permute-start(f32[1,8,8,128]{3,2,1,0:T(8,128)S(1)} %get-tuple-element.22), channel_id=1, source_target_pairs={{8,16},{12,20},{0,4},{24,28},{16,8},{20,12},{4,0},{28,24},{9,17},{... | collective-permute-start | bytes 98312 | tf_op jit(solution)/shard_map/ppermute | solution.py:329
  13.0 0.0 collective-permute-done.2.refs_2_
  13.0 0.0 collective-permute-done.3.refs_3_
  13.0 6.0 %interior.1 = (f32[8,16,256]{2,1,0:T(8,128)S(1)}, f32[3,18,32,128]{3,2,1,0:T(8,128)S(1)}) custom-call(f32[3,8,16,256]{3,2,1,0:T(8,128)S(1)} %pad_maximum_fusion.own.refs_0_, f32[2,3,8,8,256]{4,3,2,1,0:T(8,128)S(1)} %get-tuple-element.18.refs_1_, f32[3,8,16,256]{3,2,1,0:T(8,128)S(1)} %collective-permute-done.2.refs_2_, ...), custom_call_target="tpu_custom_call" | custom-call | flops 20000000 | bytes 20000000 | tf_op jit(solution)/shard_map/interior/pallas_call | solution.py:362
  19.0 0.0 collective-permute-done.4.refs_2_
  19.0 0.0 collective-permute-done.5.refs_3_
  19.1 0.1 collective-permute-start.6
  19.1 1.2 %collective-permute-done.6.refs_4_ = f32[2,1,8,8,128]{4,3,2,1,0:T(8,128)S(1)} collective-permute-done((f32[2,1,8,8,128]{4,3,2,1,0:T(8,128)S(1)}, f32[2,1,8,8,128]{4,3,2,1,0:T(8,128)S(1)}, u32[]{:S(2)}, u32[]{:S(2)}) %collective-permute-start.6) | collective-permute-done | bytes 65568 | tf_op jit(solution)/shard_map/ppermute | solution.py:329
  20.4 4.9 %edges.1 = f32[8,16,256]{2,1,0:T(8,128)} custom-call(f32[3,18,32,128]{3,2,1,0:T(8,128)S(1)} %get-tuple-element.23.refs_0_, f32[8,16,256]{2,1,0:T(8,128)S(1)} %get-tuple-element.24.refs_1_, f32[1,8,8,128]{3,2,1,0:T(8,128)S(1)} %collective-permute-done.4.refs_2_, f32[1,8,8,128]{3,2,1,0:T(8,128)S(1)} %collective-permute-done.5.refs_3_, ...), custom_call_target="tpu_custom_call" | custom-call | tf_op jit(solution)/shard_map/edges/pallas_call | solution.py:371
  (2 shorter events, 0.0 us)
Async XLA Ops:
  1.1 6.7 %collective-permute-start = (f32[3,8,8,256]{3,2,1,0:T(8,128)S(1)}, f32[3,8,8,256]{3,2,1,0:T(8,128)S(1)}, u32[]{:S(2)}, u32[]{:S(2)}) collective-permute-start(f32[3,8,8,256]{3,2,1,0:T(8,128)S(1)} %get-tuple-element.16), channel_id=1, source_target_pairs={{0,1},{4,5},{2,3},{6,7},{1,0},{5,4},{3,2},{7,6},{8,9},{12,13},{10,... | collective-permute-start | bytes 589832 | tf_op jit(solution)/shard_map/ppermute | solution.py:329
  2.7 6.4 %collective-permute-start.1 = (f32[3,8,8,256]{3,2,1,0:T(8,128)S(1)}, f32[3,8,8,256]{3,2,1,0:T(8,128)S(1)}, u32[]{:S(2)}, u32[]{:S(2)}) collective-permute-start(f32[3,8,8,256]{3,2,1,0:T(8,128)S(1)} %get-tuple-element.17), channel_id=1, source_target_pairs={{1,2},{5,6},{0,4},{3,7},{2,1},{6,5},{4,0},{7,3},{9,10},{13,14},{8,... | collective-permute-start | bytes 589832 | tf_op jit(solution)/shard_map/ppermute | solution.py:329
  2.8 10.3 %collective-permute-start.2 = (f32[3,8,16,256]{3,2,1,0:T(8,128)S(1)}, f32[3,8,16,256]{3,2,1,0:T(8,128)S(1)}, u32[]{:S(2)}, u32[]{:S(2)}) collective-permute-start(f32[3,8,16,256]{3,2,1,0:T(8,128)S(1)} %pad_maximum_fusion.own.refs_0_), channel_id=1, source_target_pairs={{0,4},{4,0},{1,5},{5,1},{2,6},{6,2},{3,7},{7,3},{8,12},{12,8},{9,1... | collective-permute-start | bytes 1179656 | tf_op jit(solution)/shard_map/ppermute | solution.py:329
  9.9 3.1 %collective-permute-start.3 = (f32[2,3,8,8,256]{4,3,2,1,0:T(8,128)S(1)}, f32[2,3,8,8,256]{4,3,2,1,0:T(8,128)S(1)}, u32[]{:S(2)}, u32[]{:S(2)}) collective-permute-start(f32[2,3,8,8,256]{4,3,2,1,0:T(8,128)S(1)} %get-tuple-element.18.refs_1_), channel_id=1, source_target_pairs={{0,4},{4,0},{1,5},{5,1},{2,6},{6,2},{3,7},{7,3},{8,12},{12,8},{9,1... | collective-permute-start | bytes 1179656 | tf_op jit(solution)/shard_map/ppermute | solution.py:329
  10.0 9.1 %collective-permute-start.4 = (f32[1,8,8,128]{3,2,1,0:T(8,128)S(1)}, f32[1,8,8,128]{3,2,1,0:T(8,128)S(1)}, u32[]{:S(2)}, u32[]{:S(2)}) collective-permute-start(f32[1,8,8,128]{3,2,1,0:T(8,128)S(1)} %get-tuple-element.21), channel_id=1, source_target_pairs={{0,8},{4,12},{16,24},{20,28},{8,0},{12,4},{24,16},{28,20},{1,9},{5... | collective-permute-start | bytes 98312 | tf_op jit(solution)/shard_map/ppermute | solution.py:329
  10.6 8.5 %collective-permute-start.5 = (f32[1,8,8,128]{3,2,1,0:T(8,128)S(1)}, f32[1,8,8,128]{3,2,1,0:T(8,128)S(1)}, u32[]{:S(2)}, u32[]{:S(2)}) collective-permute-start(f32[1,8,8,128]{3,2,1,0:T(8,128)S(1)} %get-tuple-element.22), channel_id=1, source_target_pairs={{8,16},{12,20},{0,4},{24,28},{16,8},{20,12},{4,0},{28,24},{9,17},{... | collective-permute-start | bytes 98312 | tf_op jit(solution)/shard_map/ppermute | solution.py:329
  19.1 1.3 %collective-permute-start.6 = (f32[2,1,8,8,128]{4,3,2,1,0:T(8,128)S(1)}, f32[2,1,8,8,128]{4,3,2,1,0:T(8,128)S(1)}, u32[]{:S(2)}, u32[]{:S(2)}) collective-permute-start(f32[2,1,8,8,128]{4,3,2,1,0:T(8,128)S(1)} %pad_maximum_fusion.1), channel_id=1, source_target_pairs={{0,4},{4,0},{1,5},{5,1},{2,6},{6,2},{3,7},{7,3},{8,12},{12,8},{9,1... | collective-permute-start | bytes 196616 | tf_op jit(solution)/shard_map/ppermute | solution.py:329

commit v5 on v4

--- a/solution.py
+++ b/solution.py
@@ -105,7 +105,7 @@
 
 
 def solve(cells, own_at, own, out):
-    (src, cond, field, wx, wy, wz, inv, sum8, cwx, cwy, cwz, cinv, res, q, cq, err) = cells
+    (src, cond, field, wx, wy, wz, vy, vz, diag, inv, sum8, cwx, cwy, cwz, cvy, cvz, cinv, res, q, cq, err) = cells
     total = cond.shape[0]
     rows, lanes = cond.shape[1:]
 
@@ -114,90 +114,85 @@
         high = min(total, own_at + own + halo)
         return (low + 1) // 2, (high + 1) // 2
 
+    def sweep(halo, body):
+        low, high = reach(halo)
+        lax.fori_loop(low, high, lambda k, carry: body(k) or carry, 0, unroll=True)
+
     zero = jnp.zeros((rows, lanes), jnp.float32)
     for ref in (q, cq, err, sum8):
         ref[0] = zero
 
-    def gather8(k, carry):
+    def gather8(k):
         t = cond[2 * k - 1] + cond[2 * k]
         t = t + ahead(t, 0)
         sum8[k] = t + ahead(t, 1)
-        return carry
-
-    lax.fori_loop(*reach(HALO), gather8, 0, unroll=True)
+
+    sweep(HALO, gather8)
 
     def weights(c, below, above, step):
         x = c + above
-        y = c + ahead(c, 0, step)
-        z = c + ahead(c, 1, step)
-        k = (c + below + x) + (y + behind(y, 0, step)) + (z + behind(z, 1, step))
-        return x, y, z, jnp.where(c > 0.0, 1.0 / k, 0.0)
-
-    def setup(k, carry):
+        y, z = c + ahead(c, 0, step), c + ahead(c, 1, step)
+        yb, zb = c + behind(c, 0, step), c + behind(c, 1, step)
+        k = (c + below + x) + (y + yb) + (z + zb)
+        return x, y, z, yb, zb, k, jnp.where(c > 0.0, 1.0 / k, 0.0)
+
+    def setup(k):
         for p in (2 * k - 1, 2 * k):
-            wx[p], wy[p], wz[p], inv[p] = weights(cond[p], cond[p - 1], cond[p + 1], 1)
-        cwx[k], cwy[k], cwz[k], cinv[k] = weights(sum8[k], sum8[k - 1], sum8[k + 1], 2)
-        return carry
-
-    low, high = reach(HALO - 2)
+            wx[p], wy[p], wz[p], vy[p], vz[p], diag[p], inv[p] = weights(cond[p], cond[p - 1], cond[p + 1], 1)
+        cwx[k], cwy[k], cwz[k], cvy[k], cvz[k], _, cinv[k] = weights(sum8[k], sum8[k - 1], sum8[k + 1], 2)
+
+    low, _ = reach(HALO - 2)
     wx[2 * low - 2] = cond[2 * low - 2] + cond[2 * low - 1]
     cwx[low - 1] = sum8[low - 1] + sum8[low]
-    lax.fori_loop(low, high, setup, 0, unroll=True)
+    sweep(HALO - 2, setup)
 
     row = lax.broadcasted_iota(jnp.int32, (rows, lanes), 0)
     lane = lax.broadcasted_iota(jnp.int32, (rows, lanes), 1)
     even_row = lax.rem(row, 2) == 0
     even_lane = lax.rem(lane, 2) == 0
 
-    def image(v, p):
-        here = v[p]
-        across = wx[p - 1] * (here - v[p - 1]) - wx[p] * (v[p + 1] - here)
-        fy = wy[p] * (ahead(here, 0) - here)
-        fz = wz[p] * (ahead(here, 1) - here)
-        return across + (behind(fy, 0) - fy) + (behind(fz, 1) - fz)
-
-    def spread(v, p, x, y, z, step):
+    def spread(v, p, x, y, z, yb, zb, step):
         here = v[p]
         n = x[p - 1] * v[p - 1] + x[p] * v[p + 1]
-        n = n + (y[p] * ahead(here, 0, step) + behind(y[p] * here, 0, step))
-        return n + (z[p] * ahead(here, 1, step) + behind(z[p] * here, 1, step))
-
-    def smooth(v, p, x, y, z, diag, step):
-        return KEEP * v[p] + SPREAD * (diag[p] * spread(v, p, x, y, z, step))
+        n = n + (y[p] * ahead(here, 0, step) + yb[p] * behind(here, 0, step))
+        return n + (z[p] * ahead(here, 1, step) + zb[p] * behind(here, 1, step))
+
+    def image(v, p):
+        return diag[p] * v[p] - spread(v, p, wx, wy, wz, vy, vz, 1)
 
     for it in range(ITERS):
         halo = 4 * (ITERS - 1 - it)
 
-        def residuals(k, carry, it=it):
+        def residuals(k, it=it):
             both = None
             for p in (2 * k - 1, 2 * k):
                 if it == 0:
                     r = 2.0 * src[p] - image(field, p)
                 else:
                     r = res[p] - image(err, p)
-                res[p] = r
+                if it < ITERS - 1:
+                    res[p] = r
                 q[p] = r * inv[p]
                 both = r if both is None else both + r
             both = both + ahead(both, 0)
             both = both + ahead(both, 1)
             cq[k] = (4.0 * both) * cinv[k]
-            return carry
-
-        lax.fori_loop(*reach(halo + 2), residuals, 0, unroll=True)
-
-        def corrections(k, carry, it=it):
-            coarse = smooth(cq, k, cwx, cwy, cwz, cinv, 2)
+
+        sweep(halo + 2, residuals)
+
+        def corrections(k, it=it):
+            coarse = KEEP * cq[k] + SPREAD * (cinv[k] * spread(cq, k, cwx, cwy, cwz, cvy, cvz, 2))
             coarse = jnp.where(even_lane, coarse, behind(coarse, 1))
             coarse = jnp.where(even_row, coarse, behind(coarse, 0))
             for p in (2 * k - 1, 2 * k):
-                e = smooth(q, p, wx, wy, wz, inv, 1) + coarse
+                e = KEEP * q[p] + SPREAD * (inv[p] * spread(q, p, wx, wy, wz, vy, vz, 1))
+                e = e + coarse
                 if it < ITERS - 1:
                     err[p] = err[p] + e if it else e
                 else:
                     out(p, field[p] + (err[p] + e if it else e))
-            return carry
-
-        lax.fori_loop(*reach(halo), corrections, 0, unroll=True)
+
+        sweep(halo, corrections)
 
 
 def layout(reflect, depth):
@@ -333,7 +328,7 @@
         total = layout(reflect, depth)[1]
         fine = pltpu.VMEM((total, rows, lanes), f32)
         coarse = pltpu.VMEM((total // 2 + 1, rows, lanes), f32)
-        return [fine] * 7 + [coarse] * 5 + [fine] * 2 + [coarse] + [fine]
+        return [fine] * 10 + [coarse] * 7 + [fine] * 2 + [coarse] + [fine]
 
     reflect = sizes["gx"] == 2
     n_x = 1 if reflect else 2

time: 25.8 us -> 21.1 us (0.82)
  the two profiles are of different devices: /device:TPU:18 before, /device:TPU:19 now
where the time goes in v5:
time: 21.1 us; the launch traced here: 21 us
  starting transfers between devices  7.38 us (35%)
  Pallas kernels  7.07 us (34%)
  waiting for transfers between devices  5.4 us (26%)
  other arithmetic  1.06 us (5%)
    ppermute x7, starting transfers between devices, exchange(): lax.ppermute(v, over, pairs)  7.38 us
    ppermute x7, waiting for transfers between devices, exchange(): lax.ppermute(v, over, pairs)  5.4 us
    pallas_call x1, Pallas kernels, shards(): pl.pallas_call(functools.partial(interior, reflect, n_x), out_shape=(bloc...  3.3 us
    pallas_call x1, Pallas kernels, shards(): pl.pallas_call(functools.partial(edges, reflect, n_x), out_shape=block, i...  2.96 us
    another operation x1, other arithmetic, shards(): own = jnp.stack(args)  1.06 us
    pallas_call x1, Pallas kernels, shards(): pl.pallas_call(pack_columns, out_shape=(jax.ShapeDtypeStruct((2, 3, depth...  0.77 us
  transfers between devices with their start and end apart: 7, of which 3 were waited for; matrix products, arithmetic and copies ran while one was open for 0% of the time, Pallas kernels for 19%

profile of v5, /device:TPU:19, one launch (start us, length us, event | category | flops | bytes accessed | tf_op | source)
XLA Modules:
  0.0 21.0 jit_solution(9783972068209852621)
XLA Ops:
  0.0 1.1 %pad_maximum_fusion.own.refs_0_ = f32[3,8,16,256]{3,2,1,0:T(8,128)S(1)} fusion(f32[1,8,16,256]{3,2,1,0:T(8,128)} %bitcast.7, f32[1,8,16,256]{3,2,1,0:T(8,128)} %bitcast.8, f32[1,8,16,256]{3,2,1,0:T(8,128)} %bitcast.9), kind=kLoop, calls=%fused_computation | loop fusion | flops 196608 | bytes 786432 | tf_op jit(solution)/shard_map/stack | solution.py:336
  1.1 1.4 %collective-permute-start = (f32[3,8,8,256]{3,2,1,0:T(8,128)S(1)}, f32[3,8,8,256]{3,2,1,0:T(8,128)S(1)}, u32[]{:S(2)}, u32[]{:S(2)}) collective-permute-start(f32[3,8,8,256]{3,2,1,0:T(8,128)S(1)} %get-tuple-element.16), channel_id=1, source_target_pairs={{0,1},{4,5},{2,3},{6,7},{1,0},{5,4},{3,2},{7,6},{8,9},{12,13},{10,... | collective-permute-start | bytes 589832 | tf_op jit(solution)/shard_map/ppermute | solution.py:324
  2.5 0.0 collective-permute-start.1
  2.5 1.0 %collective-permute-start.2 = (f32[3,8,16,256]{3,2,1,0:T(8,128)S(1)}, f32[3,8,16,256]{3,2,1,0:T(8,128)S(1)}, u32[]{:S(2)}, u32[]{:S(2)}) collective-permute-start(f32[3,8,16,256]{3,2,1,0:T(8,128)S(1)} %pad_maximum_fusion.own.refs_0_), channel_id=1, source_target_pairs={{0,4},{4,0},{1,5},{5,1},{2,6},{6,2},{3,7},{7,3},{8,12},{12,8},{9,1... | collective-permute-start | bytes 1179656 | tf_op jit(solution)/shard_map/ppermute | solution.py:324
  3.4 3.5 %collective-permute-done.got_a = f32[3,8,8,256]{3,2,1,0:T(8,128)S(1)} collective-permute-done((f32[3,8,8,256]{3,2,1,0:T(8,128)S(1)}, f32[3,8,8,256]{3,2,1,0:T(8,128)S(1)}, u32[]{:S(2)}, u32[]{:S(2)}) %collective-permute-start) | collective-permute-done | bytes 196640 | tf_op jit(solution)/shard_map/ppermute | solution.py:324
  6.9 1.0 %collective-permute-done.1.got_b = f32[3,8,8,256]{3,2,1,0:T(8,128)S(1)} collective-permute-done((f32[3,8,8,256]{3,2,1,0:T(8,128)S(1)}, f32[3,8,8,256]{3,2,1,0:T(8,128)S(1)}, u32[]{:S(2)}, u32[]{:S(2)}) %collective-permute-start.1) | collective-permute-done | bytes 196640 | tf_op jit(solution)/shard_map/ppermute | solution.py:324
  7.9 0.8 %pack_columns.1 = (f32[2,3,8,8,256]{4,3,2,1,0:T(8,128)S(1)}, f32[1,8,8,128]{3,2,1,0:T(8,128)S(1)}, f32[1,8,8,128]{3,2,1,0:T(8,128)S(1)}) custom-call(f32[3,8,16,256]{3,2,1,0:T(8,128)S(1)} %pad_maximum_fusion.own.refs_0_, f32[3,8,8,256]{3,2,1,0:T(8,128)S(1)} %collective-permute-done.got_a, f32[3,8,8,256]{3,2,1,0:T(8,128)S(1)} %collective-permute-done.1.got_b), custom_call_target="tpu_custom_call" | custom-call | tf_op jit(solution)/shard_map/pack_columns/pallas_call | solution.py:346
  8.7 1.9 %collective-permute-start.3 = (f32[2,3,8,8,256]{4,3,2,1,0:T(8,128)S(1)}, f32[2,3,8,8,256]{4,3,2,1,0:T(8,128)S(1)}, u32[]{:S(2)}, u32[]{:S(2)}) collective-permute-start(f32[2,3,8,8,256]{4,3,2,1,0:T(8,128)S(1)} %get-tuple-element.18.refs_1_), channel_id=1, source_target_pairs={{0,4},{4,0},{1,5},{5,1},{2,6},{6,2},{3,7},{7,3},{8,12},{12,8},{9,1... | collective-permute-start | bytes 1179656 | tf_op jit(solution)/shard_map/ppermute | solution.py:324
  10.6 0.3 %collective-permute-start.4 = (f32[1,8,8,128]{3,2,1,0:T(8,128)S(1)}, f32[1,8,8,128]{3,2,1,0:T(8,128)S(1)}, u32[]{:S(2)}, u32[]{:S(2)}) collective-permute-start(f32[1,8,8,128]{3,2,1,0:T(8,128)S(1)} %get-tuple-element.21), channel_id=1, source_target_pairs={{0,8},{4,12},{16,24},{20,28},{8,0},{12,4},{24,16},{28,20},{1,9},{5... | collective-permute-start | bytes 98312 | tf_op jit(solution)/shard_map/ppermute | solution.py:324
  10.9 2.2 %collective-permute-start.5 = (f32[1,8,8,128]{3,2,1,0:T(8,128)S(1)}, f32[1,8,8,128]{3,2,1,0:T(8,128)S(1)}, u32[]{:S(2)}, u32[]{:S(2)}) collective-permute-start(f32[1,8,8,128]{3,2,1,0:T(8,128)S(1)} %get-tuple-element.22), channel_id=1, source_target_pairs={{8,16},{12,20},{0,4},{24,28},{16,8},{20,12},{4,0},{28,24},{9,17},{... | collective-permute-start | bytes 98312 | tf_op jit(solution)/shard_map/ppermute | solution.py:324
  13.1 0.0 collective-permute-done.2.refs_2_
  13.1 0.0 collective-permute-done.3.refs_3_
  13.1 3.3 %interior.1 = (f32[8,16,256]{2,1,0:T(8,128)S(1)}, f32[3,18,32,128]{3,2,1,0:T(8,128)S(1)}) custom-call(f32[3,8,16,256]{3,2,1,0:T(8,128)S(1)} %pad_maximum_fusion.own.refs_0_, f32[2,3,8,8,256]{4,3,2,1,0:T(8,128)S(1)} %get-tuple-element.18.refs_1_, f32[3,8,16,256]{3,2,1,0:T(8,128)S(1)} %collective-permute-done.2.refs_2_, ...), custom_call_target="tpu_custom_call" | custom-call | flops 20000000 | bytes 20000000 | tf_op jit(solution)/shard_map/interior/pallas_call | solution.py:357
  16.4 0.0 collective-permute-done.4.refs_2_
  16.4 0.0 collective-permute-done.5.refs_3_
  16.4 0.7 %collective-permute-start.6 = (f32[2,1,8,8,128]{4,3,2,1,0:T(8,128)S(1)}, f32[2,1,8,8,128]{4,3,2,1,0:T(8,128)S(1)}, u32[]{:S(2)}, u32[]{:S(2)}) collective-permute-start(f32[2,1,8,8,128]{4,3,2,1,0:T(8,128)S(1)} %pad_maximum_fusion.1), channel_id=1, source_target_pairs={{0,4},{4,0},{1,5},{5,1},{2,6},{6,2},{3,7},{7,3},{8,12},{12,8},{9,1... | collective-permute-start | bytes 196616 | tf_op jit(solution)/shard_map/ppermute | solution.py:324
  17.1 0.9 %collective-permute-done.6.refs_4_ = f32[2,1,8,8,128]{4,3,2,1,0:T(8,128)S(1)} collective-permute-done((f32[2,1,8,8,128]{4,3,2,1,0:T(8,128)S(1)}, f32[2,1,8,8,128]{4,3,2,1,0:T(8,128)S(1)}, u32[]{:S(2)}, u32[]{:S(2)}) %collective-permute-start.6) | collective-permute-done | bytes 65568 | tf_op jit(solution)/shard_map/ppermute | solution.py:324
  18.0 3.0 %edges.1 = f32[8,16,256]{2,1,0:T(8,128)} custom-call(f32[3,18,32,128]{3,2,1,0:T(8,128)S(1)} %get-tuple-element.23.refs_0_, f32[8,16,256]{2,1,0:T(8,128)S(1)} %get-tuple-element.24.refs_1_, f32[1,8,8,128]{3,2,1,0:T(8,128)S(1)} %collective-permute-done.4.refs_2_, f32[1,8,8,128]{3,2,1,0:T(8,128)S(1)} %collective-permute-done.5.refs_3_, ...), custom_call_target="tpu_custom_call" | custom-call | tf_op jit(solution)/shard_map/edges/pallas_call | solution.py:366
  (2 shorter events, 0.0 us)
Async XLA Ops:
  1.1 5.8 %collective-permute-start = (f32[3,8,8,256]{3,2,1,0:T(8,128)S(1)}, f32[3,8,8,256]{3,2,1,0:T(8,128)S(1)}, u32[]{:S(2)}, u32[]{:S(2)}) collective-permute-start(f32[3,8,8,256]{3,2,1,0:T(8,128)S(1)} %get-tuple-element.16), channel_id=1, source_target_pairs={{0,1},{4,5},{2,3},{6,7},{1,0},{5,4},{3,2},{7,6},{8,9},{12,13},{10,... | collective-permute-start | bytes 589832 | tf_op jit(solution)/shard_map/ppermute | solution.py:324
  2.5 5.5 %collective-permute-start.1 = (f32[3,8,8,256]{3,2,1,0:T(8,128)S(1)}, f32[3,8,8,256]{3,2,1,0:T(8,128)S(1)}, u32[]{:S(2)}, u32[]{:S(2)}) collective-permute-start(f32[3,8,8,256]{3,2,1,0:T(8,128)S(1)} %get-tuple-element.17), channel_id=1, source_target_pairs={{1,2},{5,6},{0,4},{3,7},{2,1},{6,5},{4,0},{7,3},{9,10},{13,14},{8,... | collective-permute-start | bytes 589832 | tf_op jit(solution)/shard_map/ppermute | solution.py:324
  2.5 10.6 %collective-permute-start.2 = (f32[3,8,16,256]{3,2,1,0:T(8,128)S(1)}, f32[3,8,16,256]{3,2,1,0:T(8,128)S(1)}, u32[]{:S(2)}, u32[]{:S(2)}) collective-permute-start(f32[3,8,16,256]{3,2,1,0:T(8,128)S(1)} %pad_maximum_fusion.own.refs_0_), channel_id=1, source_target_pairs={{0,4},{4,0},{1,5},{5,1},{2,6},{6,2},{3,7},{7,3},{8,12},{12,8},{9,1... | collective-permute-start | bytes 1179656 | tf_op jit(solution)/shard_map/ppermute | solution.py:324
  8.7 4.4 %collective-permute-start.3 = (f32[2,3,8,8,256]{4,3,2,1,0:T(8,128)S(1)}, f32[2,3,8,8,256]{4,3,2,1,0:T(8,128)S(1)}, u32[]{:S(2)}, u32[]{:S(2)}) collective-permute-start(f32[2,3,8,8,256]{4,3,2,1,0:T(8,128)S(1)} %get-tuple-element.18.refs_1_), channel_id=1, source_target_pairs={{0,4},{4,0},{1,5},{5,1},{2,6},{6,2},{3,7},{7,3},{8,12},{12,8},{9,1... | collective-permute-start | bytes 1179656 | tf_op jit(solution)/shard_map/ppermute | solution.py:324
  10.6 5.8 %collective-permute-start.4 = (f32[1,8,8,128]{3,2,1,0:T(8,128)S(1)}, f32[1,8,8,128]{3,2,1,0:T(8,128)S(1)}, u32[]{:S(2)}, u32[]{:S(2)}) collective-permute-start(f32[1,8,8,128]{3,2,1,0:T(8,128)S(1)} %get-tuple-element.21), channel_id=1, source_target_pairs={{0,8},{4,12},{16,24},{20,28},{8,0},{12,4},{24,16},{28,20},{1,9},{5... | collective-permute-start | bytes 98312 | tf_op jit(solution)/shard_map/ppermute | solution.py:324
  10.9 5.5 %collective-permute-start.5 = (f32[1,8,8,128]{3,2,1,0:T(8,128)S(1)}, f32[1,8,8,128]{3,2,1,0:T(8,128)S(1)}, u32[]{:S(2)}, u32[]{:S(2)}) collective-permute-start(f32[1,8,8,128]{3,2,1,0:T(8,128)S(1)} %get-tuple-element.22), channel_id=1, source_target_pairs={{8,16},{12,20},{0,4},{24,28},{16,8},{20,12},{4,0},{28,24},{9,17},{... | collective-permute-start | bytes 98312 | tf_op jit(solution)/shard_map/ppermute | solution.py:324
  16.4 1.6 %collective-permute-start.6 = (f32[2,1,8,8,128]{4,3,2,1,0:T(8,128)S(1)}, f32[2,1,8,8,128]{4,3,2,1,0:T(8,128)S(1)}, u32[]{:S(2)}, u32[]{:S(2)}) collective-permute-start(f32[2,1,8,8,128]{4,3,2,1,0:T(8,128)S(1)} %pad_maximum_fusion.1), channel_id=1, source_target_pairs={{0,4},{4,0},{1,5},{5,1},{2,6},{6,2},{3,7},{7,3},{8,12},{12,8},{9,1... | collective-permute-start | bytes 196616 | tf_op jit(solution)/shard_map/ppermute | solution.py:324

commit v6 on v5

v6 whole, which is shorter than its diff:
```python
import functools

import jax
import jax.numpy as jnp
from jax import lax
from jax.experimental import pallas as pl
from jax.experimental.pallas import tpu as pltpu
from jax.sharding import PartitionSpec as P

ITERS = 2
HALO = 4 * ITERS
LANES = 128
KEEP = 48.0 / 41.0
SPREAD = 32.0 / 41.0
VMEM = pl.BlockSpec(memory_space=pltpu.VMEM)


def ahead(v, axis, n=1):
    return pltpu.roll(v, v.shape[axis] - n, axis)


def behind(v, axis, n=1):
    return pltpu.roll(v, n, axis)


def swaps(axis, sizes):
    count, fill = sizes[axis], sizes["gx"]
    over = [name for name in sizes if name in (axis, "gx")]
    filled = axis != "gx" and fill % 2 == 0

    def at(i, k):
        return i * fill + k if over[0] == axis else k * count + i

    rounds = []
    for start in (0, 1):
        pairs = [(i, i + 1) for i in range(start, count - 1, 2)]
        left = set(range(count)) - {i for pair in pairs for i in pair}
        if not pairs:
            continue
        if filled:
            pairs = [(at(i, k), at(j, k)) for i, j in pairs for k in range(fill)]
            pairs += [(at(i, k), at(i, k + 1)) for i in sorted(left) for k in range(0, fill, 2)]
        rounds.append(pairs + [(j, i) for i, j in pairs])
    return (tuple(over) if filled else axis), rounds


def is_odd(axis):
    return lax.rem(lax.axis_index(axis), 2)


def beyond(axis):
    at = lax.axis_index(axis)
    return at == 0, at == lax.axis_size(axis) - 1


def is_odd(axis):
    return lax.rem(lax.axis_index(axis), 2)


def pack_rows(own, first, second):
    odd = is_odd("gy")
    last = own.shape[2] - HALO
    first[...] = own[:, :, pl.ds(pl.multiple_of((1 - odd) * last, 8), HALO), :]
    second[...] = own[:, :, pl.ds(pl.multiple_of(odd * last, 8), HALO), :]


def slots(rows):
    return [(a, g, a * (rows // 8) + g) for a in range(3) for g in range(rows // 8)]


def pack_columns(own, got_a, got_b, strips, rim):
    odd_y, odd_z = is_odd("gy"), is_odd("grp")
    first_y, last_y = beyond("gy")
    _, depth, inner, width = own.shape
    groups = inner // 8 + 2
    lane = lax.broadcasted_iota(jnp.int32, (8, LANES), 1)
    for p in range(depth):
        for a in range(3):
            from_a, from_b = got_a[a, p], got_b[a, p]
            rim[0, a, p] = jnp.where(first_y, 0.0, jnp.where(odd_y == 1, from_a, from_b))
            rim[1, a, p] = jnp.where(last_y, 0.0, jnp.where(odd_y == 1, from_b, from_a))
        heads = [jnp.zeros((8, LANES), jnp.float32) for _ in range(strips.shape[1])]
        tails = list(heads)
        for a, g, slot in slots(8 * groups):
            t, at = slot // 16, 8 * (slot % 16)
            if g == 0 or g == groups - 1:
                rows = rim[min(g, 1), a, p]
            else:
                rows = own[a, p, 8 * g - 8 : 8 * g, :]
            head = pltpu.roll(rows[:, 0:LANES], at, 1)
            tail = pltpu.roll(rows[:, width - LANES : width], (at + LANES // 2) % LANES, 1)
            far = (at + LANES // 2 - HALO) % LANES
            heads[t] = jnp.where((lane >= at) & (lane < at + HALO), head, heads[t])
            tails[t] = jnp.where((lane >= far) & (lane < far + HALO), tail, tails[t])
        for t, (head, tail) in enumerate(zip(heads, tails)):
            strips[0, t, p] = jnp.where(odd_z == 1, head, tail)
            strips[1, t, p] = jnp.where(odd_z == 1, tail, head)


def shifts(parts, step):
    if parts == 1:
        return (lambda v: [ahead(v[0], 1, step)]), (lambda v: [behind(v[0], 1, step)])
    return (lambda v: [v[1], ahead(v[0], 1)]), (lambda v: [behind(v[1], 1), v[0]])


def each(op, *lists):
    return [op(*values) for values in zip(*lists)]


def add(*lists):
    return each(lambda *values: functools.reduce(lambda x, y: x + y, values), *lists)


def times(x, y):
    return each(lambda v, w: v * w, x, y)


def solve(cells, own_at, own, out):
    (src, cond, field, wx, wy, wz, vy, vz, diag, inv, sum8, cwx, cwy, cwz, cvy, cvz, cinv, res, q, cq, err) = cells
    total, parts, rows, lanes = cond.shape

    def load(ref, p):
        return [ref[p, i] for i in range(ref.shape[1])]

    def store(ref, p, values):
        for i, v in enumerate(values):
            ref[p, i] = v

    def reach(halo):
        low = max(1, own_at - halo)
        high = min(total, own_at + own + halo)
        return range((low + 1) // 2, (high + 1) // 2)

    fine = (1, *shifts(parts, 1))
    coarse = (2, *shifts(1, 3 - parts))
    zero = jnp.zeros((rows, lanes), jnp.float32)
    for ref in (q, cq, err, sum8):
        store(ref, 0, [zero] * ref.shape[1])

    def gather(v):
        t = v[0] + v[1] if parts == 2 else v[0] + ahead(v[0], 1)
        return [t + ahead(t, 0)]

    for k in reach(HALO):
        store(sum8, k, gather(add(load(cond, 2 * k - 1), load(cond, 2 * k))))

    def weights(ref, p, level):
        step, ahead_z, behind_z = level
        c = load(ref, p)
        x = add(c, load(ref, p + 1))
        y, yb = ([v + shift(v, 0, step) for v in c] for shift in (ahead, behind))
        z, zb = add(c, ahead_z(c)), add(c, behind_z(c))
        k = add(add(c, load(ref, p - 1), x), add(y, yb), add(z, zb))
        return x, y, z, yb, zb, k, each(lambda v, w: jnp.where(v > 0.0, 1.0 / w, 0.0), c, k)

    low = reach(HALO - 2).start
    store(wx, 2 * low - 2, add(load(cond, 2 * low - 2), load(cond, 2 * low - 1)))
    store(cwx, low - 1, add(load(sum8, low - 1), load(sum8, low)))
    for k in reach(HALO - 2):
        for p in (2 * k - 1, 2 * k):
            for ref, v in zip((wx, wy, wz, vy, vz, diag, inv), weights(cond, p, fine)):
                store(ref, p, v)
        for ref, v in zip((cwx, cwy, cwz, cvy, cvz, None, cinv), weights(sum8, k, coarse)):
            if ref is not None:
                store(ref, k, v)

    even_row = lax.rem(lax.broadcasted_iota(jnp.int32, (rows, lanes), 0), 2) == 0
    even_lane = lax.rem(lax.broadcasted_iota(jnp.int32, (rows, lanes), 1), 2) == 0

    def spread(v, p, refs, level):
        x, y, z, yb, zb = refs
        step, ahead_z, behind_z = level
        here = load(v, p)
        n = add(times(load(x, p - 1), load(v, p - 1)), times(load(x, p), load(v, p + 1)))
        n = add(n, times(load(y, p), [ahead(u, 0, step) for u in here]))
        n = add(n, times(load(yb, p), [behind(u, 0, step) for u in here]))
        return add(n, add(times(load(z, p), ahead_z(here)), times(load(zb, p), behind_z(here))))

    def smooth(v, p, refs, scale, level):
        n = times(load(scale, p), spread(v, p, refs, level))
        return each(lambda u, w: KEEP * u + SPREAD * w, load(v, p), n)

    around, coarse_around = (wx, wy, wz, vy, vz), (cwx, cwy, cwz, cvy, cvz)

    for it in range(ITERS):
        halo = 4 * (ITERS - 1 - it)
        for k in reach(halo + 2):
            found = []
            for p in (2 * k - 1, 2 * k):
                v = field if it == 0 else err
                start = [2.0 * u for u in load(src, p)] if it == 0 else load(res, p)
                n = spread(v, p, around, fine)
                r = each(lambda u, d, w, m: u - (d * w - m), start, load(diag, p), load(v, p), n)
                if it < ITERS - 1:
                    store(res, p, r)
                store(q, p, times(r, load(inv, p)))
                found.append(r)
            store(cq, k, times([4.0 * gather(add(*found))[0]], load(cinv, k)))

        for k in reach(halo):
            (c,) = smooth(cq, k, coarse_around, cinv, coarse)
            if parts == 1:
                c = jnp.where(even_lane, c, behind(c, 1))
            c = jnp.where(even_row, c, behind(c, 0))
            for p in (2 * k - 1, 2 * k):
                e = [u + c for u in smooth(q, p, around, inv, fine)]
                if it:
                    e = add(load(err, p), e)
                if it < ITERS - 1:
                    store(err, p, e)
                else:
                    out(p, add(load(field, p), e))


def layout(reflect, depth):
    return (1, depth + HALO + 2) if reflect else (1 + HALO, depth + 2 * HALO + 2)


def each_plane(reflect, depth, place):
    odd_x = is_odd("gx")
    own_at, _ = layout(reflect, depth)

    def own_plane(p, carry):
        to = jnp.where(odd_x == 1, depth - 1 - p, p) if reflect else p
        place(None, p, own_at + to)
        return carry

    lax.fori_loop(0, depth, own_plane, 0, unroll=True)

    def near_plane(p, carry):
        if reflect:
            place(0, jnp.where(odd_x == 1, depth - 1 - p, p), own_at + depth + p)
            return carry
        for i in range(2):
            above = odd_x == i
            at = jnp.where(above, p, depth - HALO + p)
            place(i, at, jnp.where(above, own_at + depth + p, 1 + p))
        return carry

    lax.fori_loop(0, HALO, near_plane, 0, unroll=True)


def out_plane(reflect, depth, p):
    own_at, _ = layout(reflect, depth)
    at = p - own_at
    return jnp.where(is_odd("gx") == 1, depth - 1 - at, at) if reflect else at


def parting(width, lanes):
    column = lax.broadcasted_iota(jnp.int32, (width, 2 * lanes), 0)
    lane = lax.broadcasted_iota(jnp.int32, (width, 2 * lanes), 1)
    wanted = jnp.where(lane < lanes, 2 * lane, 2 * (lane - lanes) + 1)
    return jnp.where((column == wanted) & (wanted < width), 1.0, 0.0)


def rearranged(v, matrix):
    bf16, f32 = jnp.bfloat16, jnp.float32
    matrix = matrix.astype(bf16)
    result = None
    for _ in range(3):
        part = v.astype(bf16)
        v = v - part.astype(f32)
        moved = jnp.dot(part, matrix, preferred_element_type=f32)
        result = moved if result is None else result + moved
    return result


def interior(reflect, n_x, *refs):
    own, rim = refs[0], refs[1]
    near, near_rim = refs[2 : 2 + n_x], refs[2 + n_x : 2 + 2 * n_x]
    result, ends = refs[2 + 2 * n_x : 4 + 2 * n_x]
    whole, halves, *cells = refs[4 + 2 * n_x :]
    _, depth, inner, width = own.shape
    rows = inner + 2 * HALO
    lanes = cells[0].shape[3]
    lane = lax.broadcasted_iota(jnp.int32, (rows, LANES), 1)

    def place(i, p_from, p_to):
        block, halo = (own, rim) if i is None else (near[i], near_rim[i])
        for a in range(3):
            tile = whole.at[a, p_to]
            tile[0:HALO, :] = halo[0, a, p_from]
            tile[HALO : HALO + inner, :] = block[a, p_from]
            tile[HALO + inner : rows, :] = halo[1, a, p_from]
            head = pltpu.roll(tile[:, 0:LANES], LANES // 2, 1)
            tail = tile[:, width - LANES : width]
            end = jnp.where((lane >= LANES // 2) & (lane < LANES // 2 + 2 * HALO), head, 0.0)
            ends[a, p_to] = jnp.where(lane >= LANES - 2 * HALO, tail, end)

    own_at, total = layout(reflect, depth)
    for a in range(3):
        for p in (0, total - 1):
            whole[a, p] = jnp.zeros((rows, width), jnp.float32)
            ends[a, p] = jnp.zeros((rows, LANES), jnp.float32)
    each_plane(reflect, depth, place)
    apart = parting(width, lanes)
    for a in range(3):
        parts = rearranged(whole[a].reshape(total * rows, width), apart)
        for i in range(2):
            cells[a][:, i] = parts[:, i * lanes : (i + 1) * lanes].reshape(total, rows, lanes)

    def out(p, v):
        for i in range(2):
            halves[p - own_at, :, i * lanes : (i + 1) * lanes] = v[i][HALO : rows - HALO, :]

    solve(cells, own_at, depth, out)
    together = rearranged(halves[...].reshape(depth * inner, 2 * lanes), apart.T)
    together = together.reshape(depth, inner, width)
    for p in range(depth):
        result[out_plane(reflect, depth, own_at + p)] = together[p]


def edges(reflect, ends, inside, got_a, got_b, result, *cells):
    depth, inner, width = inside.shape
    rows = inner + 2 * HALO
    odd_z = is_odd("grp")
    first_z, last_z = beyond("grp")
    lane = lax.broadcasted_iota(jnp.int32, (8, LANES), 1)
    in_halo = (lane < HALO) | ((lane >= LANES // 2 - HALO) & (lane < LANES // 2))
    own_at, total = layout(reflect, depth)
    for p in (0, total - 1):
        for a in range(3):
            cells[a][p, 0] = ends[a, p]

    def place(i, p_from, p_to):
        at_plane = p_from if i is None else (i + 1) * depth + p_from
        for t in range(got_a.shape[0]):
            va, vb = got_a[t, at_plane], got_b[t, at_plane]
            upper = jnp.where(last_z, 0.0, jnp.where(odd_z == 1, vb, va))
            lower = jnp.where(first_z, 0.0, jnp.where(odd_z == 1, va, vb))
            for a, g, slot in slots(rows):
                if slot // 16 == t:
                    at = 8 * (slot % 16)
                    both = jnp.where((lane >= at) & (lane < at + HALO), upper, lower)
                    both = pltpu.roll(both, (LANES - at) % LANES, 1)
                    part = slice(8 * g, 8 * g + 8)
                    cells[a][p_to, 0, part, :] = jnp.where(in_halo, both, ends[a, p_to, part, :])

    each_plane(reflect, depth, place)
    result[...] = inside[...]
    wide = lax.broadcasted_iota(jnp.int32, (inner, LANES), 1)

    def out(p, v):
        at = out_plane(reflect, depth, p)
        v = v[0][HALO : rows - HALO, :]
        head = pltpu.roll(v, LANES // 2, 1)
        result[at, :, 0:LANES] = jnp.where(wide < HALO, head, result[at, :, 0:LANES])
        tail = result[at, :, width - LANES : width]
        result[at, :, width - LANES : width] = jnp.where(wide >= LANES - HALO, v, tail)

    solve(cells, own_at, depth, out)


def shards(sizes, source_term, conductivity, initial_field):
    depth, inner, width = source_term.shape
    rows = inner + 2 * HALO
    f32 = jnp.float32
    params = pltpu.CompilerParams(vmem_limit_bytes=48 * 1024 * 1024)
    args = (source_term, conductivity, initial_field)

    def exchange(values, axis):
        over, rounds = swaps(axis, sizes)
        found = [lax.ppermute(v, over, pairs) for v, pairs in reversed(list(zip(values, rounds)))]
        return found[::-1] + [jnp.zeros_like(v) for v in values[len(found) :]]

    def work(parts, lanes):
        total = layout(reflect, depth)[1]
        fine = pltpu.VMEM((total, parts, rows, lanes), f32)
        coarse = pltpu.VMEM((total // 2 + 1, 1, rows, lanes), f32)
        return [fine] * 10 + [coarse] * 7 + [fine] * 2 + [coarse] + [fine]

    reflect = sizes["gx"] == 2
    n_x = 1 if reflect else 2
    face = jax.ShapeDtypeStruct((3, depth, HALO, width), f32)
    own = jnp.stack(args)
    msgs = pl.pallas_call(
        pack_rows, out_shape=(face, face), in_specs=[VMEM], out_specs=(VMEM, VMEM),
        compiler_params=params, name="pack_rows",
    )(own)
    got = exchange(msgs, "gy")
    near = exchange([own] * n_x, "gx")
    n_tiles = -(-3 * (rows // 8) // 16)
    strips, rim = pl.pallas_call(
        pack_columns,
        out_shape=(
            jax.ShapeDtypeStruct((2, n_tiles, depth, 8, LANES), f32),
            jax.ShapeDtypeStruct((2, 3, depth, HALO, width), f32),
        ),
        in_specs=[VMEM] * 3, out_specs=(VMEM, VMEM),
        compiler_params=params, name="pack_columns",
    )(own, *got)
    strips = jnp.concatenate([strips] + exchange([strips] * n_x, "gx"), axis=2)
    strips, rim = lax.optimization_barrier((strips, rim))
    near_rim = exchange([rim] * n_x, "gx")
    strips = exchange([strips[0], strips[1]], "grp")

    block = jax.ShapeDtypeStruct(source_term.shape, f32)
    total = layout(reflect, depth)[1]
    lanes = -(-width // (2 * LANES)) * LANES
    apart = [pltpu.VMEM((3, total, rows, width), f32), pltpu.VMEM((depth, inner, 2 * lanes), f32)]
    inside, ends = pl.pallas_call(
        functools.partial(interior, reflect, n_x),
        out_shape=(block, jax.ShapeDtypeStruct((3, total, rows, LANES), f32)),
        in_specs=[VMEM] * (2 + 2 * n_x), out_specs=(VMEM, VMEM), scratch_shapes=apart + work(2, lanes),
        compiler_params=params, name="interior",
        cost_estimate=pl.CostEstimate(flops=20_000_000, bytes_accessed=20_000_000, transcendentals=0),
    )(own, rim, *near, *near_rim)
    inside, ends, *strips = lax.optimization_barrier((inside, ends, *strips[::-1]))
    strips = strips[::-1]
    return pl.pallas_call(
        functools.partial(edges, reflect),
        out_shape=block,
        in_specs=[VMEM] * 4, out_specs=VMEM, scratch_shapes=work(1, LANES),
        compiler_params=params, name="edges",
    )(ends, inside, *strips)


def solution(mesh):
    spec = P("gx", "gy", "grp")
    return jax.shard_map(
        functools.partial(shards, dict(mesh.shape)),
        mesh=mesh,
        in_specs=(spec,) * 3,
        out_specs=spec,
        check_vma=False,
    )
```

time: 21.1 us -> 20.6 us (0.976)
  the two profiles are of different devices: /device:TPU:19 before, /device:TPU:18 now
where the time goes in v6:
time: 20.6 us; the launch traced here: 20.5 us
  waiting for transfers between devices  8.33 us (40%)
  Pallas kernels  5.53 us (27%)
  starting transfers between devices  5.48 us (27%)
  other arithmetic  1.07 us (5%)
    ppermute x7, waiting for transfers between devices, exchange(): lax.ppermute(v, over, pairs)  8.33 us
    ppermute x7, starting transfers between devices, exchange(): lax.ppermute(v, over, pairs)  5.48 us
    pallas_call x1, Pallas kernels, shards(): pl.pallas_call(functools.partial(edges, reflect), out_shape=block, in_spe...  2.76 us
    pallas_call x1, Pallas kernels, shards(): pl.pallas_call(functools.partial(interior, reflect, n_x), out_shape=(bloc...  2.48 us
    another operation x1, other arithmetic, shards(): own = jnp.stack(args)  1.06 us
  transfers between devices with their start and end apart: 7, of which 4 were waited for; matrix products, arithmetic and copies ran while one was open for 0% of the time, Pallas kernels for 12%

profile of v6, /device:TPU:18, one launch (start us, length us, event | category | flops | bytes accessed | tf_op | source)
XLA Modules:
  0.0 20.5 jit_solution(15768738445530955273)
XLA Ops:
  0.0 1.1 %pad_maximum_fusion.own.refs_0_ = f32[3,8,16,256]{3,2,1,0:T(8,128)S(1)} fusion(f32[1,8,16,256]{3,2,1,0:T(8,128)} %bitcast.7, f32[1,8,16,256]{3,2,1,0:T(8,128)} %bitcast.8, f32[1,8,16,256]{3,2,1,0:T(8,128)} %bitcast.9), kind=kLoop, calls=%fused_computation | loop fusion | flops 196608 | bytes 786432 | tf_op jit(solution)/shard_map/stack | solution.py:375
  1.1 1.6 %collective-permute-start = (f32[3,8,8,256]{3,2,1,0:T(8,128)S(1)}, f32[3,8,8,256]{3,2,1,0:T(8,128)S(1)}, u32[]{:S(2)}, u32[]{:S(2)}) collective-permute-start(f32[3,8,8,256]{3,2,1,0:T(8,128)S(1)} %get-tuple-element.17), channel_id=1, source_target_pairs={{0,1},{4,5},{2,3},{6,7},{1,0},{5,4},{3,2},{7,6},{8,9},{12,13},{10,... | collective-permute-start | bytes 589832 | tf_op jit(solution)/shard_map/ppermute | solution.py:363
  2.7 0.0 collective-permute-start.1
  2.8 5.1 %collective-permute-done.got_a = f32[3,8,8,256]{3,2,1,0:T(8,128)S(1)} collective-permute-done((f32[3,8,8,256]{3,2,1,0:T(8,128)S(1)}, f32[3,8,8,256]{3,2,1,0:T(8,128)S(1)}, u32[]{:S(2)}, u32[]{:S(2)}) %collective-permute-start) | collective-permute-done | bytes 196640 | tf_op jit(solution)/shard_map/ppermute | solution.py:363
  7.8 1.3 %collective-permute-done.1.got_b = f32[3,8,8,256]{3,2,1,0:T(8,128)S(1)} collective-permute-done((f32[3,8,8,256]{3,2,1,0:T(8,128)S(1)}, f32[3,8,8,256]{3,2,1,0:T(8,128)S(1)}, u32[]{:S(2)}, u32[]{:S(2)}) %collective-permute-start.1) | collective-permute-done | bytes 196640 | tf_op jit(solution)/shard_map/ppermute | solution.py:363
  9.1 0.2 %pack_columns.1 = (f32[2,1,8,8,128]{4,3,2,1,0:T(8,128)S(1)}, f32[2,3,8,8,256]{4,3,2,1,0:T(8,128)S(1)}) custom-call(f32[3,8,16,256]{3,2,1,0:T(8,128)S(1)} %pad_maximum_fusion.own.refs_0_, f32[3,8,8,256]{3,2,1,0:T(8,128)S(1)} %collective-permute-done.got_a, f32[3,8,8,256]{3,2,1,0:T(8,128)S(1)} %collective-permute-done.1.got_b), custom_call_target="tpu_custom_call" | custom-call | tf_op jit(solution)/shard_map/pack_columns/pallas_call | solution.py:383
  9.4 0.1 collective-permute-start.2
  9.4 0.5 %collective-permute-start.3 = (f32[3,8,16,256]{3,2,1,0:T(8,128)S(1)}, f32[3,8,16,256]{3,2,1,0:T(8,128)S(1)}, u32[]{:S(2)}, u32[]{:S(2)}) collective-permute-start(f32[3,8,16,256]{3,2,1,0:T(8,128)S(1)} %pad_maximum_fusion.own.refs_0_), channel_id=1, source_target_pairs={{0,4},{4,0},{1,5},{5,1},{2,6},{6,2},{3,7},{7,3},{8,12},{12,8},{9,1... | collective-permute-start | bytes 1179656 | tf_op jit(solution)/shard_map/ppermute | solution.py:363
  9.9 0.7 %collective-permute-done.2 = f32[2,1,8,8,128]{4,3,2,1,0:T(8,128)S(1)} collective-permute-done((f32[2,1,8,8,128]{4,3,2,1,0:T(8,128)S(1)}, f32[2,1,8,8,128]{4,3,2,1,0:T(8,128)S(1)}, u32[]{:S(2)}, u32[]{:S(2)}) %collective-permute-start.2) | collective-permute-done | bytes 65568 | tf_op jit(solution)/shard_map/ppermute | solution.py:363
  10.7 0.2 %collective-permute-start.4 = (f32[2,3,8,8,256]{4,3,2,1,0:T(8,128)S(1)}, f32[2,3,8,8,256]{4,3,2,1,0:T(8,128)S(1)}, u32[]{:S(2)}, u32[]{:S(2)}) collective-permute-start(f32[2,3,8,8,256]{4,3,2,1,0:T(8,128)S(1)} %get-tuple-element.21.refs_1_), channel_id=1, source_target_pairs={{0,4},{4,0},{1,5},{5,1},{2,6},{6,2},{3,7},{7,3},{8,12},{12,8},{9,1... | collective-permute-start | bytes 1179656 | tf_op jit(solution)/shard_map/ppermute | solution.py:363
  10.9 0.6 %collective-permute-start.6 = (f32[1,16,8,128]{3,2,1,0:T(8,128)S(1)}, f32[1,16,8,128]{3,2,1,0:T(8,128)S(1)}, u32[]{:S(2)}, u32[]{:S(2)}) collective-permute-start(f32[1,16,8,128]{3,2,1,0:T(8,128)S(1)} %get-tuple-element.29), channel_id=1, source_target_pairs={{0,8},{4,12},{16,24},{20,28},{8,0},{12,4},{24,16},{28,20},{1,9},{5... | collective-permute-start | bytes 196616 | tf_op jit(solution)/shard_map/ppermute | solution.py:363
  11.5 2.4 %collective-permute-start.5 = (f32[1,16,8,128]{3,2,1,0:T(8,128)S(1)}, f32[1,16,8,128]{3,2,1,0:T(8,128)S(1)}, u32[]{:S(2)}, u32[]{:S(2)}) collective-permute-start(f32[1,16,8,128]{3,2,1,0:T(8,128)S(1)} %get-tuple-element.30), channel_id=1, source_target_pairs={{8,16},{12,20},{0,4},{24,28},{16,8},{20,12},{4,0},{28,24},{9,17},{... | collective-permute-start | bytes 196616 | tf_op jit(solution)/shard_map/ppermute | solution.py:363
  14.0 0.0 collective-permute-done.3.refs_2_
  14.0 0.0 collective-permute-done.4.refs_3_
  14.0 2.5 %interior.1 = (f32[8,16,256]{2,1,0:T(8,128)S(1)}, f32[3,18,32,128]{3,2,1,0:T(8,128)S(1)}) custom-call(f32[3,8,16,256]{3,2,1,0:T(8,128)S(1)} %pad_maximum_fusion.own.refs_0_, f32[2,3,8,8,256]{4,3,2,1,0:T(8,128)S(1)} %get-tuple-element.21.refs_1_, f32[3,8,16,256]{3,2,1,0:T(8,128)S(1)} %collective-permute-done.3.refs_2_, ...), custom_call_target="tpu_custom_call" | custom-call | flops 20000000 | bytes 20000000 | tf_op jit(solution)/shard_map/interior/pallas_call | solution.py:401
  16.5 0.0 collective-permute-done.6.got_a
  16.5 1.2 %collective-permute-done.5.got_b = f32[1,16,8,128]{3,2,1,0:T(8,128)S(1)} collective-permute-done((f32[1,16,8,128]{3,2,1,0:T(8,128)S(1)}, f32[1,16,8,128]{3,2,1,0:T(8,128)S(1)}, u32[]{:S(2)}, u32[]{:S(2)}) %collective-permute-start.5) | collective-permute-done | bytes 65568 | tf_op jit(solution)/shard_map/ppermute | solution.py:363
  17.7 2.8 %edges.1 = f32[8,16,256]{2,1,0:T(8,128)} custom-call(f32[3,18,32,128]{3,2,1,0:T(8,128)S(1)} %get-tuple-element.25.ends, f32[8,16,256]{2,1,0:T(8,128)S(1)} %get-tuple-element.26.inside, f32[1,16,8,128]{3,2,1,0:T(8,128)S(1)} %collective-permute-done.6.got_a, f32[1,16,8,128]{3,2,1,0:T(8,128)S(1)} %collective-permute-done.5.got_b), custom_call_target="tpu_custom_call" | custom-call | tf_op jit(solution)/shard_map/edges/pallas_call | solution.py:410
  (3 shorter events, 0.1 us)
Async XLA Ops:
  1.1 6.7 %collective-permute-start = (f32[3,8,8,256]{3,2,1,0:T(8,128)S(1)}, f32[3,8,8,256]{3,2,1,0:T(8,128)S(1)}, u32[]{:S(2)}, u32[]{:S(2)}) collective-permute-start(f32[3,8,8,256]{3,2,1,0:T(8,128)S(1)} %get-tuple-element.17), channel_id=1, source_target_pairs={{0,1},{4,5},{2,3},{6,7},{1,0},{5,4},{3,2},{7,6},{8,9},{12,13},{10,... | collective-permute-start | bytes 589832 | tf_op jit(solution)/shard_map/ppermute | solution.py:363
  2.7 6.4 %collective-permute-start.1 = (f32[3,8,8,256]{3,2,1,0:T(8,128)S(1)}, f32[3,8,8,256]{3,2,1,0:T(8,128)S(1)}, u32[]{:S(2)}, u32[]{:S(2)}) collective-permute-start(f32[3,8,8,256]{3,2,1,0:T(8,128)S(1)} %get-tuple-element.18), channel_id=1, source_target_pairs={{1,2},{5,6},{0,4},{3,7},{2,1},{6,5},{4,0},{7,3},{9,10},{13,14},{8,... | collective-permute-start | bytes 589832 | tf_op jit(solution)/shard_map/ppermute | solution.py:363
  9.4 1.3 %collective-permute-start.2 = (f32[2,1,8,8,128]{4,3,2,1,0:T(8,128)S(1)}, f32[2,1,8,8,128]{4,3,2,1,0:T(8,128)S(1)}, u32[]{:S(2)}, u32[]{:S(2)}) collective-permute-start(f32[2,1,8,8,128]{4,3,2,1,0:T(8,128)S(1)} %get-tuple-element.19), channel_id=1, source_target_pairs={{0,4},{4,0},{1,5},{5,1},{2,6},{6,2},{3,7},{7,3},{8,12},{12,8},{9,1... | collective-permute-start | bytes 196616 | tf_op jit(solution)/shard_map/ppermute | solution.py:363
  9.4 4.5 %collective-permute-start.3 = (f32[3,8,16,256]{3,2,1,0:T(8,128)S(1)}, f32[3,8,16,256]{3,2,1,0:T(8,128)S(1)}, u32[]{:S(2)}, u32[]{:S(2)}) collective-permute-start(f32[3,8,16,256]{3,2,1,0:T(8,128)S(1)} %pad_maximum_fusion.own.refs_0_), channel_id=1, source_target_pairs={{0,4},{4,0},{1,5},{5,1},{2,6},{6,2},{3,7},{7,3},{8,12},{12,8},{9,1... | collective-permute-start | bytes 1179656 | tf_op jit(solution)/shard_map/ppermute | solution.py:363
  10.7 3.3 %collective-permute-start.4 = (f32[2,3,8,8,256]{4,3,2,1,0:T(8,128)S(1)}, f32[2,3,8,8,256]{4,3,2,1,0:T(8,128)S(1)}, u32[]{:S(2)}, u32[]{:S(2)}) collective-permute-start(f32[2,3,8,8,256]{4,3,2,1,0:T(8,128)S(1)} %get-tuple-element.21.refs_1_), channel_id=1, source_target_pairs={{0,4},{4,0},{1,5},{5,1},{2,6},{6,2},{3,7},{7,3},{8,12},{12,8},{9,1... | collective-permute-start | bytes 1179656 | tf_op jit(solution)/shard_map/ppermute | solution.py:363
  10.9 5.5 %collective-permute-start.6 = (f32[1,16,8,128]{3,2,1,0:T(8,128)S(1)}, f32[1,16,8,128]{3,2,1,0:T(8,128)S(1)}, u32[]{:S(2)}, u32[]{:S(2)}) collective-permute-start(f32[1,16,8,128]{3,2,1,0:T(8,128)S(1)} %get-tuple-element.29), channel_id=1, source_target_pairs={{0,8},{4,12},{16,24},{20,28},{8,0},{12,4},{24,16},{28,20},{1,9},{5... | collective-permute-start | bytes 196616 | tf_op jit(solution)/shard_map/ppermute | solution.py:363
  11.5 6.2 %collective-permute-start.5 = (f32[1,16,8,128]{3,2,1,0:T(8,128)S(1)}, f32[1,16,8,128]{3,2,1,0:T(8,128)S(1)}, u32[]{:S(2)}, u32[]{:S(2)}) collective-permute-start(f32[1,16,8,128]{3,2,1,0:T(8,128)S(1)} %get-tuple-element.30), channel_id=1, source_target_pairs={{8,16},{12,20},{0,4},{24,28},{16,8},{20,12},{4,0},{28,24},{9,17},{... | collective-permute-start | bytes 196616 | tf_op jit(solution)/shard_map/ppermute | solution.py:363

commit v7 on v6

--- a/solution.py
+++ b/solution.py
@@ -57,15 +57,34 @@
     return lax.rem(lax.axis_index(axis), 2)
 
 
-def pack_rows(own, first, second):
+def fetch(copies, sems):
+    copies = [pltpu.make_async_copy(src, dst, sems.at[i]) for i, (src, dst) in enumerate(copies)]
+    for copy in copies:
+        copy.start()
+    for copy in copies:
+        copy.wait()
+
+
+def pack_rows(s, c, f, first, second, sems):
     odd = is_odd("gy")
-    last = own.shape[2] - HALO
-    first[...] = own[:, :, pl.ds(pl.multiple_of((1 - odd) * last, 8), HALO), :]
-    second[...] = own[:, :, pl.ds(pl.multiple_of(odd * last, 8), HALO), :]
-
-
-def slots(rows):
-    return [(a, g, a * (rows // 8) + g) for a in range(3) for g in range(rows // 8)]
+    last = s.shape[1] - HALO
+    rows = [pl.ds(pl.multiple_of(at * last, 8), HALO) for at in (1 - odd, odd)]
+    fetch(
+        [(ref.at[:, part, :], dst.at[a]) for part, dst in zip(rows, (first, second)) for a, ref in enumerate((s, c, f))],
+        sems,
+    )
+
+
+def pack_block(s, c, f, own, sems):
+    fetch([(ref, own.at[a]) for a, ref in enumerate((s, c, f))], sems)
+
+
+def head_lane(a, g):
+    return 16 * a + LANES // 2 * (g % 2) + 8 * (g // 2)
+
+
+def tail_lane(a, g):
+    return 16 * a + LANES // 2 * (g % 2) + 8 * (1 - g // 2)
 
 
 def pack_columns(own, got_a, got_b, strips, rim):
@@ -79,22 +98,21 @@
             from_a, from_b = got_a[a, p], got_b[a, p]
             rim[0, a, p] = jnp.where(first_y, 0.0, jnp.where(odd_y == 1, from_a, from_b))
             rim[1, a, p] = jnp.where(last_y, 0.0, jnp.where(odd_y == 1, from_b, from_a))
-        heads = [jnp.zeros((8, LANES), jnp.float32) for _ in range(strips.shape[1])]
-        tails = list(heads)
-        for a, g, slot in slots(8 * groups):
-            t, at = slot // 16, 8 * (slot % 16)
-            if g == 0 or g == groups - 1:
-                rows = rim[min(g, 1), a, p]
-            else:
-                rows = own[a, p, 8 * g - 8 : 8 * g, :]
-            head = pltpu.roll(rows[:, 0:LANES], at, 1)
-            tail = pltpu.roll(rows[:, width - LANES : width], (at + LANES // 2) % LANES, 1)
-            far = (at + LANES // 2 - HALO) % LANES
-            heads[t] = jnp.where((lane >= at) & (lane < at + HALO), head, heads[t])
-            tails[t] = jnp.where((lane >= far) & (lane < far + HALO), tail, tails[t])
-        for t, (head, tail) in enumerate(zip(heads, tails)):
-            strips[0, t, p] = jnp.where(odd_z == 1, head, tail)
-            strips[1, t, p] = jnp.where(odd_z == 1, tail, head)
+        head = tail = jnp.zeros((8, LANES), jnp.float32)
+        for a in range(3):
+            for g in range(groups):
+                if g == 0 or g == groups - 1:
+                    rows = rim[min(g, 1), a, p]
+                else:
+                    rows = own[a, p, 8 * g - 8 : 8 * g, :]
+                to = head_lane(a, g)
+                moved = pltpu.roll(rows[:, 0:LANES], to, 1)
+                head = jnp.where((lane >= to) & (lane < to + HALO), moved, head)
+                to = tail_lane(a, g)
+                moved = pltpu.roll(rows[:, width - LANES : width], (to + HALO) % LANES, 1)
+                tail = jnp.where((lane >= to) & (lane < to + HALO), moved, tail)
+        strips[0, p] = jnp.where(odd_z == 1, head, tail)
+        strips[1, p] = jnp.where(odd_z == 1, tail, head)
 
 
 def shifts(parts, step):
@@ -137,8 +155,12 @@
     for ref in (q, cq, err, sum8):
         store(ref, 0, [zero] * ref.shape[1])
 
+    even_row = lax.rem(lax.broadcasted_iota(jnp.int32, (rows, lanes), 0), 2) == 0
+    even_lane = lax.rem(lax.broadcasted_iota(jnp.int32, (rows, lanes), 1), 2) == 0
+
     def gather(v):
-        t = v[0] + v[1] if parts == 2 else v[0] + ahead(v[0], 1)
+        other = v[1] if parts == 2 else jnp.where(even_lane, ahead(v[0], 1), behind(v[0], 1))
+        t = v[0] + other
         return [t + ahead(t, 0)]
 
     for k in reach(HALO):
@@ -163,9 +185,6 @@
         for ref, v in zip((cwx, cwy, cwz, cvy, cvz, None, cinv), weights(sum8, k, coarse)):
             if ref is not None:
                 store(ref, k, v)
-
-    even_row = lax.rem(lax.broadcasted_iota(jnp.int32, (rows, lanes), 0), 2) == 0
-    even_lane = lax.rem(lax.broadcasted_iota(jnp.int32, (rows, lanes), 1), 2) == 0
 
     def spread(v, p, refs, level):
         x, y, z, yb, zb = refs
@@ -199,8 +218,6 @@
 
         for k in reach(halo):
             (c,) = smooth(cq, k, coarse_around, cinv, coarse)
-            if parts == 1:
-                c = jnp.where(even_lane, c, behind(c, 1))
             c = jnp.where(even_row, c, behind(c, 0))
             for p in (2 * k - 1, 2 * k):
                 e = [u + c for u in smooth(q, p, around, inv, fine)]
@@ -220,24 +237,16 @@
     odd_x = is_odd("gx")
     own_at, _ = layout(reflect, depth)
 
-    def own_plane(p, carry):
-        to = jnp.where(odd_x == 1, depth - 1 - p, p) if reflect else p
-        place(None, p, own_at + to)
-        return carry
-
-    lax.fori_loop(0, depth, own_plane, 0, unroll=True)
-
-    def near_plane(p, carry):
+    for p in range(depth):
+        place(None, jnp.where(odd_x == 1, depth - 1 - p, p) if reflect else p, own_at + p)
+    for p in range(HALO):
         if reflect:
             place(0, jnp.where(odd_x == 1, depth - 1 - p, p), own_at + depth + p)
-            return carry
+            continue
         for i in range(2):
             above = odd_x == i
             at = jnp.where(above, p, depth - HALO + p)
             place(i, at, jnp.where(above, own_at + depth + p, 1 + p))
-        return carry
-
-    lax.fori_loop(0, HALO, near_plane, 0, unroll=True)
 
 
 def out_plane(reflect, depth, p):
@@ -251,6 +260,15 @@
     lane = lax.broadcasted_iota(jnp.int32, (width, 2 * lanes), 1)
     wanted = jnp.where(lane < lanes, 2 * lane, 2 * (lane - lanes) + 1)
     return jnp.where((column == wanted) & (wanted < width), 1.0, 0.0)
+
+
+def ending(width):
+    column = lax.broadcasted_iota(jnp.int32, (width, 2 * LANES), 0)
+    lane = lax.broadcasted_iota(jnp.int32, (width, 2 * LANES), 1)
+    lane = jnp.where(lane < LANES, lane, lane - LANES - LANES // 2)
+    last = (lane >= 8) & (lane < 24) & (column == lane + width - 24)
+    first = (lane >= 40) & (lane < 56) & (column == lane - 40)
+    return jnp.where(last | first, 1.0, 0.0)
 
 
 def rearranged(v, matrix):
@@ -273,7 +291,6 @@
     _, depth, inner, width = own.shape
     rows = inner + 2 * HALO
     lanes = cells[0].shape[3]
-    lane = lax.broadcasted_iota(jnp.int32, (rows, LANES), 1)
 
     def place(i, p_from, p_to):
         block, halo = (own, rim) if i is None else (near[i], near_rim[i])
@@ -282,22 +299,20 @@
             tile[0:HALO, :] = halo[0, a, p_from]
             tile[HALO : HALO + inner, :] = block[a, p_from]
             tile[HALO + inner : rows, :] = halo[1, a, p_from]
-            head = pltpu.roll(tile[:, 0:LANES], LANES // 2, 1)
-            tail = tile[:, width - LANES : width]
-            end = jnp.where((lane >= LANES // 2) & (lane < LANES // 2 + 2 * HALO), head, 0.0)
-            ends[a, p_to] = jnp.where(lane >= LANES - 2 * HALO, tail, end)
 
     own_at, total = layout(reflect, depth)
     for a in range(3):
         for p in (0, total - 1):
             whole[a, p] = jnp.zeros((rows, width), jnp.float32)
-            ends[a, p] = jnp.zeros((rows, LANES), jnp.float32)
     each_plane(reflect, depth, place)
     apart = parting(width, lanes)
+    target = jnp.concatenate([apart, ending(width)], 1)
     for a in range(3):
-        parts = rearranged(whole[a].reshape(total * rows, width), apart)
+        parts = rearranged(whole[a].reshape(total * rows, width), target).reshape(total, rows, -1)
         for i in range(2):
-            cells[a][:, i] = parts[:, i * lanes : (i + 1) * lanes].reshape(total, rows, lanes)
+            cells[a][:, i] = parts[:, :, i * lanes : (i + 1) * lanes]
+        low = parts[:, 0 : rows - 8, 2 * lanes : 2 * lanes + LANES]
+        ends[a] = low + parts[:, 8:rows, 2 * lanes + LANES :]
 
     def out(p, v):
         for i in range(2):
@@ -312,11 +327,11 @@
 
 def edges(reflect, ends, inside, got_a, got_b, result, *cells):
     depth, inner, width = inside.shape
-    rows = inner + 2 * HALO
+    groups = ends.shape[2] // 8
     odd_z = is_odd("grp")
     first_z, last_z = beyond("grp")
     lane = lax.broadcasted_iota(jnp.int32, (8, LANES), 1)
-    in_halo = (lane < HALO) | ((lane >= LANES // 2 - HALO) & (lane < LANES // 2))
+    half = LANES // 2
     own_at, total = layout(reflect, depth)
     for p in (0, total - 1):
         for a in range(3):
@@ -324,35 +339,43 @@
 
     def place(i, p_from, p_to):
         at_plane = p_from if i is None else (i + 1) * depth + p_from
-        for t in range(got_a.shape[0]):
-            va, vb = got_a[t, at_plane], got_b[t, at_plane]
-            upper = jnp.where(last_z, 0.0, jnp.where(odd_z == 1, vb, va))
-            lower = jnp.where(first_z, 0.0, jnp.where(odd_z == 1, va, vb))
-            for a, g, slot in slots(rows):
-                if slot // 16 == t:
-                    at = 8 * (slot % 16)
-                    both = jnp.where((lane >= at) & (lane < at + HALO), upper, lower)
-                    both = pltpu.roll(both, (LANES - at) % LANES, 1)
-                    part = slice(8 * g, 8 * g + 8)
-                    cells[a][p_to, 0, part, :] = jnp.where(in_halo, both, ends[a, p_to, part, :])
+        va, vb = got_a[at_plane], got_b[at_plane]
+        right = jnp.where(last_z, 0.0, jnp.where(odd_z == 1, vb, va))
+        left = jnp.where(first_z, 0.0, jnp.where(odd_z == 1, va, vb))
+        side = lax.rem(lane, 16) < 8
+        lower = jnp.where(side, right, left)
+        upper = jnp.where(side, pltpu.roll(right, LANES - 8, 1), pltpu.roll(left, 8, 1))
+        middle = jnp.where(lane < half, upper, lower)
+        for a in range(3):
+            for t, (groups_of, shift) in enumerate(((lower, 24), (middle, 24 + half), (upper, 24))):
+                moved = pltpu.roll(groups_of, (shift - 16 * a) % LANES, 1)
+                here = lax.rem(lane, half)
+                part = slice(8 * t, 8 * t + 8)
+                cells[a][p_to, 0, part, :] = jnp.where((here >= 24) & (here < 40), moved, ends[a, p_to, part, :])
 
     each_plane(reflect, depth, place)
-    result[...] = inside[...]
-    wide = lax.broadcasted_iota(jnp.int32, (inner, LANES), 1)
 
     def out(p, v):
         at = out_plane(reflect, depth, p)
-        v = v[0][HALO : rows - HALO, :]
-        head = pltpu.roll(v, LANES // 2, 1)
-        result[at, :, 0:LANES] = jnp.where(wide < HALO, head, result[at, :, 0:LANES])
-        tail = result[at, :, width - LANES : width]
-        result[at, :, width - LANES : width] = jnp.where(wide >= LANES - HALO, v, tail)
+        v = v[0][8:16]
+        for i in range(2):
+            part = slice(8 * i, 8 * i + 8)
+            head = pltpu.roll(v, (LANES - 40 - half * i) % LANES, 1)
+            tail = pltpu.roll(v, (LANES - 24 - half * i) % LANES, 1)
+            for c in range(0, width, LANES):
+                tile = inside[at, part, c : c + LANES]
+                if c == 0:
+                    tile = jnp.where(lane < HALO, head, tile)
+                if c == width - LANES:
+                    tile = jnp.where(lane >= LANES - HALO, tail, tile)
+                result[at, part, c : c + LANES] = tile
 
     solve(cells, own_at, depth, out)
 
 
 def shards(sizes, source_term, conductivity, initial_field):
     depth, inner, width = source_term.shape
+    assert inner == 16 and depth >= HALO and depth % 2 == 0 and width % LANES == 0
     rows = inner + 2 * HALO
     f32 = jnp.float32
     params = pltpu.CompilerParams(vmem_limit_bytes=48 * 1024 * 1024)
@@ -363,7 +386,7 @@
         found = [lax.ppermute(v, over, pairs) for v, pairs in reversed(list(zip(values, rounds)))]
         return found[::-1] + [jnp.zeros_like(v) for v in values[len(found) :]]
 
-    def work(parts, lanes):
+    def work(parts, rows, lanes):
         total = layout(reflect, depth)[1]
         fine = pltpu.VMEM((total, parts, rows, lanes), f32)
         coarse = pltpu.VMEM((total // 2 + 1, 1, rows, lanes), f32)
@@ -372,24 +395,29 @@
     reflect = sizes["gx"] == 2
     n_x = 1 if reflect else 2
     face = jax.ShapeDtypeStruct((3, depth, HALO, width), f32)
-    own = jnp.stack(args)
+    args = [pltpu.with_memory_space_constraint(v, pltpu.HBM) for v in args]
+    hbm = [pl.BlockSpec(memory_space=pltpu.HBM)] * 3
     msgs = pl.pallas_call(
-        pack_rows, out_shape=(face, face), in_specs=[VMEM], out_specs=(VMEM, VMEM),
-        compiler_params=params, name="pack_rows",
-    )(own)
+        pack_rows, out_shape=(face, face), in_specs=hbm, out_specs=(VMEM, VMEM),
+        scratch_shapes=[pltpu.SemaphoreType.DMA((6,))], compiler_params=params, name="pack_rows",
+    )(*args)
+    own = pl.pallas_call(
+        pack_block, out_shape=jax.ShapeDtypeStruct((3, depth, inner, width), f32), in_specs=hbm, out_specs=VMEM,
+        scratch_shapes=[pltpu.SemaphoreType.DMA((3,))], compiler_params=params, name="pack_block",
+        cost_estimate=pl.CostEstimate(flops=0, bytes_accessed=2_000_000, transcendentals=0),
+    )(*args)
     got = exchange(msgs, "gy")
     near = exchange([own] * n_x, "gx")
-    n_tiles = -(-3 * (rows // 8) // 16)
     strips, rim = pl.pallas_call(
         pack_columns,
         out_shape=(
-            jax.ShapeDtypeStruct((2, n_tiles, depth, 8, LANES), f32),
+            jax.ShapeDtypeStruct((2, depth, 8, LANES), f32),
             jax.ShapeDtypeStruct((2, 3, depth, HALO, width), f32),
         ),
         in_specs=[VMEM] * 3, out_specs=(VMEM, VMEM),
         compiler_params=params, name="pack_columns",
     )(own, *got)
-    strips = jnp.concatenate([strips] + exchange([strips] * n_x, "gx"), axis=2)
+    strips = jnp.concatenate([strips] + exchange([strips] * n_x, "gx"), axis=1)
     strips, rim = lax.optimization_barrier((strips, rim))
     near_rim = exchange([rim] * n_x, "gx")
     strips = exchange([strips[0], strips[1]], "grp")
@@ -400,8 +428,8 @@
     apart = [pltpu.VMEM((3, total, rows, width), f32), pltpu.VMEM((depth, inner, 2 * lanes), f32)]
     inside, ends = pl.pallas_call(
         functools.partial(interior, reflect, n_x),
-        out_shape=(block, jax.ShapeDtypeStruct((3, total, rows, LANES), f32)),
-        in_specs=[VMEM] * (2 + 2 * n_x), out_specs=(VMEM, VMEM), scratch_shapes=apart + work(2, lanes),
+        out_shape=(block, jax.ShapeDtypeStruct((3, total, rows - 8, LANES), f32)),
+        in_specs=[VMEM] * (2 + 2 * n_x), out_specs=(VMEM, VMEM), scratch_shapes=apart + work(2, rows, lanes),
         compiler_params=params, name="interior",
         cost_estimate=pl.CostEstimate(flops=20_000_000, bytes_accessed=20_000_000, transcendentals=0),
     )(own, rim, *near, *near_rim)
@@ -410,7 +438,7 @@
     return pl.pallas_call(
         functools.partial(edges, reflect),
         out_shape=block,
-        in_specs=[VMEM] * 4, out_specs=VMEM, scratch_shapes=work(1, LANES),
+        in_specs=[VMEM] * 4, out_specs=VMEM, scratch_shapes=work(1, rows - 8, LANES),
         compiler_params=params, name="edges",
     )(ends, inside, *strips)
 

time: 20.6 us -> 20.6 us (level)
  Pallas kernels: 5.53 us -> 7.94 us
  waiting for transfers between devices: 8.33 us -> 6.93 us
  other arithmetic: 1.07 us -> 0.01 us
    pallas_call x2 -> x3, Pallas kernels: 0.29 us -> 2.36 us  [the longest x1 1.06 us: shards(): pl.pallas_call(pack_block, out_shape=jax.ShapeDtypeStruct((3, depth, inne...]
    ppermute x7, waiting for transfers between devices: 8.33 us -> 6.93 us  [exchange(): lax.ppermute(v, over, pairs)]
    another operation x1 -> x0, other arithmetic: 1.06 us -> none  [shards(): own = jnp.stack(args)]
    pallas_call x1, Pallas kernels: 2.48 us -> 2.82 us  [shards(): pl.pallas_call(functools.partial(interior, reflect, n_x), out_shape=(bloc...]
  transfers between devices with their start and end apart: 7 -> 7, of which waited for: 4 -> 4; matrix products, arithmetic and copies ran while one was open for 0% -> 0% of each run, Pallas kernels for 12% -> 19%
where the time goes in v7:
time: 20.6 us; the launch traced here: 20.4 us
  Pallas kernels  7.94 us (39%)
  waiting for transfers between devices  6.93 us (34%)
  starting transfers between devices  5.48 us (27%)
    ppermute x7, waiting for transfers between devices, exchange(): lax.ppermute(v, over, pairs)  6.93 us
    ppermute x7, starting transfers between devices, exchange(): lax.ppermute(v, over, pairs)  5.48 us
    pallas_call x1, Pallas kernels, shards(): pl.pallas_call(functools.partial(interior, reflect, n_x), out_shape=(bloc...  2.82 us
    pallas_call x1, Pallas kernels, shards(): pl.pallas_call(functools.partial(edges, reflect), out_shape=block, in_spe...  2.75 us
    pallas_call x1, Pallas kernels, shards(): pl.pallas_call(pack_block, out_shape=jax.ShapeDtypeStruct((3, depth, inne...  1.06 us
    pallas_call x1, Pallas kernels, shards(): pl.pallas_call(pack_rows, out_shape=(face, face), in_specs=hbm, out_specs...  1.05 us
  transfers between devices with their start and end apart: 7, of which 4 were waited for; matrix products, arithmetic and copies ran while one was open for 0% of the time, Pallas kernels for 19%

profile of v7, /device:TPU:18, one launch (start us, length us, event | category | flops | bytes accessed | tf_op | source)
XLA Modules:
  0.0 20.4 jit_solution(11984114951011700496)
XLA Ops:
  0.0 1.0 %pack_rows.1 = (f32[3,8,8,256]{3,2,1,0:T(8,128)S(1)}, f32[3,8,8,256]{3,2,1,0:T(8,128)S(1)}) custom-call(f32[8,16,256]{2,1,0:T(8,128)} %s.3, f32[8,16,256]{2,1,0:T(8,128)} %c.3, f32[8,16,256]{2,1,0:T(8,128)} %f.3), custom_call_target="tpu_custom_call" | custom-call | tf_op jit(solution)/shard_map/pack_rows/pallas_call | solution.py:400
  1.1 1.6 %collective-permute-start = (f32[3,8,8,256]{3,2,1,0:T(8,128)S(1)}, f32[3,8,8,256]{3,2,1,0:T(8,128)S(1)}, u32[]{:S(2)}, u32[]{:S(2)}) collective-permute-start(f32[3,8,8,256]{3,2,1,0:T(8,128)S(1)} %get-tuple-element.17), channel_id=1, source_target_pairs={{0,1},{4,5},{2,3},{6,7},{1,0},{5,4},{3,2},{7,6},{8,9},{12,13},{10,... | collective-permute-start | bytes 589832 | tf_op jit(solution)/shard_map/ppermute | solution.py:386
  2.7 0.0 collective-permute-start.1
  2.7 1.1 %pack_block.1.own.refs_0_ = f32[3,8,16,256]{3,2,1,0:T(8,128)S(1)} custom-call(f32[8,16,256]{2,1,0:T(8,128)} %s.3, f32[8,16,256]{2,1,0:T(8,128)} %c.3, f32[8,16,256]{2,1,0:T(8,128)} %f.3), custom_call_target="tpu_custom_call" | custom-call | bytes 2000000 | tf_op jit(solution)/shard_map/pack_block/pallas_call | solution.py:404
  3.8 4.0 %collective-permute-done.got_a = f32[3,8,8,256]{3,2,1,0:T(8,128)S(1)} collective-permute-done((f32[3,8,8,256]{3,2,1,0:T(8,128)S(1)}, f32[3,8,8,256]{3,2,1,0:T(8,128)S(1)}, u32[]{:S(2)}, u32[]{:S(2)}) %collective-permute-start) | collective-permute-done | bytes 196640 | tf_op jit(solution)/shard_map/ppermute | solution.py:386
  7.8 1.3 %collective-permute-done.1.got_b = f32[3,8,8,256]{3,2,1,0:T(8,128)S(1)} collective-permute-done((f32[3,8,8,256]{3,2,1,0:T(8,128)S(1)}, f32[3,8,8,256]{3,2,1,0:T(8,128)S(1)}, u32[]{:S(2)}, u32[]{:S(2)}) %collective-permute-start.1) | collective-permute-done | bytes 196640 | tf_op jit(solution)/shard_map/ppermute | solution.py:386
  9.1 0.3 %pack_columns.1 = (f32[2,8,8,128]{3,2,1,0:T(8,128)S(1)}, f32[2,3,8,8,256]{4,3,2,1,0:T(8,128)S(1)}) custom-call(f32[3,8,16,256]{3,2,1,0:T(8,128)S(1)} %pack_block.1.own.refs_0_, f32[3,8,8,256]{3,2,1,0:T(8,128)S(1)} %collective-permute-done.got_a, f32[3,8,8,256]{3,2,1,0:T(8,128)S(1)} %collective-permute-done.1.got_b), custom_call_target="tpu_custom_call" | custom-call | tf_op jit(solution)/shard_map/pack_columns/pallas_call | solution.py:411
  9.3 0.1 collective-permute-start.2
  9.4 0.5 %collective-permute-start.3 = (f32[3,8,16,256]{3,2,1,0:T(8,128)S(1)}, f32[3,8,16,256]{3,2,1,0:T(8,128)S(1)}, u32[]{:S(2)}, u32[]{:S(2)}) collective-permute-start(f32[3,8,16,256]{3,2,1,0:T(8,128)S(1)} %pack_block.1.own.refs_0_), channel_id=1, source_target_pairs={{0,4},{4,0},{1,5},{5,1},{2,6},{6,2},{3,7},{7,3},{8,12},{12,8},{9,1... | collective-permute-start | bytes 1179656 | tf_op jit(solution)/shard_map/ppermute | solution.py:386
  9.9 0.7 %collective-permute-done.2 = f32[2,8,8,128]{3,2,1,0:T(8,128)S(1)} collective-permute-done((f32[2,8,8,128]{3,2,1,0:T(8,128)S(1)}, f32[2,8,8,128]{3,2,1,0:T(8,128)S(1)}, u32[]{:S(2)}, u32[]{:S(2)}) %collective-permute-start.2) | collective-permute-done | bytes 65568 | tf_op jit(solution)/shard_map/ppermute | solution.py:386
  10.7 0.2 %collective-permute-start.4 = (f32[2,3,8,8,256]{4,3,2,1,0:T(8,128)S(1)}, f32[2,3,8,8,256]{4,3,2,1,0:T(8,128)S(1)}, u32[]{:S(2)}, u32[]{:S(2)}) collective-permute-start(f32[2,3,8,8,256]{4,3,2,1,0:T(8,128)S(1)} %get-tuple-element.21.refs_1_), channel_id=1, source_target_pairs={{0,4},{4,0},{1,5},{5,1},{2,6},{6,2},{3,7},{7,3},{8,12},{12,8},{9,1... | collective-permute-start | bytes 1179656 | tf_op jit(solution)/shard_map/ppermute | solution.py:386
  10.9 0.6 %collective-permute-start.6 = (f32[16,8,128]{2,1,0:T(8,128)S(1)}, f32[16,8,128]{2,1,0:T(8,128)S(1)}, u32[]{:S(2)}, u32[]{:S(2)}) collective-permute-start(f32[16,8,128]{2,1,0:T(8,128)S(1)} %get-tuple-element.29), channel_id=1, source_target_pairs={{0,8},{4,12},{16,24},{20,28},{8,0},{12,4},{24,16},{28,20},{1,9},{5... | collective-permute-start | bytes 196616 | tf_op jit(solution)/shard_map/ppermute | solution.py:386
  11.5 2.4 %collective-permute-start.5 = (f32[16,8,128]{2,1,0:T(8,128)S(1)}, f32[16,8,128]{2,1,0:T(8,128)S(1)}, u32[]{:S(2)}, u32[]{:S(2)}) collective-permute-start(f32[16,8,128]{2,1,0:T(8,128)S(1)} %get-tuple-element.30), channel_id=1, source_target_pairs={{8,16},{12,20},{0,4},{24,28},{16,8},{20,12},{4,0},{28,24},{9,17},{... | collective-permute-start | bytes 196616 | tf_op jit(solution)/shard_map/ppermute | solution.py:386
  13.9 0.0 collective-permute-done.3.refs_2_
  13.9 0.0 collective-permute-done.4.refs_3_
  13.9 2.8 %interior.1 = (f32[8,16,256]{2,1,0:T(8,128)S(1)}, f32[3,18,24,128]{3,2,1,0:T(8,128)S(1)}) custom-call(f32[3,8,16,256]{3,2,1,0:T(8,128)S(1)} %pack_block.1.own.refs_0_, f32[2,3,8,8,256]{4,3,2,1,0:T(8,128)S(1)} %get-tuple-element.21.refs_1_, f32[3,8,16,256]{3,2,1,0:T(8,128)S(1)} %collective-permute-done.3.refs_2_, ...), custom_call_target="tpu_custom_call" | custom-call | flops 20000000 | bytes 20000000 | tf_op jit(solution)/shard_map/interior/pallas_call | solution.py:429
  16.8 0.0 collective-permute-done.6.got_a
  16.8 0.9 %collective-permute-done.5.got_b = f32[16,8,128]{2,1,0:T(8,128)S(1)} collective-permute-done((f32[16,8,128]{2,1,0:T(8,128)S(1)}, f32[16,8,128]{2,1,0:T(8,128)S(1)}, u32[]{:S(2)}, u32[]{:S(2)}) %collective-permute-start.5) | collective-permute-done | bytes 65568 | tf_op jit(solution)/shard_map/ppermute | solution.py:386
  17.7 2.8 %edges.1 = f32[8,16,256]{2,1,0:T(8,128)} custom-call(f32[3,18,24,128]{3,2,1,0:T(8,128)S(1)} %get-tuple-element.25.ends, f32[8,16,256]{2,1,0:T(8,128)S(1)} %get-tuple-element.26.inside, f32[16,8,128]{2,1,0:T(8,128)S(1)} %collective-permute-done.6.got_a, f32[16,8,128]{2,1,0:T(8,128)S(1)} %collective-permute-done.5.got_b), custom_call_target="tpu_custom_call" | custom-call | tf_op jit(solution)/shard_map/edges/pallas_call | solution.py:438
  (2 shorter events, 0.0 us)
Async XLA Ops:
  1.1 6.7 %collective-permute-start = (f32[3,8,8,256]{3,2,1,0:T(8,128)S(1)}, f32[3,8,8,256]{3,2,1,0:T(8,128)S(1)}, u32[]{:S(2)}, u32[]{:S(2)}) collective-permute-start(f32[3,8,8,256]{3,2,1,0:T(8,128)S(1)} %get-tuple-element.17), channel_id=1, source_target_pairs={{0,1},{4,5},{2,3},{6,7},{1,0},{5,4},{3,2},{7,6},{8,9},{12,13},{10,... | collective-permute-start | bytes 589832 | tf_op jit(solution)/shard_map/ppermute | solution.py:386
  2.7 6.4 %collective-permute-start.1 = (f32[3,8,8,256]{3,2,1,0:T(8,128)S(1)}, f32[3,8,8,256]{3,2,1,0:T(8,128)S(1)}, u32[]{:S(2)}, u32[]{:S(2)}) collective-permute-start(f32[3,8,8,256]{3,2,1,0:T(8,128)S(1)} %get-tuple-element.18), channel_id=1, source_target_pairs={{1,2},{5,6},{0,4},{3,7},{2,1},{6,5},{4,0},{7,3},{9,10},{13,14},{8,... | collective-permute-start | bytes 589832 | tf_op jit(solution)/shard_map/ppermute | solution.py:386
  9.3 1.3 %collective-permute-start.2 = (f32[2,8,8,128]{3,2,1,0:T(8,128)S(1)}, f32[2,8,8,128]{3,2,1,0:T(8,128)S(1)}, u32[]{:S(2)}, u32[]{:S(2)}) collective-permute-start(f32[2,8,8,128]{3,2,1,0:T(8,128)S(1)} %get-tuple-element.19), channel_id=1, source_target_pairs={{0,4},{4,0},{1,5},{5,1},{2,6},{6,2},{3,7},{7,3},{8,12},{12,8},{9,1... | collective-permute-start | bytes 196616 | tf_op jit(solution)/shard_map/ppermute | solution.py:386
  9.4 4.5 %collective-permute-start.3 = (f32[3,8,16,256]{3,2,1,0:T(8,128)S(1)}, f32[3,8,16,256]{3,2,1,0:T(8,128)S(1)}, u32[]{:S(2)}, u32[]{:S(2)}) collective-permute-start(f32[3,8,16,256]{3,2,1,0:T(8,128)S(1)} %pack_block.1.own.refs_0_), channel_id=1, source_target_pairs={{0,4},{4,0},{1,5},{5,1},{2,6},{6,2},{3,7},{7,3},{8,12},{12,8},{9,1... | collective-permute-start | bytes 1179656 | tf_op jit(solution)/shard_map/ppermute | solution.py:386
  10.7 3.3 %collective-permute-start.4 = (f32[2,3,8,8,256]{4,3,2,1,0:T(8,128)S(1)}, f32[2,3,8,8,256]{4,3,2,1,0:T(8,128)S(1)}, u32[]{:S(2)}, u32[]{:S(2)}) collective-permute-start(f32[2,3,8,8,256]{4,3,2,1,0:T(8,128)S(1)} %get-tuple-element.21.refs_1_), channel_id=1, source_target_pairs={{0,4},{4,0},{1,5},{5,1},{2,6},{6,2},{3,7},{7,3},{8,12},{12,8},{9,1... | collective-permute-start | bytes 1179656 | tf_op jit(solution)/shard_map/ppermute | solution.py:386
  10.9 5.9 %collective-permute-start.6 = (f32[16,8,128]{2,1,0:T(8,128)S(1)}, f32[16,8,128]{2,1,0:T(8,128)S(1)}, u32[]{:S(2)}, u32[]{:S(2)}) collective-permute-start(f32[16,8,128]{2,1,0:T(8,128)S(1)} %get-tuple-element.29), channel_id=1, source_target_pairs={{0,8},{4,12},{16,24},{20,28},{8,0},{12,4},{24,16},{28,20},{1,9},{5... | collective-permute-start | bytes 196616 | tf_op jit(solution)/shard_map/ppermute | solution.py:386
  11.5 6.2 %collective-permute-start.5 = (f32[16,8,128]{2,1,0:T(8,128)S(1)}, f32[16,8,128]{2,1,0:T(8,128)S(1)}, u32[]{:S(2)}, u32[]{:S(2)}) collective-permute-start(f32[16,8,128]{2,1,0:T(8,128)S(1)} %get-tuple-element.30), channel_id=1, source_target_pairs={{8,16},{12,20},{0,4},{24,28},{16,8},{20,12},{4,0},{28,24},{9,17},{... | collective-permute-start | bytes 196616 | tf_op jit(solution)/shard_map/ppermute | solution.py:386

commit v8 on v7

--- a/solution.py
+++ b/solution.py
@@ -57,26 +57,52 @@
     return lax.rem(lax.axis_index(axis), 2)
 
 
-def fetch(copies, sems):
-    copies = [pltpu.make_async_copy(src, dst, sems.at[i]) for i, (src, dst) in enumerate(copies)]
+def prepare(reflect, s, c, f, own, first, second, sems):
+    copies = [pltpu.make_async_copy(ref, own.at[a], sems.at[a]) for a, ref in enumerate((s, c, f))]
     for copy in copies:
         copy.start()
     for copy in copies:
         copy.wait()
-
-
-def pack_rows(s, c, f, first, second, sems):
+    _, depth, inner, width = own.shape
+    row = lax.broadcasted_iota(jnp.int32, (inner, width), 0)
+    column = lax.broadcasted_iota(jnp.int32, (inner, width), 1)
+    outer = jnp.where(is_odd("gx") == 1, depth - 1, 0)
+    for p in range(depth):
+        cond, field = own[1, p], own[2, p]
+
+        def flux(shift, axis):
+            return (cond + shift(cond, axis)) * (field - shift(field, axis))
+
+        total = jnp.where(row < inner - 1, flux(ahead, 0), 0.0) + jnp.where(row > 0, flux(behind, 0), 0.0)
+        total += jnp.where(column < width - 1, flux(ahead, 1), 0.0) + jnp.where(column > 0, flux(behind, 1), 0.0)
+        for other in (p - 1, p + 1):
+            if 0 <= other < depth:
+                total += (cond + own[1, other]) * (field - own[2, other])
+        if reflect and p in (0, depth - 1):
+            total += jnp.where(outer == p, cond * field, 0.0)
+        own[0, p] = 2.0 * own[0, p] - total
+
     odd = is_odd("gy")
-    last = s.shape[1] - HALO
-    rows = [pl.ds(pl.multiple_of(at * last, 8), HALO) for at in (1 - odd, odd)]
-    fetch(
-        [(ref.at[:, part, :], dst.at[a]) for part, dst in zip(rows, (first, second)) for a, ref in enumerate((s, c, f))],
-        sems,
-    )
-
-
-def pack_block(s, c, f, own, sems):
-    fetch([(ref, own.at[a]) for a, ref in enumerate((s, c, f))], sems)
+    row = lax.broadcasted_iota(jnp.int32, (HALO, width), 0)
+    lane = lax.broadcasted_iota(jnp.int32, (HALO, LANES), 1)
+    for message, high in ((first, odd == 0), (second, odd == 1)):
+        rows = pl.ds(pl.multiple_of(jnp.where(high, inner - HALO, 0), 8), HALO)
+        sides = jnp.zeros((HALO, LANES), jnp.float32)
+        for p in range(depth):
+            field = own[2, p, rows, :]
+            below = jnp.where(row == HALO - 1, pltpu.roll(field, HALO - 1, 0), own[0, p, rows, :])
+            above = jnp.where(row == 0, pltpu.roll(field, 1, 0), own[0, p, rows, :])
+            message[p] = jnp.where(high, above, below)
+            message[depth + p] = own[1, p, rows, :]
+            sides = jnp.where(lane == p, pltpu.roll(field[:, 0:LANES], p, 1), sides)
+            sides = jnp.where(lane == depth + p, pltpu.roll(field[:, width - LANES : width], depth + p + 1, 1), sides)
+        if reflect:
+            message[2 * depth] = own[2, depth - 1 - outer, rows, :]
+        else:
+            message[2 * depth] = own[2, 0, rows, :]
+            message[2 * depth + 1] = own[2, depth - 1, rows, :]
+        message[message.shape[0] - 1] = jnp.zeros((HALO, width), jnp.float32)
+        message[message.shape[0] - 1, :, 0:LANES] = sides
 
 
 def head_lane(a, g):
@@ -87,17 +113,40 @@
     return 16 * a + LANES // 2 * (g % 2) + 8 * (1 - g // 2)
 
 
-def pack_columns(own, got_a, got_b, strips, rim):
+def pack_columns(reflect, own, got_a, got_b, strips, rim):
     odd_y, odd_z = is_odd("gy"), is_odd("grp")
     first_y, last_y = beyond("gy")
     _, depth, inner, width = own.shape
     groups = inner // 8 + 2
+    odd_x = is_odd("gx")
     lane = lax.broadcasted_iota(jnp.int32, (8, LANES), 1)
+    row = lax.broadcasted_iota(jnp.int32, (8, width), 0)
+    wide = lax.broadcasted_iota(jnp.int32, (8, width), 1)
+
+    def spread_out(v):
+        return jnp.concatenate([v] * (width // LANES), 1)
+
     for p in range(depth):
-        for a in range(3):
-            from_a, from_b = got_a[a, p], got_b[a, p]
-            rim[0, a, p] = jnp.where(first_y, 0.0, jnp.where(odd_y == 1, from_a, from_b))
-            rim[1, a, p] = jnp.where(last_y, 0.0, jnp.where(odd_y == 1, from_b, from_a))
+        for side, (low, outside) in enumerate(((True, first_y), (False, last_y))):
+
+            def take(i):
+                strip = jnp.where(odd_y == (1 if low else 0), got_a[i], got_b[i])
+                return jnp.where(outside, 0.0, strip)
+
+            g = take(p)
+            sides = take(got_a.shape[0] - 1)[:, 0:LANES]
+            field = jnp.where(wide == 0, spread_out(pltpu.roll(sides, (LANES - p) % LANES, 1)), 0.0)
+            last = spread_out(pltpu.roll(sides, LANES - 1 - depth - p, 1))
+            field = jnp.where(wide == width - 1, last, field)
+            moved = pltpu.roll(g, HALO - 1 if low else 1, 0)
+            field = jnp.where(row == (HALO - 1 if low else 0), moved, field)
+            if reflect and p in (0, depth - 1):
+                field = jnp.where(odd_x == (1 if p == 0 else 0), take(2 * depth), field)
+            elif not reflect and p in (0, depth - 1):
+                field = take(2 * depth + (0 if p == 0 else 1))
+            rim[side, 0, p] = g
+            rim[side, 1, p] = take(depth + p)
+            rim[side, 2, p] = field
         head = tail = jnp.zeros((8, LANES), jnp.float32)
         for a in range(3):
             for g in range(groups):
@@ -133,7 +182,7 @@
     return each(lambda v, w: v * w, x, y)
 
 
-def solve(cells, own_at, own, out):
+def solve(cells, own_at, own, out, seams):
     (src, cond, field, wx, wy, wz, vy, vz, diag, inv, sum8, cwx, cwy, cwz, cvy, cvz, cinv, res, q, cq, err) = cells
     total, parts, rows, lanes = cond.shape
 
@@ -199,6 +248,26 @@
         n = times(load(scale, p), spread(v, p, refs, level))
         return each(lambda u, w: KEEP * u + SPREAD * w, load(v, p), n)
 
+    def between(p):
+        planes, along_y, along_z = seams
+        here = load(field, p)
+        r = load(src, p)
+
+        def less(r, weights, there, where=None):
+            flux = each(lambda w, u, v: w * (u - v), weights, here, there)
+            return each(lambda x, y: x - (y if where is None else jnp.where(where, y, 0.0)), r, flux)
+
+        if p in planes:
+            r = less(r, load(wx, p), load(field, p + 1))
+        if p - 1 in planes:
+            r = less(r, load(wx, p - 1), load(field, p - 1))
+        r = less(r, load(wy, p), [ahead(v, 0) for v in here], along_y[0])
+        r = less(r, load(vy, p), [behind(v, 0) for v in here], along_y[1])
+        if along_z is not None:
+            r = less(r, load(wz, p), fine[1](here), along_z[0])
+            r = less(r, load(vz, p), fine[2](here), along_z[1])
+        return r
+
     around, coarse_around = (wx, wy, wz, vy, vz), (cwx, cwy, cwz, cvy, cvz)
 
     for it in range(ITERS):
@@ -206,10 +275,11 @@
         for k in reach(halo + 2):
             found = []
             for p in (2 * k - 1, 2 * k):
-                v = field if it == 0 else err
-                start = [2.0 * u for u in load(src, p)] if it == 0 else load(res, p)
-                n = spread(v, p, around, fine)
-                r = each(lambda u, d, w, m: u - (d * w - m), start, load(diag, p), load(v, p), n)
+                if it == 0:
+                    r = between(p)
+                else:
+                    n = spread(err, p, around, fine)
+                    r = each(lambda u, d, w, m: u - (d * w - m), load(res, p), load(diag, p), load(err, p), n)
                 if it < ITERS - 1:
                     store(res, p, r)
                 store(q, p, times(r, load(inv, p)))
@@ -247,6 +317,11 @@
             above = odd_x == i
             at = jnp.where(above, p, depth - HALO + p)
             place(i, at, jnp.where(above, own_at + depth + p, 1 + p))
+
+
+def x_seams(reflect, depth):
+    own_at, _ = layout(reflect, depth)
+    return (own_at + depth - 1,) if reflect else (own_at - 1, own_at + depth - 1)
 
 
 def out_plane(reflect, depth, p):
@@ -318,7 +393,9 @@
         for i in range(2):
             halves[p - own_at, :, i * lanes : (i + 1) * lanes] = v[i][HALO : rows - HALO, :]
 
-    solve(cells, own_at, depth, out)
+    row = lax.broadcasted_iota(jnp.int32, (rows, lanes), 0)
+    along_y = (row == HALO - 1) | (row == HALO + inner - 1), (row == HALO) | (row == HALO + inner)
+    solve(cells, own_at, depth, out, (x_seams(reflect, depth), along_y, None))
     together = rearranged(halves[...].reshape(depth * inner, 2 * lanes), apart.T)
     together = together.reshape(depth, inner, width)
     for p in range(depth):
@@ -370,7 +447,12 @@
                     tile = jnp.where(lane >= LANES - HALO, tail, tile)
                 result[at, part, c : c + LANES] = tile
 
-    solve(cells, own_at, depth, out)
+    row = lax.broadcasted_iota(jnp.int32, ends.shape[2:], 0)
+    lane_in_half = lax.rem(lax.broadcasted_iota(jnp.int32, ends.shape[2:], 1), half)
+    upper_half = lax.broadcasted_iota(jnp.int32, ends.shape[2:], 1) >= half
+    face = jnp.where(upper_half, inner, HALO)
+    along_z = tuple((lane_in_half == at) | (lane_in_half == at + 16) for at in (23, 24))
+    solve(cells, own_at, depth, out, (x_seams(reflect, depth), (row == face - 1, row == face), along_z))
 
 
 def shards(sizes, source_term, conductivity, initial_field):
@@ -394,22 +476,18 @@
 
     reflect = sizes["gx"] == 2
     n_x = 1 if reflect else 2
-    face = jax.ShapeDtypeStruct((3, depth, HALO, width), f32)
     args = [pltpu.with_memory_space_constraint(v, pltpu.HBM) for v in args]
-    hbm = [pl.BlockSpec(memory_space=pltpu.HBM)] * 3
-    msgs = pl.pallas_call(
-        pack_rows, out_shape=(face, face), in_specs=hbm, out_specs=(VMEM, VMEM),
-        scratch_shapes=[pltpu.SemaphoreType.DMA((6,))], compiler_params=params, name="pack_rows",
-    )(*args)
-    own = pl.pallas_call(
-        pack_block, out_shape=jax.ShapeDtypeStruct((3, depth, inner, width), f32), in_specs=hbm, out_specs=VMEM,
-        scratch_shapes=[pltpu.SemaphoreType.DMA((3,))], compiler_params=params, name="pack_block",
-        cost_estimate=pl.CostEstimate(flops=0, bytes_accessed=2_000_000, transcendentals=0),
+    face = jax.ShapeDtypeStruct((2 * depth + n_x + 1, HALO, width), f32)
+    own, *msgs = pl.pallas_call(
+        functools.partial(prepare, reflect),
+        out_shape=(jax.ShapeDtypeStruct((3, depth, inner, width), f32), face, face),
+        in_specs=[pl.BlockSpec(memory_space=pltpu.HBM)] * 3, out_specs=(VMEM,) * 3,
+        scratch_shapes=[pltpu.SemaphoreType.DMA((3,))], compiler_params=params, name="prepare",
     )(*args)
     got = exchange(msgs, "gy")
     near = exchange([own] * n_x, "gx")
     strips, rim = pl.pallas_call(
-        pack_columns,
+        functools.partial(pack_columns, reflect),
         out_shape=(
             jax.ShapeDtypeStruct((2, depth, 8, LANES), f32),
             jax.ShapeDtypeStruct((2, 3, depth, HALO, width), f32),

time: 20.6 us -> 19.9 us (0.966)
  Pallas kernels: 7.94 us -> 7.08 us
  waiting for transfers between devices: 6.93 us -> 7.17 us
    pallas_call x3 -> x2, Pallas kernels: 2.36 us -> 1.75 us  [the longest x1 1.33 us: shards(): pl.pallas_call(functools.partial(prepare, reflect), out_shape=(jax.ShapeD...]
    ppermute x7, waiting for transfers between devices: 6.93 us -> 7.17 us  [exchange(): lax.ppermute(v, over, pairs)]
    pallas_call x1, Pallas kernels: 2.82 us -> 2.59 us  [shards(): pl.pallas_call(functools.partial(interior, reflect, n_x), out_shape=(bloc...]
  transfers between devices with their start and end apart: 7 -> 7, of which waited for: 4 -> 4; matrix products, arithmetic and copies ran while one was open for 0% -> 0% of each run, Pallas kernels for 19% -> 13%
where the time goes in v8:
time: 19.9 us; the launch traced here: 19.8 us
  waiting for transfers between devices  7.17 us (36%)
  Pallas kernels  7.08 us (36%)
  starting transfers between devices  5.48 us (28%)
    ppermute x7, waiting for transfers between devices, exchange(): lax.ppermute(v, over, pairs)  7.17 us
    ppermute x7, starting transfers between devices, exchange(): lax.ppermute(v, over, pairs)  5.48 us
    pallas_call x1, Pallas kernels, shards(): pl.pallas_call(functools.partial(edges, reflect), out_shape=block, in_spe...  2.74 us
    pallas_call x1, Pallas kernels, shards(): pl.pallas_call(functools.partial(interior, reflect, n_x), out_shape=(bloc...  2.59 us
    pallas_call x1, Pallas kernels, shards(): pl.pallas_call(functools.partial(prepare, reflect), out_shape=(jax.ShapeD...  1.33 us
    pallas_call x1, Pallas kernels, shards(): pl.pallas_call(functools.partial(pack_columns, reflect), out_shape=(jax.S...  0.42 us
  transfers between devices with their start and end apart: 7, of which 4 were waited for; matrix products, arithmetic and copies ran while one was open for 0% of the time, Pallas kernels for 13%

profile of v8, /device:TPU:18, one launch (start us, length us, event | category | flops | bytes accessed | tf_op | source)
XLA Modules:
  0.0 19.8 jit_solution(6631107499572065011)
XLA Ops:
  0.0 1.3 %prepare.1 = (f32[3,8,16,256]{3,2,1,0:T(8,128)S(1)}, f32[18,8,256]{2,1,0:T(8,128)S(1)}, f32[18,8,256]{2,1,0:T(8,128)S(1)}) custom-call(f32[8,16,256]{2,1,0:T(8,128)} %s.1, f32[8,16,256]{2,1,0:T(8,128)} %c.1, f32[8,16,256]{2,1,0:T(8,128)} %f.1), custom_call_target="tpu_custom_call" | custom-call | tf_op jit(solution)/shard_map/prepare/pallas_call | solution.py:481
  1.3 1.6 %collective-permute-start = (f32[18,8,256]{2,1,0:T(8,128)S(1)}, f32[18,8,256]{2,1,0:T(8,128)S(1)}, u32[]{:S(2)}, u32[]{:S(2)}) collective-permute-start(f32[18,8,256]{2,1,0:T(8,128)S(1)} %get-tuple-element.19), channel_id=1, source_target_pairs={{0,1},{4,5},{2,3},{6,7},{1,0},{5,4},{3,2},{7,6},{8,9},{12,13},{10,... | collective-permute-start | bytes 442376 | tf_op jit(solution)/shard_map/ppermute | solution.py:468
  3.0 0.0 collective-permute-start.1
  3.0 4.0 %collective-permute-done.got_a = f32[18,8,256]{2,1,0:T(8,128)S(1)} collective-permute-done((f32[18,8,256]{2,1,0:T(8,128)S(1)}, f32[18,8,256]{2,1,0:T(8,128)S(1)}, u32[]{:S(2)}, u32[]{:S(2)}) %collective-permute-start) | collective-permute-done | bytes 147488 | tf_op jit(solution)/shard_map/ppermute | solution.py:468
  7.0 1.3 %collective-permute-done.1.got_b = f32[18,8,256]{2,1,0:T(8,128)S(1)} collective-permute-done((f32[18,8,256]{2,1,0:T(8,128)S(1)}, f32[18,8,256]{2,1,0:T(8,128)S(1)}, u32[]{:S(2)}, u32[]{:S(2)}) %collective-permute-start.1) | collective-permute-done | bytes 147488 | tf_op jit(solution)/shard_map/ppermute | solution.py:468
  8.3 0.4 %pack_columns.1 = (f32[2,8,8,128]{3,2,1,0:T(8,128)S(1)}, f32[2,3,8,8,256]{4,3,2,1,0:T(8,128)S(1)}) custom-call(f32[3,8,16,256]{3,2,1,0:T(8,128)S(1)} %get-tuple-element.18.own.refs_0_, f32[18,8,256]{2,1,0:T(8,128)S(1)} %collective-permute-done.got_a, f32[18,8,256]{2,1,0:T(8,128)S(1)} %collective-permute-done.1.got_b), custom_call_target="tpu_custom_call" | custom-call | tf_op jit(solution)/shard_map/pack_columns/pallas_call | solution.py:489
  8.7 0.1 collective-permute-start.2
  8.8 0.5 %collective-permute-start.3 = (f32[3,8,16,256]{3,2,1,0:T(8,128)S(1)}, f32[3,8,16,256]{3,2,1,0:T(8,128)S(1)}, u32[]{:S(2)}, u32[]{:S(2)}) collective-permute-start(f32[3,8,16,256]{3,2,1,0:T(8,128)S(1)} %get-tuple-element.18.own.refs_0_), channel_id=1, source_target_pairs={{0,4},{4,0},{1,5},{5,1},{2,6},{6,2},{3,7},{7,3},{8,12},{12,8},{9,1... | collective-permute-start | bytes 1179656 | tf_op jit(solution)/shard_map/ppermute | solution.py:468
  9.3 0.7 %collective-permute-done.2 = f32[2,8,8,128]{3,2,1,0:T(8,128)S(1)} collective-permute-done((f32[2,8,8,128]{3,2,1,0:T(8,128)S(1)}, f32[2,8,8,128]{3,2,1,0:T(8,128)S(1)}, u32[]{:S(2)}, u32[]{:S(2)}) %collective-permute-start.2) | collective-permute-done | bytes 65568 | tf_op jit(solution)/shard_map/ppermute | solution.py:468
  10.1 0.2 %collective-permute-start.4 = (f32[2,3,8,8,256]{4,3,2,1,0:T(8,128)S(1)}, f32[2,3,8,8,256]{4,3,2,1,0:T(8,128)S(1)}, u32[]{:S(2)}, u32[]{:S(2)}) collective-permute-start(f32[2,3,8,8,256]{4,3,2,1,0:T(8,128)S(1)} %get-tuple-element.23.refs_1_), channel_id=1, source_target_pairs={{0,4},{4,0},{1,5},{5,1},{2,6},{6,2},{3,7},{7,3},{8,12},{12,8},{9,1... | collective-permute-start | bytes 1179656 | tf_op jit(solution)/shard_map/ppermute | solution.py:468
  10.3 0.6 %collective-permute-start.6 = (f32[16,8,128]{2,1,0:T(8,128)S(1)}, f32[16,8,128]{2,1,0:T(8,128)S(1)}, u32[]{:S(2)}, u32[]{:S(2)}) collective-permute-start(f32[16,8,128]{2,1,0:T(8,128)S(1)} %get-tuple-element.31), channel_id=1, source_target_pairs={{0,8},{4,12},{16,24},{20,28},{8,0},{12,4},{24,16},{28,20},{1,9},{5... | collective-permute-start | bytes 196616 | tf_op jit(solution)/shard_map/ppermute | solution.py:468
  10.9 2.4 %collective-permute-start.5 = (f32[16,8,128]{2,1,0:T(8,128)S(1)}, f32[16,8,128]{2,1,0:T(8,128)S(1)}, u32[]{:S(2)}, u32[]{:S(2)}) collective-permute-start(f32[16,8,128]{2,1,0:T(8,128)S(1)} %get-tuple-element.32), channel_id=1, source_target_pairs={{8,16},{12,20},{0,4},{24,28},{16,8},{20,12},{4,0},{28,24},{9,17},{... | collective-permute-start | bytes 196616 | tf_op jit(solution)/shard_map/ppermute | solution.py:468
  13.3 0.0 collective-permute-done.3.refs_2_
  13.3 0.0 collective-permute-done.4.refs_3_
  13.3 2.6 %interior.1 = (f32[8,16,256]{2,1,0:T(8,128)S(1)}, f32[3,18,24,128]{3,2,1,0:T(8,128)S(1)}) custom-call(f32[3,8,16,256]{3,2,1,0:T(8,128)S(1)} %get-tuple-element.18.own.refs_0_, f32[2,3,8,8,256]{4,3,2,1,0:T(8,128)S(1)} %get-tuple-element.23.refs_1_, f32[3,8,16,256]{3,2,1,0:T(8,128)S(1)} %collective-permute-done.3.refs_2_, ...), custom_call_target="tpu_custom_call" | custom-call | flops 20000000 | bytes 20000000 | tf_op jit(solution)/shard_map/interior/pallas_call | solution.py:507
  15.9 0.0 collective-permute-done.6.got_a
  16.0 1.1 %collective-permute-done.5.got_b = f32[16,8,128]{2,1,0:T(8,128)S(1)} collective-permute-done((f32[16,8,128]{2,1,0:T(8,128)S(1)}, f32[16,8,128]{2,1,0:T(8,128)S(1)}, u32[]{:S(2)}, u32[]{:S(2)}) %collective-permute-start.5) | collective-permute-done | bytes 65568 | tf_op jit(solution)/shard_map/ppermute | solution.py:468
  17.1 2.7 %edges.1 = f32[8,16,256]{2,1,0:T(8,128)} custom-call(f32[3,18,24,128]{3,2,1,0:T(8,128)S(1)} %get-tuple-element.27.ends, f32[8,16,256]{2,1,0:T(8,128)S(1)} %get-tuple-element.28.inside, f32[16,8,128]{2,1,0:T(8,128)S(1)} %collective-permute-done.6.got_a, f32[16,8,128]{2,1,0:T(8,128)S(1)} %collective-permute-done.5.got_b), custom_call_target="tpu_custom_call" | custom-call | tf_op jit(solution)/shard_map/edges/pallas_call | solution.py:516
  (2 shorter events, 0.0 us)
Async XLA Ops:
  1.3 5.7 %collective-permute-start = (f32[18,8,256]{2,1,0:T(8,128)S(1)}, f32[18,8,256]{2,1,0:T(8,128)S(1)}, u32[]{:S(2)}, u32[]{:S(2)}) collective-permute-start(f32[18,8,256]{2,1,0:T(8,128)S(1)} %get-tuple-element.19), channel_id=1, source_target_pairs={{0,1},{4,5},{2,3},{6,7},{1,0},{5,4},{3,2},{7,6},{8,9},{12,13},{10,... | collective-permute-start | bytes 442376 | tf_op jit(solution)/shard_map/ppermute | solution.py:468
  3.0 5.3 %collective-permute-start.1 = (f32[18,8,256]{2,1,0:T(8,128)S(1)}, f32[18,8,256]{2,1,0:T(8,128)S(1)}, u32[]{:S(2)}, u32[]{:S(2)}) collective-permute-start(f32[18,8,256]{2,1,0:T(8,128)S(1)} %get-tuple-element.20), channel_id=1, source_target_pairs={{1,2},{5,6},{0,4},{3,7},{2,1},{6,5},{4,0},{7,3},{9,10},{13,14},{8,... | collective-permute-start | bytes 442376 | tf_op jit(solution)/shard_map/ppermute | solution.py:468
  8.7 1.3 %collective-permute-start.2 = (f32[2,8,8,128]{3,2,1,0:T(8,128)S(1)}, f32[2,8,8,128]{3,2,1,0:T(8,128)S(1)}, u32[]{:S(2)}, u32[]{:S(2)}) collective-permute-start(f32[2,8,8,128]{3,2,1,0:T(8,128)S(1)} %get-tuple-element.21), channel_id=1, source_target_pairs={{0,4},{4,0},{1,5},{5,1},{2,6},{6,2},{3,7},{7,3},{8,12},{12,8},{9,1... | collective-permute-start | bytes 196616 | tf_op jit(solution)/shard_map/ppermute | solution.py:468
  8.8 4.5 %collective-permute-start.3 = (f32[3,8,16,256]{3,2,1,0:T(8,128)S(1)}, f32[3,8,16,256]{3,2,1,0:T(8,128)S(1)}, u32[]{:S(2)}, u32[]{:S(2)}) collective-permute-start(f32[3,8,16,256]{3,2,1,0:T(8,128)S(1)} %get-tuple-element.18.own.refs_0_), channel_id=1, source_target_pairs={{0,4},{4,0},{1,5},{5,1},{2,6},{6,2},{3,7},{7,3},{8,12},{12,8},{9,1... | collective-permute-start | bytes 1179656 | tf_op jit(solution)/shard_map/ppermute | solution.py:468
  10.1 3.3 %collective-permute-start.4 = (f32[2,3,8,8,256]{4,3,2,1,0:T(8,128)S(1)}, f32[2,3,8,8,256]{4,3,2,1,0:T(8,128)S(1)}, u32[]{:S(2)}, u32[]{:S(2)}) collective-permute-start(f32[2,3,8,8,256]{4,3,2,1,0:T(8,128)S(1)} %get-tuple-element.23.refs_1_), channel_id=1, source_target_pairs={{0,4},{4,0},{1,5},{5,1},{2,6},{6,2},{3,7},{7,3},{8,12},{12,8},{9,1... | collective-permute-start | bytes 1179656 | tf_op jit(solution)/shard_map/ppermute | solution.py:468
  10.3 5.7 %collective-permute-start.6 = (f32[16,8,128]{2,1,0:T(8,128)S(1)}, f32[16,8,128]{2,1,0:T(8,128)S(1)}, u32[]{:S(2)}, u32[]{:S(2)}) collective-permute-start(f32[16,8,128]{2,1,0:T(8,128)S(1)} %get-tuple-element.31), channel_id=1, source_target_pairs={{0,8},{4,12},{16,24},{20,28},{8,0},{12,4},{24,16},{28,20},{1,9},{5... | collective-permute-start | bytes 196616 | tf_op jit(solution)/shard_map/ppermute | solution.py:468
  10.9 6.2 %collective-permute-start.5 = (f32[16,8,128]{2,1,0:T(8,128)S(1)}, f32[16,8,128]{2,1,0:T(8,128)S(1)}, u32[]{:S(2)}, u32[]{:S(2)}) collective-permute-start(f32[16,8,128]{2,1,0:T(8,128)S(1)} %get-tuple-element.32), channel_id=1, source_target_pairs={{8,16},{12,20},{0,4},{24,28},{16,8},{20,12},{4,0},{28,24},{9,17},{... | collective-permute-start | bytes 196616 | tf_op jit(solution)/shard_map/ppermute | solution.py:468

commit v9 on v8

--- a/solution.py
+++ b/solution.py
@@ -55,6 +55,22 @@
 
 def is_odd(axis):
     return lax.rem(lax.axis_index(axis), 2)
+
+
+def far_row(high, distance):
+    if isinstance(high, bool):
+        return HALO - distance if high else distance - 1
+    return jnp.where(high, HALO - distance, distance - 1)
+
+
+def shifted_rows(high, v, n):
+    if isinstance(high, bool):
+        return pltpu.roll(v, HALO - n if high else n, 0)
+    return jnp.where(high, pltpu.roll(v, HALO - n, 0), pltpu.roll(v, n, 0))
+
+
+def inward(high, v):
+    return shifted_rows(high, v, HALO - 1)
 
 
 def prepare(reflect, s, c, f, own, first, second, sems):
@@ -87,20 +103,28 @@
     lane = lax.broadcasted_iota(jnp.int32, (HALO, LANES), 1)
     for message, high in ((first, odd == 0), (second, odd == 1)):
         rows = pl.ds(pl.multiple_of(jnp.where(high, inner - HALO, 0), 8), HALO)
+        at = functools.partial(far_row, high)
         sides = jnp.zeros((HALO, LANES), jnp.float32)
-        for p in range(depth):
-            field = own[2, p, rows, :]
-            below = jnp.where(row == HALO - 1, pltpu.roll(field, HALO - 1, 0), own[0, p, rows, :])
-            above = jnp.where(row == 0, pltpu.roll(field, 1, 0), own[0, p, rows, :])
-            message[p] = jnp.where(high, above, below)
-            message[depth + p] = own[1, p, rows, :]
-            sides = jnp.where(lane == p, pltpu.roll(field[:, 0:LANES], p, 1), sides)
-            sides = jnp.where(lane == depth + p, pltpu.roll(field[:, width - LANES : width], depth + p + 1, 1), sides)
+        for p in range(0, depth, 2):
+            sums = own[1, p, rows, :] + own[1, p + 1, rows, :]
+            sums = sums + inward(high, sums)
+            rests = own[0, p, rows, :] + own[0, p + 1, rows, :]
+            rests = shifted_rows(high, rests + inward(high, rests), 2)
+            for i, seventh in enumerate((sums, rests)):
+                field = own[2, p + i, rows, :]
+                cond = jnp.where(row == at(7), seventh, own[1, p + i, rows, :])
+                message[p + i] = jnp.where(row == at(8), inward(high, field), cond)
+                head, tail = field[:, 0:LANES], field[:, width - LANES : width]
+                sides = jnp.where(lane == p + i, pltpu.roll(head, p + i, 1), sides)
+                sides = jnp.where(lane == depth + p + i, pltpu.roll(tail, depth + p + i + 1, 1), sides)
+            near = jnp.where(high, HALO - 1 - row, row) < 4
+            message[depth + p // 2] = jnp.where(near, own[0, p, rows, :], pltpu.roll(own[0, p + 1, rows, :], 4, 0))
+        planes = depth + depth // 2
         if reflect:
-            message[2 * depth] = own[2, depth - 1 - outer, rows, :]
+            message[planes] = own[2, depth - 1 - outer, rows, :]
         else:
-            message[2 * depth] = own[2, 0, rows, :]
-            message[2 * depth + 1] = own[2, depth - 1, rows, :]
+            message[planes] = own[2, 0, rows, :]
+            message[planes + 1] = own[2, depth - 1, rows, :]
         message[message.shape[0] - 1] = jnp.zeros((HALO, width), jnp.float32)
         message[message.shape[0] - 1, :, 0:LANES] = sides
 
@@ -129,23 +153,32 @@
     for p in range(depth):
         for side, (low, outside) in enumerate(((True, first_y), (False, last_y))):
 
+            at = functools.partial(far_row, low)
+
             def take(i):
                 strip = jnp.where(odd_y == (1 if low else 0), got_a[i], got_b[i])
                 return jnp.where(outside, 0.0, strip)
 
-            g = take(p)
+            cond, mixed = take(p), take(depth + p // 2)
+            g = mixed if p % 2 == 0 else pltpu.roll(mixed, 4, 0)
+            g = jnp.where(row >= 4 if low else row < 4, g, 0.0)
+            if p % 2:
+                g = jnp.where(row == at(5), shifted_rows(low, cond, HALO - 2), g)
             sides = take(got_a.shape[0] - 1)[:, 0:LANES]
             field = jnp.where(wide == 0, spread_out(pltpu.roll(sides, (LANES - p) % LANES, 1)), 0.0)
             last = spread_out(pltpu.roll(sides, LANES - 1 - depth - p, 1))
             field = jnp.where(wide == width - 1, last, field)
-            moved = pltpu.roll(g, HALO - 1 if low else 1, 0)
-            field = jnp.where(row == (HALO - 1 if low else 0), moved, field)
+            field = jnp.where(row == at(1), shifted_rows(low, cond, 1), field)
+            planes = depth + depth // 2
             if reflect and p in (0, depth - 1):
-                field = jnp.where(odd_x == (1 if p == 0 else 0), take(2 * depth), field)
+                field = jnp.where(odd_x == (1 if p == 0 else 0), take(planes), field)
             elif not reflect and p in (0, depth - 1):
-                field = take(2 * depth + (0 if p == 0 else 1))
+                field = take(planes + (0 if p == 0 else 1))
+            cond = jnp.where(row == at(8), 0.0, cond)
+            if p % 2:
+                cond = jnp.where(row == at(7), 0.0, cond)
             rim[side, 0, p] = g
-            rim[side, 1, p] = take(depth + p)
+            rim[side, 1, p] = cond
             rim[side, 2, p] = field
         head = tail = jnp.zeros((8, LANES), jnp.float32)
         for a in range(3):
@@ -477,7 +510,7 @@
     reflect = sizes["gx"] == 2
     n_x = 1 if reflect else 2
     args = [pltpu.with_memory_space_constraint(v, pltpu.HBM) for v in args]
-    face = jax.ShapeDtypeStruct((2 * depth + n_x + 1, HALO, width), f32)
+    face = jax.ShapeDtypeStruct((depth + depth // 2 + n_x + 1, HALO, width), f32)
     own, *msgs = pl.pallas_call(
         functools.partial(prepare, reflect),
         out_shape=(jax.ShapeDtypeStruct((3, depth, inner, width), f32), face, face),

time: 19.9 us -> 19.5 us (0.980)
  waiting for transfers between devices: 7.17 us -> 6.65 us
    ppermute x7, waiting for transfers between devices: 7.17 us -> 6.65 us  [exchange(): lax.ppermute(v, over, pairs)]
where the time goes in v9:
time: 19.5 us; the launch traced here: 19.3 us
  Pallas kernels  7.11 us (36%)
  waiting for transfers between devices  6.65 us (34%)
  starting transfers between devices  5.48 us (28%)
    ppermute x7, waiting for transfers between devices, exchange(): lax.ppermute(v, over, pairs)  6.65 us
    ppermute x7, starting transfers between devices, exchange(): lax.ppermute(v, over, pairs)  5.48 us
    pallas_call x1, Pallas kernels, shards(): pl.pallas_call(functools.partial(edges, reflect), out_shape=block, in_spe...  2.74 us
    pallas_call x1, Pallas kernels, shards(): pl.pallas_call(functools.partial(interior, reflect, n_x), out_shape=(bloc...  2.59 us
    pallas_call x1, Pallas kernels, shards(): pl.pallas_call(functools.partial(prepare, reflect), out_shape=(jax.ShapeD...  1.36 us
    pallas_call x1, Pallas kernels, shards(): pl.pallas_call(functools.partial(pack_columns, reflect), out_shape=(jax.S...  0.42 us
  transfers between devices with their start and end apart: 7, of which 4 were waited for; matrix products, arithmetic and copies ran while one was open for 0% of the time, Pallas kernels for 13%

profile of v9, /device:TPU:18, one launch (start us, length us, event | category | flops | bytes accessed | tf_op | source)
XLA Modules:
  0.0 19.3 jit_solution(15333452081814771901)
XLA Ops:
  0.0 1.4 %prepare.1 = (f32[3,8,16,256]{3,2,1,0:T(8,128)S(1)}, f32[14,8,256]{2,1,0:T(8,128)S(1)}, f32[14,8,256]{2,1,0:T(8,128)S(1)}) custom-call(f32[8,16,256]{2,1,0:T(8,128)} %s.1, f32[8,16,256]{2,1,0:T(8,128)} %c.1, f32[8,16,256]{2,1,0:T(8,128)} %f.1), custom_call_target="tpu_custom_call" | custom-call | tf_op jit(solution)/shard_map/prepare/pallas_call | solution.py:514
  1.4 1.6 %collective-permute-start = (f32[14,8,256]{2,1,0:T(8,128)S(1)}, f32[14,8,256]{2,1,0:T(8,128)S(1)}, u32[]{:S(2)}, u32[]{:S(2)}) collective-permute-start(f32[14,8,256]{2,1,0:T(8,128)S(1)} %get-tuple-element.19), channel_id=1, source_target_pairs={{0,1},{4,5},{2,3},{6,7},{1,0},{5,4},{3,2},{7,6},{8,9},{12,13},{10,... | collective-permute-start | bytes 344072 | tf_op jit(solution)/shard_map/ppermute | solution.py:501
  3.0 0.0 collective-permute-start.1
  3.0 3.3 %collective-permute-done.got_a = f32[14,8,256]{2,1,0:T(8,128)S(1)} collective-permute-done((f32[14,8,256]{2,1,0:T(8,128)S(1)}, f32[14,8,256]{2,1,0:T(8,128)S(1)}, u32[]{:S(2)}, u32[]{:S(2)}) %collective-permute-start) | collective-permute-done | bytes 114720 | tf_op jit(solution)/shard_map/ppermute | solution.py:501
  6.3 1.5 %collective-permute-done.1.got_b = f32[14,8,256]{2,1,0:T(8,128)S(1)} collective-permute-done((f32[14,8,256]{2,1,0:T(8,128)S(1)}, f32[14,8,256]{2,1,0:T(8,128)S(1)}, u32[]{:S(2)}, u32[]{:S(2)}) %collective-permute-start.1) | collective-permute-done | bytes 114720 | tf_op jit(solution)/shard_map/ppermute | solution.py:501
  7.8 0.4 %pack_columns.1 = (f32[2,8,8,128]{3,2,1,0:T(8,128)S(1)}, f32[2,3,8,8,256]{4,3,2,1,0:T(8,128)S(1)}) custom-call(f32[3,8,16,256]{3,2,1,0:T(8,128)S(1)} %get-tuple-element.18.own.refs_0_, f32[14,8,256]{2,1,0:T(8,128)S(1)} %collective-permute-done.got_a, f32[14,8,256]{2,1,0:T(8,128)S(1)} %collective-permute-done.1.got_b), custom_call_target="tpu_custom_call" | custom-call | tf_op jit(solution)/shard_map/pack_columns/pallas_call | solution.py:522
  8.2 0.1 collective-permute-start.2
  8.3 0.5 %collective-permute-start.3 = (f32[3,8,16,256]{3,2,1,0:T(8,128)S(1)}, f32[3,8,16,256]{3,2,1,0:T(8,128)S(1)}, u32[]{:S(2)}, u32[]{:S(2)}) collective-permute-start(f32[3,8,16,256]{3,2,1,0:T(8,128)S(1)} %get-tuple-element.18.own.refs_0_), channel_id=1, source_target_pairs={{0,4},{4,0},{1,5},{5,1},{2,6},{6,2},{3,7},{7,3},{8,12},{12,8},{9,1... | collective-permute-start | bytes 1179656 | tf_op jit(solution)/shard_map/ppermute | solution.py:501
  8.8 0.7 %collective-permute-done.2 = f32[2,8,8,128]{3,2,1,0:T(8,128)S(1)} collective-permute-done((f32[2,8,8,128]{3,2,1,0:T(8,128)S(1)}, f32[2,8,8,128]{3,2,1,0:T(8,128)S(1)}, u32[]{:S(2)}, u32[]{:S(2)}) %collective-permute-start.2) | collective-permute-done | bytes 65568 | tf_op jit(solution)/shard_map/ppermute | solution.py:501
  9.6 0.2 %collective-permute-start.4 = (f32[2,3,8,8,256]{4,3,2,1,0:T(8,128)S(1)}, f32[2,3,8,8,256]{4,3,2,1,0:T(8,128)S(1)}, u32[]{:S(2)}, u32[]{:S(2)}) collective-permute-start(f32[2,3,8,8,256]{4,3,2,1,0:T(8,128)S(1)} %get-tuple-element.23.refs_1_), channel_id=1, source_target_pairs={{0,4},{4,0},{1,5},{5,1},{2,6},{6,2},{3,7},{7,3},{8,12},{12,8},{9,1... | collective-permute-start | bytes 1179656 | tf_op jit(solution)/shard_map/ppermute | solution.py:501
  9.8 0.6 %collective-permute-start.6 = (f32[16,8,128]{2,1,0:T(8,128)S(1)}, f32[16,8,128]{2,1,0:T(8,128)S(1)}, u32[]{:S(2)}, u32[]{:S(2)}) collective-permute-start(f32[16,8,128]{2,1,0:T(8,128)S(1)} %get-tuple-element.31), channel_id=1, source_target_pairs={{0,8},{4,12},{16,24},{20,28},{8,0},{12,4},{24,16},{28,20},{1,9},{5... | collective-permute-start | bytes 196616 | tf_op jit(solution)/shard_map/ppermute | solution.py:501
  10.4 2.4 %collective-permute-start.5 = (f32[16,8,128]{2,1,0:T(8,128)S(1)}, f32[16,8,128]{2,1,0:T(8,128)S(1)}, u32[]{:S(2)}, u32[]{:S(2)}) collective-permute-start(f32[16,8,128]{2,1,0:T(8,128)S(1)} %get-tuple-element.32), channel_id=1, source_target_pairs={{8,16},{12,20},{0,4},{24,28},{16,8},{20,12},{4,0},{28,24},{9,17},{... | collective-permute-start | bytes 196616 | tf_op jit(solution)/shard_map/ppermute | solution.py:501
  12.8 0.0 collective-permute-done.3.refs_2_
  12.9 0.0 collective-permute-done.4.refs_3_
  12.9 2.6 %interior.1 = (f32[8,16,256]{2,1,0:T(8,128)S(1)}, f32[3,18,24,128]{3,2,1,0:T(8,128)S(1)}) custom-call(f32[3,8,16,256]{3,2,1,0:T(8,128)S(1)} %get-tuple-element.18.own.refs_0_, f32[2,3,8,8,256]{4,3,2,1,0:T(8,128)S(1)} %get-tuple-element.23.refs_1_, f32[3,8,16,256]{3,2,1,0:T(8,128)S(1)} %collective-permute-done.3.refs_2_, ...), custom_call_target="tpu_custom_call" | custom-call | flops 20000000 | bytes 20000000 | tf_op jit(solution)/shard_map/interior/pallas_call | solution.py:540
  15.5 0.0 collective-permute-done.6.got_a
  15.5 1.1 %collective-permute-done.5.got_b = f32[16,8,128]{2,1,0:T(8,128)S(1)} collective-permute-done((f32[16,8,128]{2,1,0:T(8,128)S(1)}, f32[16,8,128]{2,1,0:T(8,128)S(1)}, u32[]{:S(2)}, u32[]{:S(2)}) %collective-permute-start.5) | collective-permute-done | bytes 65568 | tf_op jit(solution)/shard_map/ppermute | solution.py:501
  16.6 2.7 %edges.1 = f32[8,16,256]{2,1,0:T(8,128)} custom-call(f32[3,18,24,128]{3,2,1,0:T(8,128)S(1)} %get-tuple-element.27.ends, f32[8,16,256]{2,1,0:T(8,128)S(1)} %get-tuple-element.28.inside, f32[16,8,128]{2,1,0:T(8,128)S(1)} %collective-permute-done.6.got_a, f32[16,8,128]{2,1,0:T(8,128)S(1)} %collective-permute-done.5.got_b), custom_call_target="tpu_custom_call" | custom-call | tf_op jit(solution)/shard_map/edges/pallas_call | solution.py:549
  (2 shorter events, 0.0 us)
Async XLA Ops:
  1.4 5.0 %collective-permute-start = (f32[14,8,256]{2,1,0:T(8,128)S(1)}, f32[14,8,256]{2,1,0:T(8,128)S(1)}, u32[]{:S(2)}, u32[]{:S(2)}) collective-permute-start(f32[14,8,256]{2,1,0:T(8,128)S(1)} %get-tuple-element.19), channel_id=1, source_target_pairs={{0,1},{4,5},{2,3},{6,7},{1,0},{5,4},{3,2},{7,6},{8,9},{12,13},{10,... | collective-permute-start | bytes 344072 | tf_op jit(solution)/shard_map/ppermute | solution.py:501
  3.0 4.8 %collective-permute-start.1 = (f32[14,8,256]{2,1,0:T(8,128)S(1)}, f32[14,8,256]{2,1,0:T(8,128)S(1)}, u32[]{:S(2)}, u32[]{:S(2)}) collective-permute-start(f32[14,8,256]{2,1,0:T(8,128)S(1)} %get-tuple-element.20), channel_id=1, source_target_pairs={{1,2},{5,6},{0,4},{3,7},{2,1},{6,5},{4,0},{7,3},{9,10},{13,14},{8,... | collective-permute-start | bytes 344072 | tf_op jit(solution)/shard_map/ppermute | solution.py:501
  8.2 1.3 %collective-permute-start.2 = (f32[2,8,8,128]{3,2,1,0:T(8,128)S(1)}, f32[2,8,8,128]{3,2,1,0:T(8,128)S(1)}, u32[]{:S(2)}, u32[]{:S(2)}) collective-permute-start(f32[2,8,8,128]{3,2,1,0:T(8,128)S(1)} %get-tuple-element.21), channel_id=1, source_target_pairs={{0,4},{4,0},{1,5},{5,1},{2,6},{6,2},{3,7},{7,3},{8,12},{12,8},{9,1... | collective-permute-start | bytes 196616 | tf_op jit(solution)/shard_map/ppermute | solution.py:501
  8.3 4.5 %collective-permute-start.3 = (f32[3,8,16,256]{3,2,1,0:T(8,128)S(1)}, f32[3,8,16,256]{3,2,1,0:T(8,128)S(1)}, u32[]{:S(2)}, u32[]{:S(2)}) collective-permute-start(f32[3,8,16,256]{3,2,1,0:T(8,128)S(1)} %get-tuple-element.18.own.refs_0_), channel_id=1, source_target_pairs={{0,4},{4,0},{1,5},{5,1},{2,6},{6,2},{3,7},{7,3},{8,12},{12,8},{9,1... | collective-permute-start | bytes 1179656 | tf_op jit(solution)/shard_map/ppermute | solution.py:501
  9.6 3.3 %collective-permute-start.4 = (f32[2,3,8,8,256]{4,3,2,1,0:T(8,128)S(1)}, f32[2,3,8,8,256]{4,3,2,1,0:T(8,128)S(1)}, u32[]{:S(2)}, u32[]{:S(2)}) collective-permute-start(f32[2,3,8,8,256]{4,3,2,1,0:T(8,128)S(1)} %get-tuple-element.23.refs_1_), channel_id=1, source_target_pairs={{0,4},{4,0},{1,5},{5,1},{2,6},{6,2},{3,7},{7,3},{8,12},{12,8},{9,1... | collective-permute-start | bytes 1179656 | tf_op jit(solution)/shard_map/ppermute | solution.py:501
  9.8 5.7 %collective-permute-start.6 = (f32[16,8,128]{2,1,0:T(8,128)S(1)}, f32[16,8,128]{2,1,0:T(8,128)S(1)}, u32[]{:S(2)}, u32[]{:S(2)}) collective-permute-start(f32[16,8,128]{2,1,0:T(8,128)S(1)} %get-tuple-element.31), channel_id=1, source_target_pairs={{0,8},{4,12},{16,24},{20,28},{8,0},{12,4},{24,16},{28,20},{1,9},{5... | collective-permute-start | bytes 196616 | tf_op jit(solution)/shard_map/ppermute | solution.py:501
  10.4 6.2 %collective-permute-start.5 = (f32[16,8,128]{2,1,0:T(8,128)S(1)}, f32[16,8,128]{2,1,0:T(8,128)S(1)}, u32[]{:S(2)}, u32[]{:S(2)}) collective-permute-start(f32[16,8,128]{2,1,0:T(8,128)S(1)} %get-tuple-element.32), channel_id=1, source_target_pairs={{8,16},{12,20},{0,4},{24,28},{16,8},{20,12},{4,0},{28,24},{9,17},{... | collective-permute-start | bytes 196616 | tf_op jit(solution)/shard_map/ppermute | solution.py:501

commit v10 on v9

--- a/solution.py
+++ b/solution.py
@@ -71,6 +71,12 @@
 
 def inward(high, v):
     return shifted_rows(high, v, HALO - 1)
+
+
+def both_ends(rows):
+    width = rows.shape[1]
+    lane = lax.broadcasted_iota(jnp.int32, (rows.shape[0], LANES), 1)
+    return jnp.where(lane < LANES // 2, rows[:, 0:LANES], rows[:, width - LANES : width])
 
 
 def prepare(reflect, s, c, f, own, first, second, sems):
@@ -86,11 +92,12 @@
     for p in range(depth):
         cond, field = own[1, p], own[2, p]
 
-        def flux(shift, axis):
-            return (cond + shift(cond, axis)) * (field - shift(field, axis))
-
-        total = jnp.where(row < inner - 1, flux(ahead, 0), 0.0) + jnp.where(row > 0, flux(behind, 0), 0.0)
-        total += jnp.where(column < width - 1, flux(ahead, 1), 0.0) + jnp.where(column > 0, flux(behind, 1), 0.0)
+        def flux(axis):
+            return (cond + ahead(cond, axis)) * (field - ahead(field, axis))
+
+        along_y = jnp.where(row < inner - 1, flux(0), 0.0)
+        along_z = jnp.where(column < width - 1, flux(1), 0.0)
+        total = (along_y - behind(along_y, 0)) + (along_z - behind(along_z, 1))
         for other in (p - 1, p + 1):
             if 0 <= other < depth:
                 total += (cond + own[1, other]) * (field - own[2, other])
@@ -114,9 +121,8 @@
                 field = own[2, p + i, rows, :]
                 cond = jnp.where(row == at(7), seventh, own[1, p + i, rows, :])
                 message[p + i] = jnp.where(row == at(8), inward(high, field), cond)
-                head, tail = field[:, 0:LANES], field[:, width - LANES : width]
-                sides = jnp.where(lane == p + i, pltpu.roll(head, p + i, 1), sides)
-                sides = jnp.where(lane == depth + p + i, pltpu.roll(tail, depth + p + i + 1, 1), sides)
+                ends = pltpu.roll(both_ends(field), 2 * (p + i) + 1, 1)
+                sides = jnp.where(lane // 2 == p + i, ends, sides)
             near = jnp.where(high, HALO - 1 - row, row) < 4
             message[depth + p // 2] = jnp.where(near, own[0, p, rows, :], pltpu.roll(own[0, p + 1, rows, :], 4, 0))
         planes = depth + depth // 2
@@ -130,11 +136,11 @@
 
 
 def head_lane(a, g):
-    return 16 * a + LANES // 2 * (g % 2) + 8 * (g // 2)
+    return 8 + 16 * a + LANES // 2 * (g % 2) + 8 * (g // 2)
 
 
 def tail_lane(a, g):
-    return 16 * a + LANES // 2 * (g % 2) + 8 * (1 - g // 2)
+    return 8 + 16 * a + LANES // 2 * (g % 2) + 8 * (1 - g // 2)
 
 
 def pack_columns(reflect, own, got_a, got_b, strips, rim):
@@ -165,9 +171,8 @@
             if p % 2:
                 g = jnp.where(row == at(5), shifted_rows(low, cond, HALO - 2), g)
             sides = take(got_a.shape[0] - 1)[:, 0:LANES]
-            field = jnp.where(wide == 0, spread_out(pltpu.roll(sides, (LANES - p) % LANES, 1)), 0.0)
-            last = spread_out(pltpu.roll(sides, LANES - 1 - depth - p, 1))
-            field = jnp.where(wide == width - 1, last, field)
+            ends = spread_out(pltpu.roll(sides, LANES - 1 - 2 * p, 1))
+            field = jnp.where((wide == 0) | (wide == width - 1), ends, 0.0)
             field = jnp.where(row == at(1), shifted_rows(low, cond, 1), field)
             planes = depth + depth // 2
             if reflect and p in (0, depth - 1):
@@ -187,12 +192,14 @@
                     rows = rim[min(g, 1), a, p]
                 else:
                     rows = own[a, p, 8 * g - 8 : 8 * g, :]
-                to = head_lane(a, g)
-                moved = pltpu.roll(rows[:, 0:LANES], to, 1)
-                head = jnp.where((lane >= to) & (lane < to + HALO), moved, head)
-                to = tail_lane(a, g)
-                moved = pltpu.roll(rows[:, width - LANES : width], (to + HALO) % LANES, 1)
-                tail = jnp.where((lane >= to) & (lane < to + HALO), moved, tail)
+                to_head, to_tail = head_lane(a, g), tail_lane(a, g)
+                if to_head == to_tail + HALO:
+                    first_moved = last_moved = pltpu.roll(both_ends(rows), to_head, 1)
+                else:
+                    first_moved = pltpu.roll(rows[:, 0:LANES], to_head, 1)
+                    last_moved = pltpu.roll(rows[:, width - LANES : width], (to_tail + HALO) % LANES, 1)
+                head = jnp.where((lane >= to_head) & (lane < to_head + HALO), first_moved, head)
+                tail = jnp.where((lane >= to_tail) & (lane < to_tail + HALO), last_moved, tail)
         strips[0, p] = jnp.where(odd_z == 1, head, tail)
         strips[1, p] = jnp.where(odd_z == 1, tail, head)
 
@@ -241,8 +248,7 @@
     even_lane = lax.rem(lax.broadcasted_iota(jnp.int32, (rows, lanes), 1), 2) == 0
 
     def gather(v):
-        other = v[1] if parts == 2 else jnp.where(even_lane, ahead(v[0], 1), behind(v[0], 1))
-        t = v[0] + other
+        t = v[0] + (v[1] if parts == 2 else ahead(v[0], 1))
         return [t + ahead(t, 0)]
 
     for k in reach(HALO):
@@ -321,6 +327,8 @@
 
         for k in reach(halo):
             (c,) = smooth(cq, k, coarse_around, cinv, coarse)
+            if parts == 1:
+                c = jnp.where(even_lane, c, behind(c, 1))
             c = jnp.where(even_row, c, behind(c, 0))
             for p in (2 * k - 1, 2 * k):
                 e = [u + c for u in smooth(q, p, around, inv, fine)]
@@ -452,13 +460,13 @@
         va, vb = got_a[at_plane], got_b[at_plane]
         right = jnp.where(last_z, 0.0, jnp.where(odd_z == 1, vb, va))
         left = jnp.where(first_z, 0.0, jnp.where(odd_z == 1, va, vb))
-        side = lax.rem(lane, 16) < 8
+        side = lax.rem(lane, 16) >= 8
         lower = jnp.where(side, right, left)
         upper = jnp.where(side, pltpu.roll(right, LANES - 8, 1), pltpu.roll(left, 8, 1))
-        middle = jnp.where(lane < half, upper, lower)
+        middle = pltpu.roll(jnp.where(lane < half, upper, lower), half, 1)
         for a in range(3):
-            for t, (groups_of, shift) in enumerate(((lower, 24), (middle, 24 + half), (upper, 24))):
-                moved = pltpu.roll(groups_of, (shift - 16 * a) % LANES, 1)
+            for t, groups_of in enumerate((lower, middle, upper)):
+                moved = groups_of if a == 1 else pltpu.roll(groups_of, (16 - 16 * a) % LANES, 1)
                 here = lax.rem(lane, half)
                 part = slice(8 * t, 8 * t + 8)
                 cells[a][p_to, 0, part, :] = jnp.where((here >= 24) & (here < 40), moved, ends[a, p_to, part, :])

time: 19.5 us -> 19 us (0.974)
  Pallas kernels: 7.11 us -> 6.68 us
    pallas_call x1, Pallas kernels: 2.74 us -> 2.45 us  [shards(): pl.pallas_call(functools.partial(edges, reflect), out_shape=block, in_spe...]
  transfers between devices with their start and end apart: 7 -> 7, of which waited for: 4 -> 4; matrix products, arithmetic and copies ran while one was open for 0% -> 0% of each run, Pallas kernels for 13% -> 14%
where the time goes in v10:
time: 19 us; the launch traced here: 18.9 us
  Pallas kernels  6.68 us (35%)
  waiting for transfers between devices  6.65 us (35%)
  starting transfers between devices  5.48 us (29%)
    ppermute x7, waiting for transfers between devices, exchange(): lax.ppermute(v, over, pairs)  6.65 us
    ppermute x7, starting transfers between devices, exchange(): lax.ppermute(v, over, pairs)  5.48 us
    pallas_call x1, Pallas kernels, shards(): pl.pallas_call(functools.partial(interior, reflect, n_x), out_shape=(bloc...  2.59 us
    pallas_call x1, Pallas kernels, shards(): pl.pallas_call(functools.partial(edges, reflect), out_shape=block, in_spe...  2.45 us
    pallas_call x1, Pallas kernels, shards(): pl.pallas_call(functools.partial(prepare, reflect), out_shape=(jax.ShapeD...  1.33 us
  transfers between devices with their start and end apart: 7, of which 4 were waited for; matrix products, arithmetic and copies ran while one was open for 0% of the time, Pallas kernels for 14%

profile of v10, /device:TPU:18, one launch (start us, length us, event | category | flops | bytes accessed | tf_op | source)
XLA Modules:
  0.0 18.9 jit_solution(8219345772330419522)
XLA Ops:
  0.0 1.3 %prepare.1 = (f32[3,8,16,256]{3,2,1,0:T(8,128)S(1)}, f32[14,8,256]{2,1,0:T(8,128)S(1)}, f32[14,8,256]{2,1,0:T(8,128)S(1)}) custom-call(f32[8,16,256]{2,1,0:T(8,128)} %s.1, f32[8,16,256]{2,1,0:T(8,128)} %c.1, f32[8,16,256]{2,1,0:T(8,128)} %f.1), custom_call_target="tpu_custom_call" | custom-call | tf_op jit(solution)/shard_map/prepare/pallas_call | solution.py:522
  1.3 1.6 %collective-permute-start = (f32[14,8,256]{2,1,0:T(8,128)S(1)}, f32[14,8,256]{2,1,0:T(8,128)S(1)}, u32[]{:S(2)}, u32[]{:S(2)}) collective-permute-start(f32[14,8,256]{2,1,0:T(8,128)S(1)} %get-tuple-element.19), channel_id=1, source_target_pairs={{0,1},{4,5},{2,3},{6,7},{1,0},{5,4},{3,2},{7,6},{8,9},{12,13},{10,... | collective-permute-start | bytes 344072 | tf_op jit(solution)/shard_map/ppermute | solution.py:509
  3.0 0.0 collective-permute-start.1
  3.0 3.3 %collective-permute-done.got_a = f32[14,8,256]{2,1,0:T(8,128)S(1)} collective-permute-done((f32[14,8,256]{2,1,0:T(8,128)S(1)}, f32[14,8,256]{2,1,0:T(8,128)S(1)}, u32[]{:S(2)}, u32[]{:S(2)}) %collective-permute-start) | collective-permute-done | bytes 114720 | tf_op jit(solution)/shard_map/ppermute | solution.py:509
  6.3 1.5 %collective-permute-done.1.got_b = f32[14,8,256]{2,1,0:T(8,128)S(1)} collective-permute-done((f32[14,8,256]{2,1,0:T(8,128)S(1)}, f32[14,8,256]{2,1,0:T(8,128)S(1)}, u32[]{:S(2)}, u32[]{:S(2)}) %collective-permute-start.1) | collective-permute-done | bytes 114720 | tf_op jit(solution)/shard_map/ppermute | solution.py:509
  7.8 0.3 %pack_columns.1 = (f32[2,8,8,128]{3,2,1,0:T(8,128)S(1)}, f32[2,3,8,8,256]{4,3,2,1,0:T(8,128)S(1)}) custom-call(f32[3,8,16,256]{3,2,1,0:T(8,128)S(1)} %get-tuple-element.18.own.refs_0_, f32[14,8,256]{2,1,0:T(8,128)S(1)} %collective-permute-done.got_a, f32[14,8,256]{2,1,0:T(8,128)S(1)} %collective-permute-done.1.got_b), custom_call_target="tpu_custom_call" | custom-call | tf_op jit(solution)/shard_map/pack_columns/pallas_call | solution.py:530
  8.1 0.1 collective-permute-start.2
  8.2 0.5 %collective-permute-start.3 = (f32[3,8,16,256]{3,2,1,0:T(8,128)S(1)}, f32[3,8,16,256]{3,2,1,0:T(8,128)S(1)}, u32[]{:S(2)}, u32[]{:S(2)}) collective-permute-start(f32[3,8,16,256]{3,2,1,0:T(8,128)S(1)} %get-tuple-element.18.own.refs_0_), channel_id=1, source_target_pairs={{0,4},{4,0},{1,5},{5,1},{2,6},{6,2},{3,7},{7,3},{8,12},{12,8},{9,1... | collective-permute-start | bytes 1179656 | tf_op jit(solution)/shard_map/ppermute | solution.py:509
  8.7 0.7 %collective-permute-done.2 = f32[2,8,8,128]{3,2,1,0:T(8,128)S(1)} collective-permute-done((f32[2,8,8,128]{3,2,1,0:T(8,128)S(1)}, f32[2,8,8,128]{3,2,1,0:T(8,128)S(1)}, u32[]{:S(2)}, u32[]{:S(2)}) %collective-permute-start.2) | collective-permute-done | bytes 65568 | tf_op jit(solution)/shard_map/ppermute | solution.py:509
  9.4 0.2 %collective-permute-start.4 = (f32[2,3,8,8,256]{4,3,2,1,0:T(8,128)S(1)}, f32[2,3,8,8,256]{4,3,2,1,0:T(8,128)S(1)}, u32[]{:S(2)}, u32[]{:S(2)}) collective-permute-start(f32[2,3,8,8,256]{4,3,2,1,0:T(8,128)S(1)} %get-tuple-element.23.refs_1_), channel_id=1, source_target_pairs={{0,4},{4,0},{1,5},{5,1},{2,6},{6,2},{3,7},{7,3},{8,12},{12,8},{9,1... | collective-permute-start | bytes 1179656 | tf_op jit(solution)/shard_map/ppermute | solution.py:509
  9.7 0.6 %collective-permute-start.6 = (f32[16,8,128]{2,1,0:T(8,128)S(1)}, f32[16,8,128]{2,1,0:T(8,128)S(1)}, u32[]{:S(2)}, u32[]{:S(2)}) collective-permute-start(f32[16,8,128]{2,1,0:T(8,128)S(1)} %get-tuple-element.31), channel_id=1, source_target_pairs={{0,8},{4,12},{16,24},{20,28},{8,0},{12,4},{24,16},{28,20},{1,9},{5... | collective-permute-start | bytes 196616 | tf_op jit(solution)/shard_map/ppermute | solution.py:509
  10.3 2.4 %collective-permute-start.5 = (f32[16,8,128]{2,1,0:T(8,128)S(1)}, f32[16,8,128]{2,1,0:T(8,128)S(1)}, u32[]{:S(2)}, u32[]{:S(2)}) collective-permute-start(f32[16,8,128]{2,1,0:T(8,128)S(1)} %get-tuple-element.32), channel_id=1, source_target_pairs={{8,16},{12,20},{0,4},{24,28},{16,8},{20,12},{4,0},{28,24},{9,17},{... | collective-permute-start | bytes 196616 | tf_op jit(solution)/shard_map/ppermute | solution.py:509
  12.7 0.0 collective-permute-done.3.refs_2_
  12.7 0.0 collective-permute-done.4.refs_3_
  12.7 2.6 %interior.1 = (f32[8,16,256]{2,1,0:T(8,128)S(1)}, f32[3,18,24,128]{3,2,1,0:T(8,128)S(1)}) custom-call(f32[3,8,16,256]{3,2,1,0:T(8,128)S(1)} %get-tuple-element.18.own.refs_0_, f32[2,3,8,8,256]{4,3,2,1,0:T(8,128)S(1)} %get-tuple-element.23.refs_1_, f32[3,8,16,256]{3,2,1,0:T(8,128)S(1)} %collective-permute-done.3.refs_2_, ...), custom_call_target="tpu_custom_call" | custom-call | flops 20000000 | bytes 20000000 | tf_op jit(solution)/shard_map/interior/pallas_call | solution.py:548
  15.3 0.0 collective-permute-done.6.got_a
  15.3 1.1 %collective-permute-done.5.got_b = f32[16,8,128]{2,1,0:T(8,128)S(1)} collective-permute-done((f32[16,8,128]{2,1,0:T(8,128)S(1)}, f32[16,8,128]{2,1,0:T(8,128)S(1)}, u32[]{:S(2)}, u32[]{:S(2)}) %collective-permute-start.5) | collective-permute-done | bytes 65568 | tf_op jit(solution)/shard_map/ppermute | solution.py:509
  16.4 2.4 %edges.1 = f32[8,16,256]{2,1,0:T(8,128)} custom-call(f32[3,18,24,128]{3,2,1,0:T(8,128)S(1)} %get-tuple-element.27.ends, f32[8,16,256]{2,1,0:T(8,128)S(1)} %get-tuple-element.28.inside, f32[16,8,128]{2,1,0:T(8,128)S(1)} %collective-permute-done.6.got_a, f32[16,8,128]{2,1,0:T(8,128)S(1)} %collective-permute-done.5.got_b), custom_call_target="tpu_custom_call" | custom-call | tf_op jit(solution)/shard_map/edges/pallas_call | solution.py:557
  (2 shorter events, 0.0 us)
Async XLA Ops:
  1.3 5.0 %collective-permute-start = (f32[14,8,256]{2,1,0:T(8,128)S(1)}, f32[14,8,256]{2,1,0:T(8,128)S(1)}, u32[]{:S(2)}, u32[]{:S(2)}) collective-permute-start(f32[14,8,256]{2,1,0:T(8,128)S(1)} %get-tuple-element.19), channel_id=1, source_target_pairs={{0,1},{4,5},{2,3},{6,7},{1,0},{5,4},{3,2},{7,6},{8,9},{12,13},{10,... | collective-permute-start | bytes 344072 | tf_op jit(solution)/shard_map/ppermute | solution.py:509
  3.0 4.8 %collective-permute-start.1 = (f32[14,8,256]{2,1,0:T(8,128)S(1)}, f32[14,8,256]{2,1,0:T(8,128)S(1)}, u32[]{:S(2)}, u32[]{:S(2)}) collective-permute-start(f32[14,8,256]{2,1,0:T(8,128)S(1)} %get-tuple-element.20), channel_id=1, source_target_pairs={{1,2},{5,6},{0,4},{3,7},{2,1},{6,5},{4,0},{7,3},{9,10},{13,14},{8,... | collective-permute-start | bytes 344072 | tf_op jit(solution)/shard_map/ppermute | solution.py:509
  8.1 1.3 %collective-permute-start.2 = (f32[2,8,8,128]{3,2,1,0:T(8,128)S(1)}, f32[2,8,8,128]{3,2,1,0:T(8,128)S(1)}, u32[]{:S(2)}, u32[]{:S(2)}) collective-permute-start(f32[2,8,8,128]{3,2,1,0:T(8,128)S(1)} %get-tuple-element.21), channel_id=1, source_target_pairs={{0,4},{4,0},{1,5},{5,1},{2,6},{6,2},{3,7},{7,3},{8,12},{12,8},{9,1... | collective-permute-start | bytes 196616 | tf_op jit(solution)/shard_map/ppermute | solution.py:509
  8.2 4.5 %collective-permute-start.3 = (f32[3,8,16,256]{3,2,1,0:T(8,128)S(1)}, f32[3,8,16,256]{3,2,1,0:T(8,128)S(1)}, u32[]{:S(2)}, u32[]{:S(2)}) collective-permute-start(f32[3,8,16,256]{3,2,1,0:T(8,128)S(1)} %get-tuple-element.18.own.refs_0_), channel_id=1, source_target_pairs={{0,4},{4,0},{1,5},{5,1},{2,6},{6,2},{3,7},{7,3},{8,12},{12,8},{9,1... | collective-permute-start | bytes 1179656 | tf_op jit(solution)/shard_map/ppermute | solution.py:509
  9.4 3.3 %collective-permute-start.4 = (f32[2,3,8,8,256]{4,3,2,1,0:T(8,128)S(1)}, f32[2,3,8,8,256]{4,3,2,1,0:T(8,128)S(1)}, u32[]{:S(2)}, u32[]{:S(2)}) collective-permute-start(f32[2,3,8,8,256]{4,3,2,1,0:T(8,128)S(1)} %get-tuple-element.23.refs_1_), channel_id=1, source_target_pairs={{0,4},{4,0},{1,5},{5,1},{2,6},{6,2},{3,7},{7,3},{8,12},{12,8},{9,1... | collective-permute-start | bytes 1179656 | tf_op jit(solution)/shard_map/ppermute | solution.py:509
  9.7 5.7 %collective-permute-start.6 = (f32[16,8,128]{2,1,0:T(8,128)S(1)}, f32[16,8,128]{2,1,0:T(8,128)S(1)}, u32[]{:S(2)}, u32[]{:S(2)}) collective-permute-start(f32[16,8,128]{2,1,0:T(8,128)S(1)} %get-tuple-element.31), channel_id=1, source_target_pairs={{0,8},{4,12},{16,24},{20,28},{8,0},{12,4},{24,16},{28,20},{1,9},{5... | collective-permute-start | bytes 196616 | tf_op jit(solution)/shard_map/ppermute | solution.py:509
  10.3 6.2 %collective-permute-start.5 = (f32[16,8,128]{2,1,0:T(8,128)S(1)}, f32[16,8,128]{2,1,0:T(8,128)S(1)}, u32[]{:S(2)}, u32[]{:S(2)}) collective-permute-start(f32[16,8,128]{2,1,0:T(8,128)S(1)} %get-tuple-element.32), channel_id=1, source_target_pairs={{8,16},{12,20},{0,4},{24,28},{16,8},{20,12},{4,0},{28,24},{9,17},{... | collective-permute-start | bytes 196616 | tf_op jit(solution)/shard_map/ppermute | solution.py:509

commit v11 on v10

--- a/solution.py
+++ b/solution.py
@@ -89,18 +89,19 @@
     row = lax.broadcasted_iota(jnp.int32, (inner, width), 0)
     column = lax.broadcasted_iota(jnp.int32, (inner, width), 1)
     outer = jnp.where(is_odd("gx") == 1, depth - 1, 0)
-    for p in range(depth):
-        cond, field = own[1, p], own[2, p]
-
-        def flux(axis):
-            return (cond + ahead(cond, axis)) * (field - ahead(field, axis))
-
-        along_y = jnp.where(row < inner - 1, flux(0), 0.0)
-        along_z = jnp.where(column < width - 1, flux(1), 0.0)
-        total = (along_y - behind(along_y, 0)) + (along_z - behind(along_z, 1))
+    conds, fields = ([own[a, p] for p in range(depth)] for a in (1, 2))
+    next_conds, next_fields = ([ahead(v, 1) for v in values] for values in (conds, fields))
+    along_z = [
+        jnp.where(column < width - 1, (c + c_next) * (f - f_next), 0.0)
+        for c, f, c_next, f_next in zip(conds, fields, next_conds, next_fields)
+    ]
+    arriving = [behind(v, 1) for v in along_z]
+    for p, (cond, field) in enumerate(zip(conds, fields)):
+        along_y = jnp.where(row < inner - 1, (cond + ahead(cond, 0)) * (field - ahead(field, 0)), 0.0)
+        total = (along_y - behind(along_y, 0)) + (along_z[p] - arriving[p])
         for other in (p - 1, p + 1):
             if 0 <= other < depth:
-                total += (cond + own[1, other]) * (field - own[2, other])
+                total += (cond + conds[other]) * (field - fields[other])
         if reflect and p in (0, depth - 1):
             total += jnp.where(outer == p, cond * field, 0.0)
         own[0, p] = 2.0 * own[0, p] - total
@@ -185,7 +186,8 @@
             rim[side, 0, p] = g
             rim[side, 1, p] = cond
             rim[side, 2, p] = field
-        head = tail = jnp.zeros((8, LANES), jnp.float32)
+    moved = {}
+    for p in range(depth):
         for a in range(3):
             for g in range(groups):
                 if g == 0 or g == groups - 1:
@@ -194,12 +196,18 @@
                     rows = own[a, p, 8 * g - 8 : 8 * g, :]
                 to_head, to_tail = head_lane(a, g), tail_lane(a, g)
                 if to_head == to_tail + HALO:
-                    first_moved = last_moved = pltpu.roll(both_ends(rows), to_head, 1)
+                    ends = pltpu.roll(both_ends(rows), to_head, 1)
+                    moved[p, a, g] = ends, ends
                 else:
-                    first_moved = pltpu.roll(rows[:, 0:LANES], to_head, 1)
-                    last_moved = pltpu.roll(rows[:, width - LANES : width], (to_tail + HALO) % LANES, 1)
-                head = jnp.where((lane >= to_head) & (lane < to_head + HALO), first_moved, head)
-                tail = jnp.where((lane >= to_tail) & (lane < to_tail + HALO), last_moved, tail)
+                    last = pltpu.roll(rows[:, width - LANES : width], (to_tail + HALO) % LANES, 1)
+                    moved[p, a, g] = pltpu.roll(rows[:, 0:LANES], to_head, 1), last
+    for p in range(depth):
+        head = tail = jnp.zeros((8, LANES), jnp.float32)
+        for a in range(3):
+            for g in range(groups):
+                to_head, to_tail = head_lane(a, g), tail_lane(a, g)
+                head = jnp.where((lane >= to_head) & (lane < to_head + HALO), moved[p, a, g][0], head)
+                tail = jnp.where((lane >= to_tail) & (lane < to_tail + HALO), moved[p, a, g][1], tail)
         strips[0, p] = jnp.where(odd_z == 1, head, tail)
         strips[1, p] = jnp.where(odd_z == 1, tail, head)
 
@@ -247,47 +255,58 @@
     even_row = lax.rem(lax.broadcasted_iota(jnp.int32, (rows, lanes), 0), 2) == 0
     even_lane = lax.rem(lax.broadcasted_iota(jnp.int32, (rows, lanes), 1), 2) == 0
 
-    def gather(v):
-        t = v[0] + (v[1] if parts == 2 else ahead(v[0], 1))
-        return [t + ahead(t, 0)]
-
-    for k in reach(HALO):
-        store(sum8, k, gather(add(load(cond, 2 * k - 1), load(cond, 2 * k))))
-
-    def weights(ref, p, level):
-        step, ahead_z, behind_z = level
+    def turned(ref, planes, level):
+        here = {p: load(ref, p) for p in planes}
+        return {p: (level[1](v), level[2](v)) for p, v in here.items()}
+
+    def planes_of(blocks):
+        return [p for k in blocks for p in (2 * k - 1, 2 * k)]
+
+    def gather(sums):
+        sums = {k: [v[0] + ahead(v[0], 0)] if parts == 1 else [v[0] + v[1]] for k, v in sums.items()}
+        if parts == 1:
+            return {k: [v[0] + u] for (k, v), u in zip(sums.items(), [ahead(v[0], 1) for v in sums.values()])}
+        return {k: [v[0] + ahead(v[0], 0)] for k, v in sums.items()}
+
+    for k, v in gather({k: add(load(cond, 2 * k - 1), load(cond, 2 * k)) for k in reach(HALO)}).items():
+        store(sum8, k, v)
+
+    def weights(ref, p, level, around_z):
+        step = level[0]
         c = load(ref, p)
         x = add(c, load(ref, p + 1))
         y, yb = ([v + shift(v, 0, step) for v in c] for shift in (ahead, behind))
-        z, zb = add(c, ahead_z(c)), add(c, behind_z(c))
+        z, zb = (add(c, v) for v in around_z)
         k = add(add(c, load(ref, p - 1), x), add(y, yb), add(z, zb))
         return x, y, z, yb, zb, k, each(lambda v, w: jnp.where(v > 0.0, 1.0 / w, 0.0), c, k)
 
     low = reach(HALO - 2).start
     store(wx, 2 * low - 2, add(load(cond, 2 * low - 2), load(cond, 2 * low - 1)))
     store(cwx, low - 1, add(load(sum8, low - 1), load(sum8, low)))
+    z_fine = turned(cond, planes_of(reach(HALO - 2)), fine)
+    z_coarse = turned(sum8, reach(HALO - 2), coarse)
     for k in reach(HALO - 2):
         for p in (2 * k - 1, 2 * k):
-            for ref, v in zip((wx, wy, wz, vy, vz, diag, inv), weights(cond, p, fine)):
+            for ref, v in zip((wx, wy, wz, vy, vz, diag, inv), weights(cond, p, fine, z_fine[p])):
                 store(ref, p, v)
-        for ref, v in zip((cwx, cwy, cwz, cvy, cvz, None, cinv), weights(sum8, k, coarse)):
+        for ref, v in zip((cwx, cwy, cwz, cvy, cvz, None, cinv), weights(sum8, k, coarse, z_coarse[k])):
             if ref is not None:
                 store(ref, k, v)
 
-    def spread(v, p, refs, level):
+    def spread(v, p, refs, level, around_z):
         x, y, z, yb, zb = refs
-        step, ahead_z, behind_z = level
+        step = level[0]
         here = load(v, p)
         n = add(times(load(x, p - 1), load(v, p - 1)), times(load(x, p), load(v, p + 1)))
         n = add(n, times(load(y, p), [ahead(u, 0, step) for u in here]))
         n = add(n, times(load(yb, p), [behind(u, 0, step) for u in here]))
-        return add(n, add(times(load(z, p), ahead_z(here)), times(load(zb, p), behind_z(here))))
-
-    def smooth(v, p, refs, scale, level):
-        n = times(load(scale, p), spread(v, p, refs, level))
+        return add(n, add(times(load(z, p), around_z[0]), times(load(zb, p), around_z[1])))
+
+    def smooth(v, p, refs, scale, level, around_z):
+        n = times(load(scale, p), spread(v, p, refs, level, around_z))
         return each(lambda u, w: KEEP * u + SPREAD * w, load(v, p), n)
 
-    def between(p):
+    def between(p, around_z):
         planes, along_y, along_z = seams
         here = load(field, p)
         r = load(src, p)
@@ -303,35 +322,45 @@
         r = less(r, load(wy, p), [ahead(v, 0) for v in here], along_y[0])
         r = less(r, load(vy, p), [behind(v, 0) for v in here], along_y[1])
         if along_z is not None:
-            r = less(r, load(wz, p), fine[1](here), along_z[0])
-            r = less(r, load(vz, p), fine[2](here), along_z[1])
+            r = less(r, load(wz, p), around_z[0], along_z[0])
+            r = less(r, load(vz, p), around_z[1], along_z[1])
         return r
 
     around, coarse_around = (wx, wy, wz, vy, vz), (cwx, cwy, cwz, cvy, cvz)
 
     for it in range(ITERS):
         halo = 4 * (ITERS - 1 - it)
-        for k in reach(halo + 2):
+        blocks = reach(halo + 2)
+        rounds = turned(err if it else field, planes_of(blocks), fine) if it or seams[2] is not None else {}
+        sums = {}
+        for k in blocks:
             found = []
             for p in (2 * k - 1, 2 * k):
                 if it == 0:
-                    r = between(p)
+                    r = between(p, rounds.get(p))
                 else:
-                    n = spread(err, p, around, fine)
+                    n = spread(err, p, around, fine, rounds[p])
                     r = each(lambda u, d, w, m: u - (d * w - m), load(res, p), load(diag, p), load(err, p), n)
                 if it < ITERS - 1:
                     store(res, p, r)
                 store(q, p, times(r, load(inv, p)))
                 found.append(r)
-            store(cq, k, times([4.0 * gather(add(*found))[0]], load(cinv, k)))
-
-        for k in reach(halo):
-            (c,) = smooth(cq, k, coarse_around, cinv, coarse)
-            if parts == 1:
-                c = jnp.where(even_lane, c, behind(c, 1))
-            c = jnp.where(even_row, c, behind(c, 0))
+            sums[k] = add(*found)
+        near = reach(halo)
+        sums = gather(sums)
+        rounds = turned(q, planes_of(near), fine)
+        for k, v in sums.items():
+            store(cq, k, times([4.0 * v[0]], load(cinv, k)))
+        coarse_rounds = turned(cq, near, coarse)
+        found = {k: smooth(cq, k, coarse_around, cinv, coarse, coarse_rounds[k])[0] for k in near}
+        if parts == 1:
+            beside = {k: behind(c, 1) for k, c in found.items()}
+            found = {k: jnp.where(even_lane, c, beside[k]) for k, c in found.items()}
+        smoothed = {p: smooth(q, p, around, inv, fine, rounds[p]) for p in planes_of(near)}
+        for k in near:
+            c = jnp.where(even_row, found[k], behind(found[k], 0))
             for p in (2 * k - 1, 2 * k):
-                e = [u + c for u in smooth(q, p, around, inv, fine)]
+                e = [u + c for u in smoothed[p]]
                 if it:
                     e = add(load(err, p), e)
                 if it < ITERS - 1:
@@ -443,9 +472,8 @@
         result[out_plane(reflect, depth, own_at + p)] = together[p]
 
 
-def edges(reflect, ends, inside, got_a, got_b, result, *cells):
+def edges(reflect, ends, inside, got_a, got_b, result, staged, sems, *cells):
     depth, inner, width = inside.shape
-    groups = ends.shape[2] // 8
     odd_z = is_odd("grp")
     first_z, last_z = beyond("grp")
     lane = lax.broadcasted_iota(jnp.int32, (8, LANES), 1)
@@ -455,45 +483,57 @@
         for a in range(3):
             cells[a][p, 0] = ends[a, p]
 
+    windows = []
+
     def place(i, p_from, p_to):
         at_plane = p_from if i is None else (i + 1) * depth + p_from
         va, vb = got_a[at_plane], got_b[at_plane]
         right = jnp.where(last_z, 0.0, jnp.where(odd_z == 1, vb, va))
         left = jnp.where(first_z, 0.0, jnp.where(odd_z == 1, va, vb))
-        side = lax.rem(lane, 16) >= 8
-        lower = jnp.where(side, right, left)
-        upper = jnp.where(side, pltpu.roll(right, LANES - 8, 1), pltpu.roll(left, 8, 1))
-        middle = pltpu.roll(jnp.where(lane < half, upper, lower), half, 1)
-        for a in range(3):
-            for t, groups_of in enumerate((lower, middle, upper)):
-                moved = groups_of if a == 1 else pltpu.roll(groups_of, (16 - 16 * a) % LANES, 1)
-                here = lax.rem(lane, half)
+        windows.append((p_to, right, left, pltpu.roll(right, LANES - 8, 1), pltpu.roll(left, 8, 1)))
+
+    here = lax.rem(lane, half)
+    in_halo = (here >= 24) & (here < 40)
+    each_plane(reflect, depth, place)
+    side = lax.rem(lane, 16) >= 8
+    groups = []
+    for p, right, left, right_moved, left_moved in windows:
+        lower, upper = jnp.where(side, right, left), jnp.where(side, right_moved, left_moved)
+        groups.append((p, lower, pltpu.roll(jnp.where(lane < half, upper, lower), half, 1), upper))
+    for a in (1, 0, 2):
+        for p, *tiles in groups:
+            for t, tile in enumerate(tiles):
+                moved = tile if a == 1 else pltpu.roll(tile, (16 - 16 * a) % LANES, 1)
                 part = slice(8 * t, 8 * t + 8)
-                cells[a][p_to, 0, part, :] = jnp.where((here >= 24) & (here < 40), moved, ends[a, p_to, part, :])
-
-    each_plane(reflect, depth, place)
-
-    def out(p, v):
-        at = out_plane(reflect, depth, p)
-        v = v[0][8:16]
-        for i in range(2):
-            part = slice(8 * i, 8 * i + 8)
-            head = pltpu.roll(v, (LANES - 40 - half * i) % LANES, 1)
-            tail = pltpu.roll(v, (LANES - 24 - half * i) % LANES, 1)
-            for c in range(0, width, LANES):
-                tile = inside[at, part, c : c + LANES]
-                if c == 0:
-                    tile = jnp.where(lane < HALO, head, tile)
-                if c == width - LANES:
-                    tile = jnp.where(lane >= LANES - HALO, tail, tile)
-                result[at, part, c : c + LANES] = tile
+                cells[a][p, 0, part, :] = jnp.where(in_halo, moved, ends[a, p, part, :])
 
     row = lax.broadcasted_iota(jnp.int32, ends.shape[2:], 0)
     lane_in_half = lax.rem(lax.broadcasted_iota(jnp.int32, ends.shape[2:], 1), half)
     upper_half = lax.broadcasted_iota(jnp.int32, ends.shape[2:], 1) >= half
     face = jnp.where(upper_half, inner, HALO)
     along_z = tuple((lane_in_half == at) | (lane_in_half == at + 16) for at in (23, 24))
-    solve(cells, own_at, depth, out, (x_seams(reflect, depth), (row == face - 1, row == face), along_z))
+    finals = []
+    solve(cells, own_at, depth, lambda p, v: finals.append((p - own_at, v[0][8:16])), (x_seams(reflect, depth), (row == face - 1, row == face), along_z))
+    moved = [
+        (p, i, pltpu.roll(v, (LANES - 40 - half * i) % LANES, 1), pltpu.roll(v, (LANES - 24 - half * i) % LANES, 1))
+        for p, v in finals
+        for i in range(2)
+    ]
+    copies = []
+    for p, i, head, tail in moved:
+        at, part = out_plane(reflect, depth, own_at + p), slice(8 * i, 8 * i + 8)
+        for c in range(0, width, LANES):
+            tile = inside[at, part, c : c + LANES]
+            if c == 0:
+                tile = jnp.where(lane < HALO, head, tile)
+            if c == width - LANES:
+                tile = jnp.where(lane >= LANES - HALO, tail, tile)
+            staged[p, part, c : c + LANES] = tile
+        if i:
+            copies.append(pltpu.make_async_copy(staged.at[p], result.at[at], sems.at[p]))
+            copies[-1].start()
+    for copy in copies:
+        copy.wait()
 
 
 def shards(sizes, source_term, conductivity, initial_field):
@@ -557,7 +597,8 @@
     return pl.pallas_call(
         functools.partial(edges, reflect),
         out_shape=block,
-        in_specs=[VMEM] * 4, out_specs=VMEM, scratch_shapes=work(1, rows - 8, LANES),
+        in_specs=[VMEM] * 4, out_specs=pl.BlockSpec(memory_space=pltpu.HBM),
+        scratch_shapes=[pltpu.VMEM((depth, inner, width), f32), pltpu.SemaphoreType.DMA((depth,))] + work(1, rows - 8, LANES),
         compiler_params=params, name="edges",
     )(ends, inside, *strips)
 

time: 19 us -> 18.4 us (0.968)
  Pallas kernels: 6.68 us -> 6.06 us
    pallas_call x1, Pallas kernels: 2.45 us -> 1.87 us  [shards(): pl.pallas_call(functools.partial(edges, reflect), out_shape=block, in_spe...]
where the time goes in v11:
time: 18.4 us; the launch traced here: 18.2 us
  waiting for transfers between devices  6.64 us (36%)
  Pallas kernels  6.06 us (33%)
  starting transfers between devices  5.48 us (30%)
    ppermute x7, waiting for transfers between devices, exchange(): lax.ppermute(v, over, pairs)  6.64 us
    ppermute x7, starting transfers between devices, exchange(): lax.ppermute(v, over, pairs)  5.48 us
    pallas_call x1, Pallas kernels, shards(): pl.pallas_call(functools.partial(interior, reflect, n_x), out_shape=(bloc...  2.6 us
    pallas_call x1, Pallas kernels, shards(): pl.pallas_call(functools.partial(edges, reflect), out_shape=block, in_spe...  1.87 us
    pallas_call x1, Pallas kernels, shards(): pl.pallas_call(functools.partial(prepare, reflect), out_shape=(jax.ShapeD...  1.34 us
  transfers between devices with their start and end apart: 7, of which 4 were waited for; matrix products, arithmetic and copies ran while one was open for 0% of the time, Pallas kernels for 14%

profile of v11, /device:TPU:18, one launch (start us, length us, event | category | flops | bytes accessed | tf_op | source)
XLA Modules:
  0.0 18.2 jit_solution(9978775333660457091)
XLA Ops:
  0.0 1.3 %prepare.1 = (f32[3,8,16,256]{3,2,1,0:T(8,128)S(1)}, f32[14,8,256]{2,1,0:T(8,128)S(1)}, f32[14,8,256]{2,1,0:T(8,128)S(1)}) custom-call(f32[8,16,256]{2,1,0:T(8,128)} %s.1, f32[8,16,256]{2,1,0:T(8,128)} %c.1, f32[8,16,256]{2,1,0:T(8,128)} %f.1), custom_call_target="tpu_custom_call" | custom-call | tf_op jit(solution)/shard_map/prepare/pallas_call | solution.py:562
  1.3 1.6 %collective-permute-start = (f32[14,8,256]{2,1,0:T(8,128)S(1)}, f32[14,8,256]{2,1,0:T(8,128)S(1)}, u32[]{:S(2)}, u32[]{:S(2)}) collective-permute-start(f32[14,8,256]{2,1,0:T(8,128)S(1)} %get-tuple-element.19), channel_id=1, source_target_pairs={{0,1},{4,5},{2,3},{6,7},{1,0},{5,4},{3,2},{7,6},{8,9},{12,13},{10,... | collective-permute-start | bytes 344072 | tf_op jit(solution)/shard_map/ppermute | solution.py:549
  3.0 0.0 collective-permute-start.1
  3.0 3.3 %collective-permute-done.got_a = f32[14,8,256]{2,1,0:T(8,128)S(1)} collective-permute-done((f32[14,8,256]{2,1,0:T(8,128)S(1)}, f32[14,8,256]{2,1,0:T(8,128)S(1)}, u32[]{:S(2)}, u32[]{:S(2)}) %collective-permute-start) | collective-permute-done | bytes 114720 | tf_op jit(solution)/shard_map/ppermute | solution.py:549
  6.3 1.5 %collective-permute-done.1.got_b = f32[14,8,256]{2,1,0:T(8,128)S(1)} collective-permute-done((f32[14,8,256]{2,1,0:T(8,128)S(1)}, f32[14,8,256]{2,1,0:T(8,128)S(1)}, u32[]{:S(2)}, u32[]{:S(2)}) %collective-permute-start.1) | collective-permute-done | bytes 114720 | tf_op jit(solution)/shard_map/ppermute | solution.py:549
  7.8 0.2 %pack_columns.1 = (f32[2,8,8,128]{3,2,1,0:T(8,128)S(1)}, f32[2,3,8,8,256]{4,3,2,1,0:T(8,128)S(1)}) custom-call(f32[3,8,16,256]{3,2,1,0:T(8,128)S(1)} %get-tuple-element.18.own.refs_0_, f32[14,8,256]{2,1,0:T(8,128)S(1)} %collective-permute-done.got_a, f32[14,8,256]{2,1,0:T(8,128)S(1)} %collective-permute-done.1.got_b), custom_call_target="tpu_custom_call" | custom-call | tf_op jit(solution)/shard_map/pack_columns/pallas_call | solution.py:570
  8.0 0.1 collective-permute-start.2
  8.1 0.5 %collective-permute-start.3 = (f32[3,8,16,256]{3,2,1,0:T(8,128)S(1)}, f32[3,8,16,256]{3,2,1,0:T(8,128)S(1)}, u32[]{:S(2)}, u32[]{:S(2)}) collective-permute-start(f32[3,8,16,256]{3,2,1,0:T(8,128)S(1)} %get-tuple-element.18.own.refs_0_), channel_id=1, source_target_pairs={{0,4},{4,0},{1,5},{5,1},{2,6},{6,2},{3,7},{7,3},{8,12},{12,8},{9,1... | collective-permute-start | bytes 1179656 | tf_op jit(solution)/shard_map/ppermute | solution.py:549
  8.6 0.7 %collective-permute-done.2 = f32[2,8,8,128]{3,2,1,0:T(8,128)S(1)} collective-permute-done((f32[2,8,8,128]{3,2,1,0:T(8,128)S(1)}, f32[2,8,8,128]{3,2,1,0:T(8,128)S(1)}, u32[]{:S(2)}, u32[]{:S(2)}) %collective-permute-start.2) | collective-permute-done | bytes 65568 | tf_op jit(solution)/shard_map/ppermute | solution.py:549
  9.4 0.2 %collective-permute-start.4 = (f32[2,3,8,8,256]{4,3,2,1,0:T(8,128)S(1)}, f32[2,3,8,8,256]{4,3,2,1,0:T(8,128)S(1)}, u32[]{:S(2)}, u32[]{:S(2)}) collective-permute-start(f32[2,3,8,8,256]{4,3,2,1,0:T(8,128)S(1)} %get-tuple-element.23.refs_1_), channel_id=1, source_target_pairs={{0,4},{4,0},{1,5},{5,1},{2,6},{6,2},{3,7},{7,3},{8,12},{12,8},{9,1... | collective-permute-start | bytes 1179656 | tf_op jit(solution)/shard_map/ppermute | solution.py:549
  9.6 0.6 %collective-permute-start.6 = (f32[16,8,128]{2,1,0:T(8,128)S(1)}, f32[16,8,128]{2,1,0:T(8,128)S(1)}, u32[]{:S(2)}, u32[]{:S(2)}) collective-permute-start(f32[16,8,128]{2,1,0:T(8,128)S(1)} %get-tuple-element.31), channel_id=1, source_target_pairs={{0,8},{4,12},{16,24},{20,28},{8,0},{12,4},{24,16},{28,20},{1,9},{5... | collective-permute-start | bytes 196616 | tf_op jit(solution)/shard_map/ppermute | solution.py:549
  10.2 2.4 %collective-permute-start.5 = (f32[16,8,128]{2,1,0:T(8,128)S(1)}, f32[16,8,128]{2,1,0:T(8,128)S(1)}, u32[]{:S(2)}, u32[]{:S(2)}) collective-permute-start(f32[16,8,128]{2,1,0:T(8,128)S(1)} %get-tuple-element.32), channel_id=1, source_target_pairs={{8,16},{12,20},{0,4},{24,28},{16,8},{20,12},{4,0},{28,24},{9,17},{... | collective-permute-start | bytes 196616 | tf_op jit(solution)/shard_map/ppermute | solution.py:549
  12.6 0.0 collective-permute-done.3.refs_2_
  12.6 0.0 collective-permute-done.4.refs_3_
  12.7 2.6 %interior.1 = (f32[8,16,256]{2,1,0:T(8,128)S(1)}, f32[3,18,24,128]{3,2,1,0:T(8,128)S(1)}) custom-call(f32[3,8,16,256]{3,2,1,0:T(8,128)S(1)} %get-tuple-element.18.own.refs_0_, f32[2,3,8,8,256]{4,3,2,1,0:T(8,128)S(1)} %get-tuple-element.23.refs_1_, f32[3,8,16,256]{3,2,1,0:T(8,128)S(1)} %collective-permute-done.3.refs_2_, ...), custom_call_target="tpu_custom_call" | custom-call | flops 20000000 | bytes 20000000 | tf_op jit(solution)/shard_map/interior/pallas_call | solution.py:588
  15.3 0.0 collective-permute-done.6.got_a
  15.3 1.1 %collective-permute-done.5.got_b = f32[16,8,128]{2,1,0:T(8,128)S(1)} collective-permute-done((f32[16,8,128]{2,1,0:T(8,128)S(1)}, f32[16,8,128]{2,1,0:T(8,128)S(1)}, u32[]{:S(2)}, u32[]{:S(2)}) %collective-permute-start.5) | collective-permute-done | bytes 65568 | tf_op jit(solution)/shard_map/ppermute | solution.py:549
  16.4 1.9 %edges.1 = f32[8,16,256]{2,1,0:T(8,128)} custom-call(f32[3,18,24,128]{3,2,1,0:T(8,128)S(1)} %get-tuple-element.27.ends, f32[8,16,256]{2,1,0:T(8,128)S(1)} %get-tuple-element.28.inside, f32[16,8,128]{2,1,0:T(8,128)S(1)} %collective-permute-done.6.got_a, f32[16,8,128]{2,1,0:T(8,128)S(1)} %collective-permute-done.5.got_b), custom_call_target="tpu_custom_call" | custom-call | tf_op jit(solution)/shard_map/edges/pallas_call | solution.py:597
  (2 shorter events, 0.0 us)
Async XLA Ops:
  1.3 5.0 %collective-permute-start = (f32[14,8,256]{2,1,0:T(8,128)S(1)}, f32[14,8,256]{2,1,0:T(8,128)S(1)}, u32[]{:S(2)}, u32[]{:S(2)}) collective-permute-start(f32[14,8,256]{2,1,0:T(8,128)S(1)} %get-tuple-element.19), channel_id=1, source_target_pairs={{0,1},{4,5},{2,3},{6,7},{1,0},{5,4},{3,2},{7,6},{8,9},{12,13},{10,... | collective-permute-start | bytes 344072 | tf_op jit(solution)/shard_map/ppermute | solution.py:549
  3.0 4.8 %collective-permute-start.1 = (f32[14,8,256]{2,1,0:T(8,128)S(1)}, f32[14,8,256]{2,1,0:T(8,128)S(1)}, u32[]{:S(2)}, u32[]{:S(2)}) collective-permute-start(f32[14,8,256]{2,1,0:T(8,128)S(1)} %get-tuple-element.20), channel_id=1, source_target_pairs={{1,2},{5,6},{0,4},{3,7},{2,1},{6,5},{4,0},{7,3},{9,10},{13,14},{8,... | collective-permute-start | bytes 344072 | tf_op jit(solution)/shard_map/ppermute | solution.py:549
  8.0 1.3 %collective-permute-start.2 = (f32[2,8,8,128]{3,2,1,0:T(8,128)S(1)}, f32[2,8,8,128]{3,2,1,0:T(8,128)S(1)}, u32[]{:S(2)}, u32[]{:S(2)}) collective-permute-start(f32[2,8,8,128]{3,2,1,0:T(8,128)S(1)} %get-tuple-element.21), channel_id=1, source_target_pairs={{0,4},{4,0},{1,5},{5,1},{2,6},{6,2},{3,7},{7,3},{8,12},{12,8},{9,1... | collective-permute-start | bytes 196616 | tf_op jit(solution)/shard_map/ppermute | solution.py:549
  8.1 4.5 %collective-permute-start.3 = (f32[3,8,16,256]{3,2,1,0:T(8,128)S(1)}, f32[3,8,16,256]{3,2,1,0:T(8,128)S(1)}, u32[]{:S(2)}, u32[]{:S(2)}) collective-permute-start(f32[3,8,16,256]{3,2,1,0:T(8,128)S(1)} %get-tuple-element.18.own.refs_0_), channel_id=1, source_target_pairs={{0,4},{4,0},{1,5},{5,1},{2,6},{6,2},{3,7},{7,3},{8,12},{12,8},{9,1... | collective-permute-start | bytes 1179656 | tf_op jit(solution)/shard_map/ppermute | solution.py:549
  9.4 3.3 %collective-permute-start.4 = (f32[2,3,8,8,256]{4,3,2,1,0:T(8,128)S(1)}, f32[2,3,8,8,256]{4,3,2,1,0:T(8,128)S(1)}, u32[]{:S(2)}, u32[]{:S(2)}) collective-permute-start(f32[2,3,8,8,256]{4,3,2,1,0:T(8,128)S(1)} %get-tuple-element.23.refs_1_), channel_id=1, source_target_pairs={{0,4},{4,0},{1,5},{5,1},{2,6},{6,2},{3,7},{7,3},{8,12},{12,8},{9,1... | collective-permute-start | bytes 1179656 | tf_op jit(solution)/shard_map/ppermute | solution.py:549
  9.6 5.7 %collective-permute-start.6 = (f32[16,8,128]{2,1,0:T(8,128)S(1)}, f32[16,8,128]{2,1,0:T(8,128)S(1)}, u32[]{:S(2)}, u32[]{:S(2)}) collective-permute-start(f32[16,8,128]{2,1,0:T(8,128)S(1)} %get-tuple-element.31), channel_id=1, source_target_pairs={{0,8},{4,12},{16,24},{20,28},{8,0},{12,4},{24,16},{28,20},{1,9},{5... | collective-permute-start | bytes 196616 | tf_op jit(solution)/shard_map/ppermute | solution.py:549
  10.2 6.2 %collective-permute-start.5 = (f32[16,8,128]{2,1,0:T(8,128)S(1)}, f32[16,8,128]{2,1,0:T(8,128)S(1)}, u32[]{:S(2)}, u32[]{:S(2)}) collective-permute-start(f32[16,8,128]{2,1,0:T(8,128)S(1)} %get-tuple-element.32), channel_id=1, source_target_pairs={{8,16},{12,20},{0,4},{24,28},{16,8},{20,12},{4,0},{28,24},{9,17},{... | collective-permute-start | bytes 196616 | tf_op jit(solution)/shard_map/ppermute | solution.py:549

commit v12 on v11

--- a/solution.py
+++ b/solution.py
@@ -42,6 +42,27 @@
             pairs += [(at(i, k), at(i, k + 1)) for i in sorted(left) for k in range(0, fill, 2)]
         rounds.append(pairs + [(j, i) for i, j in pairs])
     return (tuple(over) if filled else axis), rounds
+
+
+def crossing(sizes):
+    names = list(sizes)
+
+    def at(**place):
+        index = 0
+        for name in names:
+            index = index * sizes[name] + place[name]
+        return index
+
+    last = sizes["grp"] - 1
+    pairs = [
+        (at(grp=g, gx=1, gy=y), at(grp=g + 1, gx=0, gy=y)) for g in range(last) for y in range(sizes["gy"])
+    ]
+    pairs += [
+        (at(grp=g, gx=x, gy=y), at(grp=g, gx=x, gy=y + 1))
+        for g, x in ((0, 0), (last, 1))
+        for y in range(0, sizes["gy"] - 1, 2)
+    ]
+    return pairs + [(j, i) for i, j in pairs]
 
 
 def is_odd(axis):
@@ -208,8 +229,9 @@
                 to_head, to_tail = head_lane(a, g), tail_lane(a, g)
                 head = jnp.where((lane >= to_head) & (lane < to_head + HALO), moved[p, a, g][0], head)
                 tail = jnp.where((lane >= to_tail) & (lane < to_tail + HALO), moved[p, a, g][1], tail)
-        strips[0, p] = jnp.where(odd_z == 1, head, tail)
-        strips[1, p] = jnp.where(odd_z == 1, tail, head)
+        swapped = (odd_x if reflect else odd_z) == 1
+        strips[0, p] = jnp.where(swapped, tail, head) if reflect else jnp.where(swapped, head, tail)
+        strips[1, p] = jnp.where(swapped, head, tail) if reflect else jnp.where(swapped, tail, head)
 
 
 def shifts(parts, step):
@@ -474,7 +496,7 @@
 
 def edges(reflect, ends, inside, got_a, got_b, result, staged, sems, *cells):
     depth, inner, width = inside.shape
-    odd_z = is_odd("grp")
+    odd_x, odd_z = is_odd("gx"), is_odd("grp")
     first_z, last_z = beyond("grp")
     lane = lax.broadcasted_iota(jnp.int32, (8, LANES), 1)
     half = LANES // 2
@@ -487,9 +509,14 @@
 
     def place(i, p_from, p_to):
         at_plane = p_from if i is None else (i + 1) * depth + p_from
-        va, vb = got_a[at_plane], got_b[at_plane]
-        right = jnp.where(last_z, 0.0, jnp.where(odd_z == 1, vb, va))
-        left = jnp.where(first_z, 0.0, jnp.where(odd_z == 1, va, vb))
+        if reflect:
+            va, vb = got_a[depth + p_from if i is None else p_from], got_b[at_plane]
+            swapped = odd_x == 0
+        else:
+            va, vb = got_a[at_plane], got_b[at_plane]
+            swapped = odd_z == 1
+        right = jnp.where(last_z, 0.0, jnp.where(swapped, vb, va))
+        left = jnp.where(first_z, 0.0, jnp.where(swapped, va, vb))
         windows.append((p_to, right, left, pltpu.roll(right, LANES - 8, 1), pltpu.roll(left, 8, 1)))
 
     here = lax.rem(lane, half)
@@ -576,10 +603,16 @@
         in_specs=[VMEM] * 3, out_specs=(VMEM, VMEM),
         compiler_params=params, name="pack_columns",
     )(own, *got)
-    strips = jnp.concatenate([strips] + exchange([strips] * n_x, "gx"), axis=1)
+    if reflect:
+        strips = jnp.concatenate([strips[0]] + exchange([strips[1]], "gx"), axis=0)
+    else:
+        strips = jnp.concatenate([strips] + exchange([strips] * n_x, "gx"), axis=1)
     strips, rim = lax.optimization_barrier((strips, rim))
     near_rim = exchange([rim] * n_x, "gx")
-    strips = exchange([strips[0], strips[1]], "grp")
+    if reflect:
+        strips = [lax.ppermute(strips, tuple(sizes), crossing(sizes))]
+    else:
+        strips = exchange([strips[0], strips[1]], "grp")
 
     block = jax.ShapeDtypeStruct(source_term.shape, f32)
     total = layout(reflect, depth)[1]
@@ -594,6 +627,8 @@
     )(own, rim, *near, *near_rim)
     inside, ends, *strips = lax.optimization_barrier((inside, ends, *strips[::-1]))
     strips = strips[::-1]
+    if reflect:
+        strips += exchange(strips, "gx")
     return pl.pallas_call(
         functools.partial(edges, reflect),
         out_shape=block,

time: 18.4 us -> 18.1 us (0.984)
  the two profiles are of different devices: /device:TPU:18 before, /device:TPU:0 now
where the time goes in v12:
time: 18.1 us; the launch traced here: 18 us
  starting transfers between devices  6.76 us (37%)
  Pallas kernels  6.06 us (33%)
  waiting for transfers between devices  5.09 us (28%)
    ppermute x6, waiting for transfers between devices, exchange(): lax.ppermute(v, over, pairs)  5.09 us
    ppermute x6, starting transfers between devices, exchange(): lax.ppermute(v, over, pairs)  3.89 us
    ppermute x1, starting transfers between devices, shards(): strips = [lax.ppermute(strips, tuple(sizes), crossing(sizes))]  2.87 us
    pallas_call x1, Pallas kernels, shards(): pl.pallas_call(functools.partial(interior, reflect, n_x), out_shape=(bloc...  2.6 us
    pallas_call x1, Pallas kernels, shards(): pl.pallas_call(functools.partial(edges, reflect), out_shape=block, in_spe...  1.87 us
    pallas_call x1, Pallas kernels, shards(): pl.pallas_call(functools.partial(prepare, reflect), out_shape=(jax.ShapeD...  1.34 us
  transfers between devices with their start and end apart: 7, of which 3 were waited for; matrix products, arithmetic and copies ran while one was open for 0% of the time, Pallas kernels for 14%

profile of v12, /device:TPU:0, one launch (start us, length us, event | category | flops | bytes accessed | tf_op | source)
XLA Modules:
  0.0 18.0 jit_solution(18297503971018540839)
XLA Ops:
  0.0 1.3 %prepare.1 = (f32[3,8,16,256]{3,2,1,0:T(8,128)S(1)}, f32[14,8,256]{2,1,0:T(8,128)S(1)}, f32[14,8,256]{2,1,0:T(8,128)S(1)}) custom-call(f32[8,16,256]{2,1,0:T(8,128)} %s.1, f32[8,16,256]{2,1,0:T(8,128)} %c.1, f32[8,16,256]{2,1,0:T(8,128)} %f.1), custom_call_target="tpu_custom_call" | custom-call | tf_op jit(solution)/shard_map/prepare/pallas_call | solution.py:589
  1.3 3.1 %collective-permute-start = (f32[14,8,256]{2,1,0:T(8,128)S(1)}, f32[14,8,256]{2,1,0:T(8,128)S(1)}, u32[]{:S(2)}, u32[]{:S(2)}) collective-permute-start(f32[14,8,256]{2,1,0:T(8,128)S(1)} %get-tuple-element.18), channel_id=1, source_target_pairs={{0,1},{4,5},{2,3},{6,7},{1,0},{5,4},{3,2},{7,6},{8,9},{12,13},{10,... | collective-permute-start | bytes 344072 | tf_op jit(solution)/shard_map/ppermute | solution.py:576
  4.4 0.0 collective-permute-start.1
  4.4 3.1 %collective-permute-done.got_a = f32[14,8,256]{2,1,0:T(8,128)S(1)} collective-permute-done((f32[14,8,256]{2,1,0:T(8,128)S(1)}, f32[14,8,256]{2,1,0:T(8,128)S(1)}, u32[]{:S(2)}, u32[]{:S(2)}) %collective-permute-start) | collective-permute-done | bytes 114720 | tf_op jit(solution)/shard_map/ppermute | solution.py:576
  7.6 0.0 collective-permute-done.1.got_b
  7.6 0.2 %pack_columns.1 = (f32[2,8,8,128]{3,2,1,0:T(8,128)S(1)}, f32[2,3,8,8,256]{4,3,2,1,0:T(8,128)S(1)}) custom-call(f32[3,8,16,256]{3,2,1,0:T(8,128)S(1)} %get-tuple-element.17.own.refs_0_, f32[14,8,256]{2,1,0:T(8,128)S(1)} %collective-permute-done.got_a, f32[14,8,256]{2,1,0:T(8,128)S(1)} %collective-permute-done.1.got_b), custom_call_target="tpu_custom_call" | custom-call | tf_op jit(solution)/shard_map/pack_columns/pallas_call | solution.py:597
  7.8 0.1 collective-permute-start.2
  7.9 0.5 %collective-permute-start.3 = (f32[3,8,16,256]{3,2,1,0:T(8,128)S(1)}, f32[3,8,16,256]{3,2,1,0:T(8,128)S(1)}, u32[]{:S(2)}, u32[]{:S(2)}) collective-permute-start(f32[3,8,16,256]{3,2,1,0:T(8,128)S(1)} %get-tuple-element.17.own.refs_0_), channel_id=1, source_target_pairs={{0,4},{4,0},{1,5},{5,1},{2,6},{6,2},{3,7},{7,3},{8,12},{12,8},{9,1... | collective-permute-start | bytes 1179656 | tf_op jit(solution)/shard_map/ppermute | solution.py:576
  8.4 0.7 %collective-permute-done.2 = f32[8,8,128]{2,1,0:T(8,128)S(1)} collective-permute-done((f32[8,8,128]{2,1,0:T(8,128)S(1)}, f32[8,8,128]{2,1,0:T(8,128)S(1)}, u32[]{:S(2)}, u32[]{:S(2)}) %collective-permute-start.2) | collective-permute-done | bytes 32800 | tf_op jit(solution)/shard_map/ppermute | solution.py:576
  9.1 0.2 collective-permute-start.4
  9.3 2.9 %collective-permute-start.5 = (f32[16,8,128]{2,1,0:T(8,128)S(1)}, f32[16,8,128]{2,1,0:T(8,128)S(1)}, u32[]{:S(2)}, u32[]{:S(2)}) collective-permute-start(f32[16,8,128]{2,1,0:T(8,128)S(1)} %pad_maximum_fusion), channel_id=1, source_target_pairs={{4,8},{5,9},{6,10},{7,11},{12,16},{13,17},{14,18},{15,19},{20,24},... | collective-permute-start | bytes 196616 | tf_op jit(solution)/shard_map/ppermute | solution.py:613
  12.2 0.0 collective-permute-done.3.refs_2_
  12.2 0.0 collective-permute-done.4.refs_3_
  12.2 2.6 %interior.1 = (f32[8,16,256]{2,1,0:T(8,128)S(1)}, f32[3,18,24,128]{3,2,1,0:T(8,128)S(1)}) custom-call(f32[3,8,16,256]{3,2,1,0:T(8,128)S(1)} %get-tuple-element.17.own.refs_0_, f32[2,3,8,8,256]{4,3,2,1,0:T(8,128)S(1)} %get-tuple-element.22.refs_1_, f32[3,8,16,256]{3,2,1,0:T(8,128)S(1)} %collective-permute-done.3.refs_2_, ...), custom_call_target="tpu_custom_call" | custom-call | flops 20000000 | bytes 20000000 | tf_op jit(solution)/shard_map/interior/pallas_call | solution.py:621
  14.8 0.0 collective-permute-done.5.got_a
  14.8 0.1 collective-permute-start.6
  14.9 1.2 %collective-permute-done.6.got_b = f32[16,8,128]{2,1,0:T(8,128)S(1)} collective-permute-done((f32[16,8,128]{2,1,0:T(8,128)S(1)}, f32[16,8,128]{2,1,0:T(8,128)S(1)}, u32[]{:S(2)}, u32[]{:S(2)}) %collective-permute-start.6) | collective-permute-done | bytes 65568 | tf_op jit(solution)/shard_map/ppermute | solution.py:576
  16.1 1.9 %edges.1 = f32[8,16,256]{2,1,0:T(8,128)} custom-call(f32[3,18,24,128]{3,2,1,0:T(8,128)S(1)} %get-tuple-element.26.ends, f32[8,16,256]{2,1,0:T(8,128)S(1)} %get-tuple-element.27.inside, f32[16,8,128]{2,1,0:T(8,128)S(1)} %collective-permute-done.5.got_a, f32[16,8,128]{2,1,0:T(8,128)S(1)} %collective-permute-done.6.got_b), custom_call_target="tpu_custom_call" | custom-call | tf_op jit(solution)/shard_map/edges/pallas_call | solution.py:632
  (2 shorter events, 0.0 us)
Async XLA Ops:
  1.3 6.2 %collective-permute-start = (f32[14,8,256]{2,1,0:T(8,128)S(1)}, f32[14,8,256]{2,1,0:T(8,128)S(1)}, u32[]{:S(2)}, u32[]{:S(2)}) collective-permute-start(f32[14,8,256]{2,1,0:T(8,128)S(1)} %get-tuple-element.18), channel_id=1, source_target_pairs={{0,1},{4,5},{2,3},{6,7},{1,0},{5,4},{3,2},{7,6},{8,9},{12,13},{10,... | collective-permute-start | bytes 344072 | tf_op jit(solution)/shard_map/ppermute | solution.py:576
  4.4 3.1 %collective-permute-start.1 = (f32[14,8,256]{2,1,0:T(8,128)S(1)}, f32[14,8,256]{2,1,0:T(8,128)S(1)}, u32[]{:S(2)}, u32[]{:S(2)}) collective-permute-start(f32[14,8,256]{2,1,0:T(8,128)S(1)} %get-tuple-element.19), channel_id=1, source_target_pairs={{1,2},{5,6},{0,4},{3,7},{2,1},{6,5},{4,0},{7,3},{9,10},{13,14},{8,... | collective-permute-start | bytes 344072 | tf_op jit(solution)/shard_map/ppermute | solution.py:576
  7.8 1.3 %collective-permute-start.2 = (f32[8,8,128]{2,1,0:T(8,128)S(1)}, f32[8,8,128]{2,1,0:T(8,128)S(1)}, u32[]{:S(2)}, u32[]{:S(2)}) collective-permute-start(f32[8,8,128]{2,1,0:T(8,128)S(1)} %get-tuple-element.30), channel_id=1, source_target_pairs={{0,4},{4,0},{1,5},{5,1},{2,6},{6,2},{3,7},{7,3},{8,12},{12,8},{9,1... | collective-permute-start | bytes 98312 | tf_op jit(solution)/shard_map/ppermute | solution.py:576
  7.9 4.2 %collective-permute-start.3 = (f32[3,8,16,256]{3,2,1,0:T(8,128)S(1)}, f32[3,8,16,256]{3,2,1,0:T(8,128)S(1)}, u32[]{:S(2)}, u32[]{:S(2)}) collective-permute-start(f32[3,8,16,256]{3,2,1,0:T(8,128)S(1)} %get-tuple-element.17.own.refs_0_), channel_id=1, source_target_pairs={{0,4},{4,0},{1,5},{5,1},{2,6},{6,2},{3,7},{7,3},{8,12},{12,8},{9,1... | collective-permute-start | bytes 1179656 | tf_op jit(solution)/shard_map/ppermute | solution.py:576
  9.1 3.0 %collective-permute-start.4 = (f32[2,3,8,8,256]{4,3,2,1,0:T(8,128)S(1)}, f32[2,3,8,8,256]{4,3,2,1,0:T(8,128)S(1)}, u32[]{:S(2)}, u32[]{:S(2)}) collective-permute-start(f32[2,3,8,8,256]{4,3,2,1,0:T(8,128)S(1)} %get-tuple-element.22.refs_1_), channel_id=1, source_target_pairs={{0,4},{4,0},{1,5},{5,1},{2,6},{6,2},{3,7},{7,3},{8,12},{12,8},{9,1... | collective-permute-start | bytes 1179656 | tf_op jit(solution)/shard_map/ppermute | solution.py:576
  9.3 5.5 %collective-permute-start.5 = (f32[16,8,128]{2,1,0:T(8,128)S(1)}, f32[16,8,128]{2,1,0:T(8,128)S(1)}, u32[]{:S(2)}, u32[]{:S(2)}) collective-permute-start(f32[16,8,128]{2,1,0:T(8,128)S(1)} %pad_maximum_fusion), channel_id=1, source_target_pairs={{4,8},{5,9},{6,10},{7,11},{12,16},{13,17},{14,18},{15,19},{20,24},... | collective-permute-start | bytes 196616 | tf_op jit(solution)/shard_map/ppermute | solution.py:613
  14.8 1.3 %collective-permute-start.6 = (f32[16,8,128]{2,1,0:T(8,128)S(1)}, f32[16,8,128]{2,1,0:T(8,128)S(1)}, u32[]{:S(2)}, u32[]{:S(2)}) collective-permute-start(f32[16,8,128]{2,1,0:T(8,128)S(1)} %collective-permute-done.5.got_a), channel_id=1, source_target_pairs={{0,4},{4,0},{1,5},{5,1},{2,6},{6,2},{3,7},{7,3},{8,12},{12,8},{9,1... | collective-permute-start | bytes 196616 | tf_op jit(solution)/shard_map/ppermute | solution.py:576

commit v13 on v12

--- a/solution.py
+++ b/solution.py
@@ -11,7 +11,7 @@
 HALO = 4 * ITERS
 LANES = 128
 KEEP = 48.0 / 41.0
-SPREAD = 32.0 / 41.0
+SPREAD_OVER_KEEP = 2.0 / 3.0
 VMEM = pl.BlockSpec(memory_space=pltpu.VMEM)
 
 
@@ -290,8 +290,10 @@
             return {k: [v[0] + u] for (k, v), u in zip(sums.items(), [ahead(v[0], 1) for v in sums.values()])}
         return {k: [v[0] + ahead(v[0], 0)] for k, v in sums.items()}
 
+    z_fine = turned(cond, planes_of(reach(HALO - 2)), fine)
     for k, v in gather({k: add(load(cond, 2 * k - 1), load(cond, 2 * k)) for k in reach(HALO)}).items():
         store(sum8, k, v)
+    z_field = turned(field, planes_of(reach(HALO - 2)), fine) if seams[2] is not None else {}
 
     def weights(ref, p, level, around_z):
         step = level[0]
@@ -300,12 +302,11 @@
         y, yb = ([v + shift(v, 0, step) for v in c] for shift in (ahead, behind))
         z, zb = (add(c, v) for v in around_z)
         k = add(add(c, load(ref, p - 1), x), add(y, yb), add(z, zb))
-        return x, y, z, yb, zb, k, each(lambda v, w: jnp.where(v > 0.0, 1.0 / w, 0.0), c, k)
+        return x, y, z, yb, zb, k, each(lambda v, w: jnp.where(v > 0.0, KEEP / w, 0.0), c, k)
 
     low = reach(HALO - 2).start
     store(wx, 2 * low - 2, add(load(cond, 2 * low - 2), load(cond, 2 * low - 1)))
     store(cwx, low - 1, add(load(sum8, low - 1), load(sum8, low)))
-    z_fine = turned(cond, planes_of(reach(HALO - 2)), fine)
     z_coarse = turned(sum8, reach(HALO - 2), coarse)
     for k in reach(HALO - 2):
         for p in (2 * k - 1, 2 * k):
@@ -325,8 +326,8 @@
         return add(n, add(times(load(z, p), around_z[0]), times(load(zb, p), around_z[1])))
 
     def smooth(v, p, refs, scale, level, around_z):
-        n = times(load(scale, p), spread(v, p, refs, level, around_z))
-        return each(lambda u, w: KEEP * u + SPREAD * w, load(v, p), n)
+        n = times([(SPREAD_OVER_KEEP / KEEP) * u for u in load(scale, p)], spread(v, p, refs, level, around_z))
+        return add(load(v, p), n)
 
     def between(p, around_z):
         planes, along_y, along_z = seams
@@ -353,7 +354,7 @@
     for it in range(ITERS):
         halo = 4 * (ITERS - 1 - it)
         blocks = reach(halo + 2)
-        rounds = turned(err if it else field, planes_of(blocks), fine) if it or seams[2] is not None else {}
+        rounds = turned(err, planes_of(blocks), fine) if it else z_field
         sums = {}
         for k in blocks:
             found = []
@@ -440,14 +441,12 @@
 
 def rearranged(v, matrix):
     bf16, f32 = jnp.bfloat16, jnp.float32
+    parts = []
+    for _ in range(3):
+        parts.append(v.astype(bf16))
+        v = v - parts[-1].astype(f32)
     matrix = matrix.astype(bf16)
-    result = None
-    for _ in range(3):
-        part = v.astype(bf16)
-        v = v - part.astype(f32)
-        moved = jnp.dot(part, matrix, preferred_element_type=f32)
-        result = moved if result is None else result + moved
-    return result
+    return jnp.dot(jnp.concatenate(parts, 1), jnp.concatenate([matrix] * 3, 0), preferred_element_type=f32)
 
 
 def interior(reflect, n_x, *refs):
@@ -470,16 +469,18 @@
     own_at, total = layout(reflect, depth)
     for a in range(3):
         for p in (0, total - 1):
-            whole[a, p] = jnp.zeros((rows, width), jnp.float32)
+            cells[a][p] = jnp.zeros((2, rows, lanes), jnp.float32)
+            ends[a, p] = jnp.zeros((rows - 8, LANES), jnp.float32)
     each_plane(reflect, depth, place)
     apart = parting(width, lanes)
     target = jnp.concatenate([apart, ending(width)], 1)
     for a in range(3):
-        parts = rearranged(whole[a].reshape(total * rows, width), target).reshape(total, rows, -1)
+        inside = slice(1, total - 1)
+        parts = rearranged(whole[a, inside].reshape((total - 2) * rows, width), target).reshape(total - 2, rows, -1)
         for i in range(2):
-            cells[a][:, i] = parts[:, :, i * lanes : (i + 1) * lanes]
+            cells[a][inside, i] = parts[:, :, i * lanes : (i + 1) * lanes]
         low = parts[:, 0 : rows - 8, 2 * lanes : 2 * lanes + LANES]
-        ends[a] = low + parts[:, 8:rows, 2 * lanes + LANES :]
+        ends[a, inside] = low + parts[:, 8:rows, 2 * lanes + LANES :]
 
     def out(p, v):
         for i in range(2):
@@ -527,7 +528,7 @@
     for p, right, left, right_moved, left_moved in windows:
         lower, upper = jnp.where(side, right, left), jnp.where(side, right_moved, left_moved)
         groups.append((p, lower, pltpu.roll(jnp.where(lane < half, upper, lower), half, 1), upper))
-    for a in (1, 0, 2):
+    for a in (1, 2, 0):
         for p, *tiles in groups:
             for t, tile in enumerate(tiles):
                 moved = tile if a == 1 else pltpu.roll(tile, (16 - 16 * a) % LANES, 1)

time: 18.1 us -> 18 us (level)
  the two profiles are of different devices: /device:TPU:0 before, /device:TPU:19 now
where the time goes in v13:
time: 18 us; the launch traced here: 17.9 us
  waiting for transfers between devices  6.99 us (39%)
  Pallas kernels  5.85 us (32%)
  starting transfers between devices  4.99 us (28%)
    ppermute x6, waiting for transfers between devices, exchange(): lax.ppermute(v, over, pairs)  6.02 us
    ppermute x6, starting transfers between devices, exchange(): lax.ppermute(v, over, pairs)  3.73 us
    pallas_call x1, Pallas kernels, shards(): pl.pallas_call(functools.partial(interior, reflect, n_x), out_shape=(bloc...  2.46 us
    pallas_call x1, Pallas kernels, shards(): pl.pallas_call(functools.partial(edges, reflect), out_shape=block, in_spe...  1.81 us
    pallas_call x1, Pallas kernels, shards(): pl.pallas_call(functools.partial(prepare, reflect), out_shape=(jax.ShapeD...  1.34 us
    ppermute x1, starting transfers between devices, shards(): strips = [lax.ppermute(strips, tuple(sizes), crossing(sizes))]  1.26 us
    ppermute x1, waiting for transfers between devices, shards(): strips = [lax.ppermute(strips, tuple(sizes), crossing(sizes))]  0.98 us
  transfers between devices with their start and end apart: 7, of which 6 were waited for; matrix products, arithmetic and copies ran while one was open for 0% of the time, Pallas kernels for 14%

profile of v13, /device:TPU:19, one launch (start us, length us, event | category | flops | bytes accessed | tf_op | source)
XLA Modules:
  0.0 17.9 jit_solution(1931786748849422918)
XLA Ops:
  0.0 1.3 %prepare.1 = (f32[3,8,16,256]{3,2,1,0:T(8,128)S(1)}, f32[14,8,256]{2,1,0:T(8,128)S(1)}, f32[14,8,256]{2,1,0:T(8,128)S(1)}) custom-call(f32[8,16,256]{2,1,0:T(8,128)} %s.1, f32[8,16,256]{2,1,0:T(8,128)} %c.1, f32[8,16,256]{2,1,0:T(8,128)} %f.1), custom_call_target="tpu_custom_call" | custom-call | tf_op jit(solution)/shard_map/prepare/pallas_call | solution.py:590
  1.3 1.4 %collective-permute-start = (f32[14,8,256]{2,1,0:T(8,128)S(1)}, f32[14,8,256]{2,1,0:T(8,128)S(1)}, u32[]{:S(2)}, u32[]{:S(2)}) collective-permute-start(f32[14,8,256]{2,1,0:T(8,128)S(1)} %get-tuple-element.18), channel_id=1, source_target_pairs={{0,1},{4,5},{2,3},{6,7},{1,0},{5,4},{3,2},{7,6},{8,9},{12,13},{10,... | collective-permute-start | bytes 344072 | tf_op jit(solution)/shard_map/ppermute | solution.py:577
  2.7 0.0 collective-permute-start.1
  2.7 2.7 %collective-permute-done.got_a = f32[14,8,256]{2,1,0:T(8,128)S(1)} collective-permute-done((f32[14,8,256]{2,1,0:T(8,128)S(1)}, f32[14,8,256]{2,1,0:T(8,128)S(1)}, u32[]{:S(2)}, u32[]{:S(2)}) %collective-permute-start) | collective-permute-done | bytes 114720 | tf_op jit(solution)/shard_map/ppermute | solution.py:577
  5.4 1.2 %collective-permute-done.1.got_b = f32[14,8,256]{2,1,0:T(8,128)S(1)} collective-permute-done((f32[14,8,256]{2,1,0:T(8,128)S(1)}, f32[14,8,256]{2,1,0:T(8,128)S(1)}, u32[]{:S(2)}, u32[]{:S(2)}) %collective-permute-start.1) | collective-permute-done | bytes 114720 | tf_op jit(solution)/shard_map/ppermute | solution.py:577
  6.6 0.2 %pack_columns.1 = (f32[2,8,8,128]{3,2,1,0:T(8,128)S(1)}, f32[2,3,8,8,256]{4,3,2,1,0:T(8,128)S(1)}) custom-call(f32[3,8,16,256]{3,2,1,0:T(8,128)S(1)} %get-tuple-element.17.own.refs_0_, f32[14,8,256]{2,1,0:T(8,128)S(1)} %collective-permute-done.got_a, f32[14,8,256]{2,1,0:T(8,128)S(1)} %collective-permute-done.1.got_b), custom_call_target="tpu_custom_call" | custom-call | tf_op jit(solution)/shard_map/pack_columns/pallas_call | solution.py:598
  6.8 1.9 %collective-permute-start.2 = (f32[8,8,128]{2,1,0:T(8,128)S(1)}, f32[8,8,128]{2,1,0:T(8,128)S(1)}, u32[]{:S(2)}, u32[]{:S(2)}) collective-permute-start(f32[8,8,128]{2,1,0:T(8,128)S(1)} %get-tuple-element.30), channel_id=1, source_target_pairs={{0,4},{4,0},{1,5},{5,1},{2,6},{6,2},{3,7},{7,3},{8,12},{12,8},{9,1... | collective-permute-start | bytes 98312 | tf_op jit(solution)/shard_map/ppermute | solution.py:577
  8.8 0.1 collective-permute-start.3
  8.9 0.8 %collective-permute-done.2 = f32[8,8,128]{2,1,0:T(8,128)S(1)} collective-permute-done((f32[8,8,128]{2,1,0:T(8,128)S(1)}, f32[8,8,128]{2,1,0:T(8,128)S(1)}, u32[]{:S(2)}, u32[]{:S(2)}) %collective-permute-start.2) | collective-permute-done | bytes 32800 | tf_op jit(solution)/shard_map/ppermute | solution.py:577
  9.6 0.3 %collective-permute-start.4 = (f32[2,3,8,8,256]{4,3,2,1,0:T(8,128)S(1)}, f32[2,3,8,8,256]{4,3,2,1,0:T(8,128)S(1)}, u32[]{:S(2)}, u32[]{:S(2)}) collective-permute-start(f32[2,3,8,8,256]{4,3,2,1,0:T(8,128)S(1)} %get-tuple-element.22.refs_1_), channel_id=1, source_target_pairs={{0,4},{4,0},{1,5},{5,1},{2,6},{6,2},{3,7},{7,3},{8,12},{12,8},{9,1... | collective-permute-start | bytes 1179656 | tf_op jit(solution)/shard_map/ppermute | solution.py:577
  10.0 1.3 %collective-permute-start.5 = (f32[16,8,128]{2,1,0:T(8,128)S(1)}, f32[16,8,128]{2,1,0:T(8,128)S(1)}, u32[]{:S(2)}, u32[]{:S(2)}) collective-permute-start(f32[16,8,128]{2,1,0:T(8,128)S(1)} %pad_maximum_fusion), channel_id=1, source_target_pairs={{4,8},{5,9},{6,10},{7,11},{12,16},{13,17},{14,18},{15,19},{20,24},... | collective-permute-start | bytes 196616 | tf_op jit(solution)/shard_map/ppermute | solution.py:614
  11.3 0.0 collective-permute-done.3.refs_2_
  11.3 0.1 collective-permute-done.4.refs_3_
  11.4 2.5 %interior.1 = (f32[8,16,256]{2,1,0:T(8,128)S(1)}, f32[3,18,24,128]{3,2,1,0:T(8,128)S(1)}) custom-call(f32[3,8,16,256]{3,2,1,0:T(8,128)S(1)} %get-tuple-element.17.own.refs_0_, f32[2,3,8,8,256]{4,3,2,1,0:T(8,128)S(1)} %get-tuple-element.22.refs_1_, f32[3,8,16,256]{3,2,1,0:T(8,128)S(1)} %collective-permute-done.3.refs_2_, ...), custom_call_target="tpu_custom_call" | custom-call | flops 20000000 | bytes 20000000 | tf_op jit(solution)/shard_map/interior/pallas_call | solution.py:622
  13.8 1.0 %collective-permute-done.5.got_a = f32[16,8,128]{2,1,0:T(8,128)S(1)} collective-permute-done((f32[16,8,128]{2,1,0:T(8,128)S(1)}, f32[16,8,128]{2,1,0:T(8,128)S(1)}, u32[]{:S(2)}, u32[]{:S(2)}) %collective-permute-start.5) | collective-permute-done | bytes 65568 | tf_op jit(solution)/shard_map/ppermute | solution.py:614
  14.8 0.0 collective-permute-start.6
  14.8 1.3 %collective-permute-done.6.got_b = f32[16,8,128]{2,1,0:T(8,128)S(1)} collective-permute-done((f32[16,8,128]{2,1,0:T(8,128)S(1)}, f32[16,8,128]{2,1,0:T(8,128)S(1)}, u32[]{:S(2)}, u32[]{:S(2)}) %collective-permute-start.6) | collective-permute-done | bytes 65568 | tf_op jit(solution)/shard_map/ppermute | solution.py:577
  16.1 1.8 %edges.1 = f32[8,16,256]{2,1,0:T(8,128)} custom-call(f32[3,18,24,128]{3,2,1,0:T(8,128)S(1)} %get-tuple-element.26.ends, f32[8,16,256]{2,1,0:T(8,128)S(1)} %get-tuple-element.27.inside, f32[16,8,128]{2,1,0:T(8,128)S(1)} %collective-permute-done.5.got_a, f32[16,8,128]{2,1,0:T(8,128)S(1)} %collective-permute-done.6.got_b), custom_call_target="tpu_custom_call" | custom-call | tf_op jit(solution)/shard_map/edges/pallas_call | solution.py:633
  (2 shorter events, 0.0 us)
Async XLA Ops:
  1.3 4.1 %collective-permute-start = (f32[14,8,256]{2,1,0:T(8,128)S(1)}, f32[14,8,256]{2,1,0:T(8,128)S(1)}, u32[]{:S(2)}, u32[]{:S(2)}) collective-permute-start(f32[14,8,256]{2,1,0:T(8,128)S(1)} %get-tuple-element.18), channel_id=1, source_target_pairs={{0,1},{4,5},{2,3},{6,7},{1,0},{5,4},{3,2},{7,6},{8,9},{12,13},{10,... | collective-permute-start | bytes 344072 | tf_op jit(solution)/shard_map/ppermute | solution.py:577
  2.7 3.9 %collective-permute-start.1 = (f32[14,8,256]{2,1,0:T(8,128)S(1)}, f32[14,8,256]{2,1,0:T(8,128)S(1)}, u32[]{:S(2)}, u32[]{:S(2)}) collective-permute-start(f32[14,8,256]{2,1,0:T(8,128)S(1)} %get-tuple-element.19), channel_id=1, source_target_pairs={{1,2},{5,6},{0,4},{3,7},{2,1},{6,5},{4,0},{7,3},{9,10},{13,14},{8,... | collective-permute-start | bytes 344072 | tf_op jit(solution)/shard_map/ppermute | solution.py:577
  6.8 2.8 %collective-permute-start.2 = (f32[8,8,128]{2,1,0:T(8,128)S(1)}, f32[8,8,128]{2,1,0:T(8,128)S(1)}, u32[]{:S(2)}, u32[]{:S(2)}) collective-permute-start(f32[8,8,128]{2,1,0:T(8,128)S(1)} %get-tuple-element.30), channel_id=1, source_target_pairs={{0,4},{4,0},{1,5},{5,1},{2,6},{6,2},{3,7},{7,3},{8,12},{12,8},{9,1... | collective-permute-start | bytes 98312 | tf_op jit(solution)/shard_map/ppermute | solution.py:577
  8.8 2.5 %collective-permute-start.3 = (f32[3,8,16,256]{3,2,1,0:T(8,128)S(1)}, f32[3,8,16,256]{3,2,1,0:T(8,128)S(1)}, u32[]{:S(2)}, u32[]{:S(2)}) collective-permute-start(f32[3,8,16,256]{3,2,1,0:T(8,128)S(1)} %get-tuple-element.17.own.refs_0_), channel_id=1, source_target_pairs={{0,4},{4,0},{1,5},{5,1},{2,6},{6,2},{3,7},{7,3},{8,12},{12,8},{9,1... | collective-permute-start | bytes 1179656 | tf_op jit(solution)/shard_map/ppermute | solution.py:577
  9.6 1.7 %collective-permute-start.4 = (f32[2,3,8,8,256]{4,3,2,1,0:T(8,128)S(1)}, f32[2,3,8,8,256]{4,3,2,1,0:T(8,128)S(1)}, u32[]{:S(2)}, u32[]{:S(2)}) collective-permute-start(f32[2,3,8,8,256]{4,3,2,1,0:T(8,128)S(1)} %get-tuple-element.22.refs_1_), channel_id=1, source_target_pairs={{0,4},{4,0},{1,5},{5,1},{2,6},{6,2},{3,7},{7,3},{8,12},{12,8},{9,1... | collective-permute-start | bytes 1179656 | tf_op jit(solution)/shard_map/ppermute | solution.py:577
  10.0 4.8 %collective-permute-start.5 = (f32[16,8,128]{2,1,0:T(8,128)S(1)}, f32[16,8,128]{2,1,0:T(8,128)S(1)}, u32[]{:S(2)}, u32[]{:S(2)}) collective-permute-start(f32[16,8,128]{2,1,0:T(8,128)S(1)} %pad_maximum_fusion), channel_id=1, source_target_pairs={{4,8},{5,9},{6,10},{7,11},{12,16},{13,17},{14,18},{15,19},{20,24},... | collective-permute-start | bytes 196616 | tf_op jit(solution)/shard_map/ppermute | solution.py:614
  14.8 1.3 %collective-permute-start.6 = (f32[16,8,128]{2,1,0:T(8,128)S(1)}, f32[16,8,128]{2,1,0:T(8,128)S(1)}, u32[]{:S(2)}, u32[]{:S(2)}) collective-permute-start(f32[16,8,128]{2,1,0:T(8,128)S(1)} %collective-permute-done.5.got_a), channel_id=1, source_target_pairs={{0,4},{4,0},{1,5},{5,1},{2,6},{6,2},{3,7},{7,3},{8,12},{12,8},{9,1... | collective-permute-start | bytes 196616 | tf_op jit(solution)/shard_map/ppermute | solution.py:577

commit v14 on v13

--- a/solution.py
+++ b/solution.py
@@ -287,7 +287,10 @@
     def gather(sums):
         sums = {k: [v[0] + ahead(v[0], 0)] if parts == 1 else [v[0] + v[1]] for k, v in sums.items()}
         if parts == 1:
-            return {k: [v[0] + u] for (k, v), u in zip(sums.items(), [ahead(v[0], 1) for v in sums.values()])}
+            nexts, lasts = ([shift(v[0], 1) for v in sums.values()] for shift in (ahead, behind))
+            return {
+                k: [v[0] + jnp.where(even_lane, u, w)] for (k, v), u, w in zip(sums.items(), nexts, lasts)
+            }
         return {k: [v[0] + ahead(v[0], 0)] for k, v in sums.items()}
 
     z_fine = turned(cond, planes_of(reach(HALO - 2)), fine)
@@ -376,9 +379,6 @@
             store(cq, k, times([4.0 * v[0]], load(cinv, k)))
         coarse_rounds = turned(cq, near, coarse)
         found = {k: smooth(cq, k, coarse_around, cinv, coarse, coarse_rounds[k])[0] for k in near}
-        if parts == 1:
-            beside = {k: behind(c, 1) for k, c in found.items()}
-            found = {k: jnp.where(even_lane, c, beside[k]) for k, c in found.items()}
         smoothed = {p: smooth(q, p, around, inv, fine, rounds[p]) for p in planes_of(near)}
         for k in near:
             c = jnp.where(even_row, found[k], behind(found[k], 0))

time: 18 us -> 18 us (level)
  no operation moved by 1% of the time
where the time goes in v14:
time: 18 us; the launch traced here: 17.8 us
  waiting for transfers between devices  6.99 us (39%)
  Pallas kernels  5.81 us (32%)
  starting transfers between devices  4.99 us (28%)
    ppermute x6, waiting for transfers between devices, exchange(): lax.ppermute(v, over, pairs)  6.02 us
    ppermute x6, starting transfers between devices, exchange(): lax.ppermute(v, over, pairs)  3.73 us
    pallas_call x1, Pallas kernels, shards(): pl.pallas_call(functools.partial(interior, reflect, n_x), out_shape=(bloc...  2.46 us
    pallas_call x1, Pallas kernels, shards(): pl.pallas_call(functools.partial(edges, reflect), out_shape=block, in_spe...  1.77 us
    pallas_call x1, Pallas kernels, shards(): pl.pallas_call(functools.partial(prepare, reflect), out_shape=(jax.ShapeD...  1.34 us
    ppermute x1, starting transfers between devices, shards(): strips = [lax.ppermute(strips, tuple(sizes), crossing(sizes))]  1.26 us
    ppermute x1, waiting for transfers between devices, shards(): strips = [lax.ppermute(strips, tuple(sizes), crossing(sizes))]  0.98 us
  transfers between devices with their start and end apart: 7, of which 6 were waited for; matrix products, arithmetic and copies ran while one was open for 0% of the time, Pallas kernels for 14%

profile of v14, /device:TPU:19, one launch (start us, length us, event | category | flops | bytes accessed | tf_op | source)
XLA Modules:
  0.0 17.8 jit_solution(5006915796590220787)
XLA Ops:
  0.0 1.3 %prepare.1 = (f32[3,8,16,256]{3,2,1,0:T(8,128)S(1)}, f32[14,8,256]{2,1,0:T(8,128)S(1)}, f32[14,8,256]{2,1,0:T(8,128)S(1)}) custom-call(f32[8,16,256]{2,1,0:T(8,128)} %s.1, f32[8,16,256]{2,1,0:T(8,128)} %c.1, f32[8,16,256]{2,1,0:T(8,128)} %f.1), custom_call_target="tpu_custom_call" | custom-call | tf_op jit(solution)/shard_map/prepare/pallas_call | solution.py:590
  1.3 1.4 %collective-permute-start = (f32[14,8,256]{2,1,0:T(8,128)S(1)}, f32[14,8,256]{2,1,0:T(8,128)S(1)}, u32[]{:S(2)}, u32[]{:S(2)}) collective-permute-start(f32[14,8,256]{2,1,0:T(8,128)S(1)} %get-tuple-element.18), channel_id=1, source_target_pairs={{0,1},{4,5},{2,3},{6,7},{1,0},{5,4},{3,2},{7,6},{8,9},{12,13},{10,... | collective-permute-start | bytes 344072 | tf_op jit(solution)/shard_map/ppermute | solution.py:577
  2.7 0.0 collective-permute-start.1
  2.7 2.7 %collective-permute-done.got_a = f32[14,8,256]{2,1,0:T(8,128)S(1)} collective-permute-done((f32[14,8,256]{2,1,0:T(8,128)S(1)}, f32[14,8,256]{2,1,0:T(8,128)S(1)}, u32[]{:S(2)}, u32[]{:S(2)}) %collective-permute-start) | collective-permute-done | bytes 114720 | tf_op jit(solution)/shard_map/ppermute | solution.py:577
  5.4 1.2 %collective-permute-done.1.got_b = f32[14,8,256]{2,1,0:T(8,128)S(1)} collective-permute-done((f32[14,8,256]{2,1,0:T(8,128)S(1)}, f32[14,8,256]{2,1,0:T(8,128)S(1)}, u32[]{:S(2)}, u32[]{:S(2)}) %collective-permute-start.1) | collective-permute-done | bytes 114720 | tf_op jit(solution)/shard_map/ppermute | solution.py:577
  6.6 0.2 %pack_columns.1 = (f32[2,8,8,128]{3,2,1,0:T(8,128)S(1)}, f32[2,3,8,8,256]{4,3,2,1,0:T(8,128)S(1)}) custom-call(f32[3,8,16,256]{3,2,1,0:T(8,128)S(1)} %get-tuple-element.17.own.refs_0_, f32[14,8,256]{2,1,0:T(8,128)S(1)} %collective-permute-done.got_a, f32[14,8,256]{2,1,0:T(8,128)S(1)} %collective-permute-done.1.got_b), custom_call_target="tpu_custom_call" | custom-call | tf_op jit(solution)/shard_map/pack_columns/pallas_call | solution.py:598
  6.8 1.9 %collective-permute-start.2 = (f32[8,8,128]{2,1,0:T(8,128)S(1)}, f32[8,8,128]{2,1,0:T(8,128)S(1)}, u32[]{:S(2)}, u32[]{:S(2)}) collective-permute-start(f32[8,8,128]{2,1,0:T(8,128)S(1)} %get-tuple-element.30), channel_id=1, source_target_pairs={{0,4},{4,0},{1,5},{5,1},{2,6},{6,2},{3,7},{7,3},{8,12},{12,8},{9,1... | collective-permute-start | bytes 98312 | tf_op jit(solution)/shard_map/ppermute | solution.py:577
  8.8 0.1 collective-permute-start.3
  8.9 0.8 %collective-permute-done.2 = f32[8,8,128]{2,1,0:T(8,128)S(1)} collective-permute-done((f32[8,8,128]{2,1,0:T(8,128)S(1)}, f32[8,8,128]{2,1,0:T(8,128)S(1)}, u32[]{:S(2)}, u32[]{:S(2)}) %collective-permute-start.2) | collective-permute-done | bytes 32800 | tf_op jit(solution)/shard_map/ppermute | solution.py:577
  9.6 0.3 %collective-permute-start.4 = (f32[2,3,8,8,256]{4,3,2,1,0:T(8,128)S(1)}, f32[2,3,8,8,256]{4,3,2,1,0:T(8,128)S(1)}, u32[]{:S(2)}, u32[]{:S(2)}) collective-permute-start(f32[2,3,8,8,256]{4,3,2,1,0:T(8,128)S(1)} %get-tuple-element.22.refs_1_), channel_id=1, source_target_pairs={{0,4},{4,0},{1,5},{5,1},{2,6},{6,2},{3,7},{7,3},{8,12},{12,8},{9,1... | collective-permute-start | bytes 1179656 | tf_op jit(solution)/shard_map/ppermute | solution.py:577
  10.0 1.3 %collective-permute-start.5 = (f32[16,8,128]{2,1,0:T(8,128)S(1)}, f32[16,8,128]{2,1,0:T(8,128)S(1)}, u32[]{:S(2)}, u32[]{:S(2)}) collective-permute-start(f32[16,8,128]{2,1,0:T(8,128)S(1)} %pad_maximum_fusion), channel_id=1, source_target_pairs={{4,8},{5,9},{6,10},{7,11},{12,16},{13,17},{14,18},{15,19},{20,24},... | collective-permute-start | bytes 196616 | tf_op jit(solution)/shard_map/ppermute | solution.py:614
  11.3 0.0 collective-permute-done.3.refs_2_
  11.3 0.1 collective-permute-done.4.refs_3_
  11.4 2.5 %interior.1 = (f32[8,16,256]{2,1,0:T(8,128)S(1)}, f32[3,18,24,128]{3,2,1,0:T(8,128)S(1)}) custom-call(f32[3,8,16,256]{3,2,1,0:T(8,128)S(1)} %get-tuple-element.17.own.refs_0_, f32[2,3,8,8,256]{4,3,2,1,0:T(8,128)S(1)} %get-tuple-element.22.refs_1_, f32[3,8,16,256]{3,2,1,0:T(8,128)S(1)} %collective-permute-done.3.refs_2_, ...), custom_call_target="tpu_custom_call" | custom-call | flops 20000000 | bytes 20000000 | tf_op jit(solution)/shard_map/interior/pallas_call | solution.py:622
  13.8 1.0 %collective-permute-done.5.got_a = f32[16,8,128]{2,1,0:T(8,128)S(1)} collective-permute-done((f32[16,8,128]{2,1,0:T(8,128)S(1)}, f32[16,8,128]{2,1,0:T(8,128)S(1)}, u32[]{:S(2)}, u32[]{:S(2)}) %collective-permute-start.5) | collective-permute-done | bytes 65568 | tf_op jit(solution)/shard_map/ppermute | solution.py:614
  14.8 0.0 collective-permute-start.6
  14.8 1.3 %collective-permute-done.6.got_b = f32[16,8,128]{2,1,0:T(8,128)S(1)} collective-permute-done((f32[16,8,128]{2,1,0:T(8,128)S(1)}, f32[16,8,128]{2,1,0:T(8,128)S(1)}, u32[]{:S(2)}, u32[]{:S(2)}) %collective-permute-start.6) | collective-permute-done | bytes 65568 | tf_op jit(solution)/shard_map/ppermute | solution.py:577
  16.1 1.8 %edges.1 = f32[8,16,256]{2,1,0:T(8,128)} custom-call(f32[3,18,24,128]{3,2,1,0:T(8,128)S(1)} %get-tuple-element.26.ends, f32[8,16,256]{2,1,0:T(8,128)S(1)} %get-tuple-element.27.inside, f32[16,8,128]{2,1,0:T(8,128)S(1)} %collective-permute-done.5.got_a, f32[16,8,128]{2,1,0:T(8,128)S(1)} %collective-permute-done.6.got_b), custom_call_target="tpu_custom_call" | custom-call | tf_op jit(solution)/shard_map/edges/pallas_call | solution.py:633
  (2 shorter events, 0.0 us)
Async XLA Ops:
  1.3 4.1 %collective-permute-start = (f32[14,8,256]{2,1,0:T(8,128)S(1)}, f32[14,8,256]{2,1,0:T(8,128)S(1)}, u32[]{:S(2)}, u32[]{:S(2)}) collective-permute-start(f32[14,8,256]{2,1,0:T(8,128)S(1)} %get-tuple-element.18), channel_id=1, source_target_pairs={{0,1},{4,5},{2,3},{6,7},{1,0},{5,4},{3,2},{7,6},{8,9},{12,13},{10,... | collective-permute-start | bytes 344072 | tf_op jit(solution)/shard_map/ppermute | solution.py:577
  2.7 3.9 %collective-permute-start.1 = (f32[14,8,256]{2,1,0:T(8,128)S(1)}, f32[14,8,256]{2,1,0:T(8,128)S(1)}, u32[]{:S(2)}, u32[]{:S(2)}) collective-permute-start(f32[14,8,256]{2,1,0:T(8,128)S(1)} %get-tuple-element.19), channel_id=1, source_target_pairs={{1,2},{5,6},{0,4},{3,7},{2,1},{6,5},{4,0},{7,3},{9,10},{13,14},{8,... | collective-permute-start | bytes 344072 | tf_op jit(solution)/shard_map/ppermute | solution.py:577
  6.8 2.8 %collective-permute-start.2 = (f32[8,8,128]{2,1,0:T(8,128)S(1)}, f32[8,8,128]{2,1,0:T(8,128)S(1)}, u32[]{:S(2)}, u32[]{:S(2)}) collective-permute-start(f32[8,8,128]{2,1,0:T(8,128)S(1)} %get-tuple-element.30), channel_id=1, source_target_pairs={{0,4},{4,0},{1,5},{5,1},{2,6},{6,2},{3,7},{7,3},{8,12},{12,8},{9,1... | collective-permute-start | bytes 98312 | tf_op jit(solution)/shard_map/ppermute | solution.py:577
  8.8 2.5 %collective-permute-start.3 = (f32[3,8,16,256]{3,2,1,0:T(8,128)S(1)}, f32[3,8,16,256]{3,2,1,0:T(8,128)S(1)}, u32[]{:S(2)}, u32[]{:S(2)}) collective-permute-start(f32[3,8,16,256]{3,2,1,0:T(8,128)S(1)} %get-tuple-element.17.own.refs_0_), channel_id=1, source_target_pairs={{0,4},{4,0},{1,5},{5,1},{2,6},{6,2},{3,7},{7,3},{8,12},{12,8},{9,1... | collective-permute-start | bytes 1179656 | tf_op jit(solution)/shard_map/ppermute | solution.py:577
  9.6 1.7 %collective-permute-start.4 = (f32[2,3,8,8,256]{4,3,2,1,0:T(8,128)S(1)}, f32[2,3,8,8,256]{4,3,2,1,0:T(8,128)S(1)}, u32[]{:S(2)}, u32[]{:S(2)}) collective-permute-start(f32[2,3,8,8,256]{4,3,2,1,0:T(8,128)S(1)} %get-tuple-element.22.refs_1_), channel_id=1, source_target_pairs={{0,4},{4,0},{1,5},{5,1},{2,6},{6,2},{3,7},{7,3},{8,12},{12,8},{9,1... | collective-permute-start | bytes 1179656 | tf_op jit(solution)/shard_map/ppermute | solution.py:577
  10.0 4.8 %collective-permute-start.5 = (f32[16,8,128]{2,1,0:T(8,128)S(1)}, f32[16,8,128]{2,1,0:T(8,128)S(1)}, u32[]{:S(2)}, u32[]{:S(2)}) collective-permute-start(f32[16,8,128]{2,1,0:T(8,128)S(1)} %pad_maximum_fusion), channel_id=1, source_target_pairs={{4,8},{5,9},{6,10},{7,11},{12,16},{13,17},{14,18},{15,19},{20,24},... | collective-permute-start | bytes 196616 | tf_op jit(solution)/shard_map/ppermute | solution.py:614
  14.8 1.3 %collective-permute-start.6 = (f32[16,8,128]{2,1,0:T(8,128)S(1)}, f32[16,8,128]{2,1,0:T(8,128)S(1)}, u32[]{:S(2)}, u32[]{:S(2)}) collective-permute-start(f32[16,8,128]{2,1,0:T(8,128)S(1)} %collective-permute-done.5.got_a), channel_id=1, source_target_pairs={{0,4},{4,0},{1,5},{5,1},{2,6},{6,2},{3,7},{7,3},{8,12},{12,8},{9,1... | collective-permute-start | bytes 196616 | tf_op jit(solution)/shard_map/ppermute | solution.py:577

commit v15 on v14

--- a/solution.py
+++ b/solution.py
@@ -594,7 +594,6 @@
         scratch_shapes=[pltpu.SemaphoreType.DMA((3,))], compiler_params=params, name="prepare",
     )(*args)
     got = exchange(msgs, "gy")
-    near = exchange([own] * n_x, "gx")
     strips, rim = pl.pallas_call(
         functools.partial(pack_columns, reflect),
         out_shape=(
@@ -608,7 +607,8 @@
         strips = jnp.concatenate([strips[0]] + exchange([strips[1]], "gx"), axis=0)
     else:
         strips = jnp.concatenate([strips] + exchange([strips] * n_x, "gx"), axis=1)
-    strips, rim = lax.optimization_barrier((strips, rim))
+    strips, own = lax.optimization_barrier((strips, own))
+    near = exchange([own] * n_x, "gx")
     near_rim = exchange([rim] * n_x, "gx")
     if reflect:
         strips = [lax.ppermute(strips, tuple(sizes), crossing(sizes))]

time: 18 us -> 18 us (level)
  no operation moved by 1% of the time
where the time goes in v15:
time: 18 us; the launch traced here: 17.8 us
  waiting for transfers between devices  6.99 us (39%)
  Pallas kernels  5.81 us (32%)
  starting transfers between devices  4.99 us (28%)
    ppermute x6, waiting for transfers between devices, exchange(): lax.ppermute(v, over, pairs)  6.02 us
    ppermute x6, starting transfers between devices, exchange(): lax.ppermute(v, over, pairs)  3.73 us
    pallas_call x1, Pallas kernels, shards(): pl.pallas_call(functools.partial(interior, reflect, n_x), out_shape=(bloc...  2.46 us
    pallas_call x1, Pallas kernels, shards(): pl.pallas_call(functools.partial(edges, reflect), out_shape=block, in_spe...  1.77 us
    pallas_call x1, Pallas kernels, shards(): pl.pallas_call(functools.partial(prepare, reflect), out_shape=(jax.ShapeD...  1.34 us
    ppermute x1, starting transfers between devices, shards(): strips = [lax.ppermute(strips, tuple(sizes), crossing(sizes))]  1.26 us
    ppermute x1, waiting for transfers between devices, shards(): strips = [lax.ppermute(strips, tuple(sizes), crossing(sizes))]  0.98 us
  transfers between devices with their start and end apart: 7, of which 6 were waited for; matrix products, arithmetic and copies ran while one was open for 0% of the time, Pallas kernels for 14%

profile of v15, /device:TPU:19, one launch (start us, length us, event | category | flops | bytes accessed | tf_op | source)
XLA Modules:
  0.0 17.8 jit_solution(13814959658000387686)
XLA Ops:
  0.0 1.3 %prepare.1 = (f32[3,8,16,256]{3,2,1,0:T(8,128)S(1)}, f32[14,8,256]{2,1,0:T(8,128)S(1)}, f32[14,8,256]{2,1,0:T(8,128)S(1)}) custom-call(f32[8,16,256]{2,1,0:T(8,128)} %s.1, f32[8,16,256]{2,1,0:T(8,128)} %c.1, f32[8,16,256]{2,1,0:T(8,128)} %f.1), custom_call_target="tpu_custom_call" | custom-call | tf_op jit(solution)/shard_map/prepare/pallas_call | solution.py:590
  1.3 1.4 %collective-permute-start = (f32[14,8,256]{2,1,0:T(8,128)S(1)}, f32[14,8,256]{2,1,0:T(8,128)S(1)}, u32[]{:S(2)}, u32[]{:S(2)}) collective-permute-start(f32[14,8,256]{2,1,0:T(8,128)S(1)} %get-tuple-element.18), channel_id=1, source_target_pairs={{0,1},{4,5},{2,3},{6,7},{1,0},{5,4},{3,2},{7,6},{8,9},{12,13},{10,... | collective-permute-start | bytes 344072 | tf_op jit(solution)/shard_map/ppermute | solution.py:577
  2.7 0.0 collective-permute-start.1
  2.7 2.7 %collective-permute-done.got_a = f32[14,8,256]{2,1,0:T(8,128)S(1)} collective-permute-done((f32[14,8,256]{2,1,0:T(8,128)S(1)}, f32[14,8,256]{2,1,0:T(8,128)S(1)}, u32[]{:S(2)}, u32[]{:S(2)}) %collective-permute-start) | collective-permute-done | bytes 114720 | tf_op jit(solution)/shard_map/ppermute | solution.py:577
  5.4 1.2 %collective-permute-done.1.got_b = f32[14,8,256]{2,1,0:T(8,128)S(1)} collective-permute-done((f32[14,8,256]{2,1,0:T(8,128)S(1)}, f32[14,8,256]{2,1,0:T(8,128)S(1)}, u32[]{:S(2)}, u32[]{:S(2)}) %collective-permute-start.1) | collective-permute-done | bytes 114720 | tf_op jit(solution)/shard_map/ppermute | solution.py:577
  6.6 0.2 %pack_columns.1 = (f32[2,8,8,128]{3,2,1,0:T(8,128)S(1)}, f32[2,3,8,8,256]{4,3,2,1,0:T(8,128)S(1)}) custom-call(f32[3,8,16,256]{3,2,1,0:T(8,128)S(1)} %get-tuple-element.21.own.refs_0_, f32[14,8,256]{2,1,0:T(8,128)S(1)} %collective-permute-done.got_a, f32[14,8,256]{2,1,0:T(8,128)S(1)} %collective-permute-done.1.got_b), custom_call_target="tpu_custom_call" | custom-call | tf_op jit(solution)/shard_map/pack_columns/pallas_call | solution.py:597
  6.8 1.9 %collective-permute-start.2 = (f32[8,8,128]{2,1,0:T(8,128)S(1)}, f32[8,8,128]{2,1,0:T(8,128)S(1)}, u32[]{:S(2)}, u32[]{:S(2)}) collective-permute-start(f32[8,8,128]{2,1,0:T(8,128)S(1)} %get-tuple-element.30), channel_id=1, source_target_pairs={{0,4},{4,0},{1,5},{5,1},{2,6},{6,2},{3,7},{7,3},{8,12},{12,8},{9,1... | collective-permute-start | bytes 98312 | tf_op jit(solution)/shard_map/ppermute | solution.py:577
  8.8 0.1 collective-permute-start.4
  8.9 0.8 %collective-permute-done.2 = f32[8,8,128]{2,1,0:T(8,128)S(1)} collective-permute-done((f32[8,8,128]{2,1,0:T(8,128)S(1)}, f32[8,8,128]{2,1,0:T(8,128)S(1)}, u32[]{:S(2)}, u32[]{:S(2)}) %collective-permute-start.2) | collective-permute-done | bytes 32800 | tf_op jit(solution)/shard_map/ppermute | solution.py:577
  9.6 0.3 %collective-permute-start.3 = (f32[3,8,16,256]{3,2,1,0:T(8,128)S(1)}, f32[3,8,16,256]{3,2,1,0:T(8,128)S(1)}, u32[]{:S(2)}, u32[]{:S(2)}) collective-permute-start(f32[3,8,16,256]{3,2,1,0:T(8,128)S(1)} %get-tuple-element.21.own.refs_0_), channel_id=1, source_target_pairs={{0,4},{4,0},{1,5},{5,1},{2,6},{6,2},{3,7},{7,3},{8,12},{12,8},{9,1... | collective-permute-start | bytes 1179656 | tf_op jit(solution)/shard_map/ppermute | solution.py:577
  10.0 1.3 %collective-permute-start.5 = (f32[16,8,128]{2,1,0:T(8,128)S(1)}, f32[16,8,128]{2,1,0:T(8,128)S(1)}, u32[]{:S(2)}, u32[]{:S(2)}) collective-permute-start(f32[16,8,128]{2,1,0:T(8,128)S(1)} %pad_maximum_fusion), channel_id=1, source_target_pairs={{4,8},{5,9},{6,10},{7,11},{12,16},{13,17},{14,18},{15,19},{20,24},... | collective-permute-start | bytes 196616 | tf_op jit(solution)/shard_map/ppermute | solution.py:614
  11.3 0.0 collective-permute-done.4.refs_3_
  11.3 0.1 collective-permute-done.3.refs_2_
  11.4 2.5 %interior.1 = (f32[8,16,256]{2,1,0:T(8,128)S(1)}, f32[3,18,24,128]{3,2,1,0:T(8,128)S(1)}) custom-call(f32[3,8,16,256]{3,2,1,0:T(8,128)S(1)} %get-tuple-element.21.own.refs_0_, f32[2,3,8,8,256]{4,3,2,1,0:T(8,128)S(1)} %get-tuple-element.22.refs_1_, f32[3,8,16,256]{3,2,1,0:T(8,128)S(1)} %collective-permute-done.3.refs_2_, ...), custom_call_target="tpu_custom_call" | custom-call | flops 20000000 | bytes 20000000 | tf_op jit(solution)/shard_map/interior/pallas_call | solution.py:622
  13.8 1.0 %collective-permute-done.5.got_a = f32[16,8,128]{2,1,0:T(8,128)S(1)} collective-permute-done((f32[16,8,128]{2,1,0:T(8,128)S(1)}, f32[16,8,128]{2,1,0:T(8,128)S(1)}, u32[]{:S(2)}, u32[]{:S(2)}) %collective-permute-start.5) | collective-permute-done | bytes 65568 | tf_op jit(solution)/shard_map/ppermute | solution.py:614
  14.8 0.0 collective-permute-start.6
  14.8 1.3 %collective-permute-done.6.got_b = f32[16,8,128]{2,1,0:T(8,128)S(1)} collective-permute-done((f32[16,8,128]{2,1,0:T(8,128)S(1)}, f32[16,8,128]{2,1,0:T(8,128)S(1)}, u32[]{:S(2)}, u32[]{:S(2)}) %collective-permute-start.6) | collective-permute-done | bytes 65568 | tf_op jit(solution)/shard_map/ppermute | solution.py:577
  16.1 1.8 %edges.1 = f32[8,16,256]{2,1,0:T(8,128)} custom-call(f32[3,18,24,128]{3,2,1,0:T(8,128)S(1)} %get-tuple-element.26.ends, f32[8,16,256]{2,1,0:T(8,128)S(1)} %get-tuple-element.27.inside, f32[16,8,128]{2,1,0:T(8,128)S(1)} %collective-permute-done.5.got_a, f32[16,8,128]{2,1,0:T(8,128)S(1)} %collective-permute-done.6.got_b), custom_call_target="tpu_custom_call" | custom-call | tf_op jit(solution)/shard_map/edges/pallas_call | solution.py:633
  (2 shorter events, 0.0 us)
Async XLA Ops:
  1.3 4.1 %collective-permute-start = (f32[14,8,256]{2,1,0:T(8,128)S(1)}, f32[14,8,256]{2,1,0:T(8,128)S(1)}, u32[]{:S(2)}, u32[]{:S(2)}) collective-permute-start(f32[14,8,256]{2,1,0:T(8,128)S(1)} %get-tuple-element.18), channel_id=1, source_target_pairs={{0,1},{4,5},{2,3},{6,7},{1,0},{5,4},{3,2},{7,6},{8,9},{12,13},{10,... | collective-permute-start | bytes 344072 | tf_op jit(solution)/shard_map/ppermute | solution.py:577
  2.7 3.9 %collective-permute-start.1 = (f32[14,8,256]{2,1,0:T(8,128)S(1)}, f32[14,8,256]{2,1,0:T(8,128)S(1)}, u32[]{:S(2)}, u32[]{:S(2)}) collective-permute-start(f32[14,8,256]{2,1,0:T(8,128)S(1)} %get-tuple-element.19), channel_id=1, source_target_pairs={{1,2},{5,6},{0,4},{3,7},{2,1},{6,5},{4,0},{7,3},{9,10},{13,14},{8,... | collective-permute-start | bytes 344072 | tf_op jit(solution)/shard_map/ppermute | solution.py:577
  6.8 2.8 %collective-permute-start.2 = (f32[8,8,128]{2,1,0:T(8,128)S(1)}, f32[8,8,128]{2,1,0:T(8,128)S(1)}, u32[]{:S(2)}, u32[]{:S(2)}) collective-permute-start(f32[8,8,128]{2,1,0:T(8,128)S(1)} %get-tuple-element.30), channel_id=1, source_target_pairs={{0,4},{4,0},{1,5},{5,1},{2,6},{6,2},{3,7},{7,3},{8,12},{12,8},{9,1... | collective-permute-start | bytes 98312 | tf_op jit(solution)/shard_map/ppermute | solution.py:577
  8.8 2.5 %collective-permute-start.4 = (f32[2,3,8,8,256]{4,3,2,1,0:T(8,128)S(1)}, f32[2,3,8,8,256]{4,3,2,1,0:T(8,128)S(1)}, u32[]{:S(2)}, u32[]{:S(2)}) collective-permute-start(f32[2,3,8,8,256]{4,3,2,1,0:T(8,128)S(1)} %get-tuple-element.22.refs_1_), channel_id=1, source_target_pairs={{0,4},{4,0},{1,5},{5,1},{2,6},{6,2},{3,7},{7,3},{8,12},{12,8},{9,1... | collective-permute-start | bytes 1179656 | tf_op jit(solution)/shard_map/ppermute | solution.py:577
  9.6 1.7 %collective-permute-start.3 = (f32[3,8,16,256]{3,2,1,0:T(8,128)S(1)}, f32[3,8,16,256]{3,2,1,0:T(8,128)S(1)}, u32[]{:S(2)}, u32[]{:S(2)}) collective-permute-start(f32[3,8,16,256]{3,2,1,0:T(8,128)S(1)} %get-tuple-element.21.own.refs_0_), channel_id=1, source_target_pairs={{0,4},{4,0},{1,5},{5,1},{2,6},{6,2},{3,7},{7,3},{8,12},{12,8},{9,1... | collective-permute-start | bytes 1179656 | tf_op jit(solution)/shard_map/ppermute | solution.py:577
  10.0 4.8 %collective-permute-start.5 = (f32[16,8,128]{2,1,0:T(8,128)S(1)}, f32[16,8,128]{2,1,0:T(8,128)S(1)}, u32[]{:S(2)}, u32[]{:S(2)}) collective-permute-start(f32[16,8,128]{2,1,0:T(8,128)S(1)} %pad_maximum_fusion), channel_id=1, source_target_pairs={{4,8},{5,9},{6,10},{7,11},{12,16},{13,17},{14,18},{15,19},{20,24},... | collective-permute-start | bytes 196616 | tf_op jit(solution)/shard_map/ppermute | solution.py:614
  14.8 1.3 %collective-permute-start.6 = (f32[16,8,128]{2,1,0:T(8,128)S(1)}, f32[16,8,128]{2,1,0:T(8,128)S(1)}, u32[]{:S(2)}, u32[]{:S(2)}) collective-permute-start(f32[16,8,128]{2,1,0:T(8,128)S(1)} %collective-permute-done.5.got_a), channel_id=1, source_target_pairs={{0,4},{4,0},{1,5},{5,1},{2,6},{6,2},{3,7},{7,3},{8,12},{12,8},{9,1... | collective-permute-start | bytes 196616 | tf_op jit(solution)/shard_map/ppermute | solution.py:577
